TPU v7x, 32 devices: a whole 2x2x4 slice. The times are simulated.
32 devices in a mesh: dp: 8 (over y, x, core), tensor: 4 (over z).
Axes of the slice: x: 2, y: 2, z: 4, core: 2. Of those that a mesh axis runs over, the one named last changes fastest.
Arguments:
- hidden_in: bfloat16 [8704, 1024], P(('dp', 'tensor')), may hold values from -6 to 6
- cotangent: bfloat16 [8704, 1024], P(('dp', 'tensor')), may hold values from -6 to 6
- group_ids: int32 [8], P('dp'), may hold values from 0 to 7
- group_sizes: int32 [8], replicated, may hold values from 1 to 4
- w_qkv: bfloat16 [2, 3, 1024, 1024], P(None, None, None, 'tensor'), may hold values from -0.1875 to 0.1875
- w_out: bfloat16 [2, 1024, 1024], P(None, 'tensor'), may hold values from -0.75 to 0.75
- w_up: bfloat16 [2, 1024, 4096], P(None, None, 'tensor'), may hold values from -0.1875 to 0.1875
- w_down: bfloat16 [2, 4096, 1024], P(None, 'tensor'), may hold values from -0.09375 to 0.09375
- gains: float32 [2, 4, 1024], replicated, may hold values from 0.25 to 1.75
- shifts: float32 [2, 4, 1024], replicated, may hold values from -1.5 to 1.5
Outputs:
- mixed: float32 [8704, 1024], P(('dp', 'tensor'))
- grad_in: float32 [8704, 1024], P(('dp', 'tensor'))
- grad_qkv: float32 [2, 3, 1024, 1024], P(None, None, None, 'tensor')
- grad_out: float32 [2, 1024, 1024], P(None, 'tensor')
- grad_up: float32 [2, 1024, 4096], P(None, None, 'tensor')
- grad_down: float32 [2, 4096, 1024], P(None, 'tensor')
- grad_gains: float32 [2, 4, 1024], replicated
- grad_shifts: float32 [2, 4, 1024], replicated
All inputs are finite; a program needn't handle non-finite values.
Results may differ from a plain program's by a relative error of at most 0.02.
Values may be sent and summed in bfloat16 or wider, within the bound.
A program may use at most 256 MiB of HBM per device.

v0:
```python
import jax
import jax.numpy as jnp
from jax import lax
from jax.sharding import PartitionSpec as P

HEAD_DIM = 64
LENGTH = 1088


eps_norm = 1e-05


def norm_rows(values, gain, shift):
    mean = jnp.mean(values, axis=-1, keepdims=True)
    centred = values - mean
    spread = jnp.mean(centred * centred, axis=-1, keepdims=True)
    return centred * lax.rsqrt(spread + eps_norm) * gain + shift


def gelu_tanh(values):
    return jax.nn.gelu(values, approximate=True)


def masked_scores(query, key):
    scale = query.shape[-1] ** (-0.5)
    scores = jnp.einsum("qhd,khd->hqk", query, key, preferred_element_type=jnp.float32) * scale
    places = jnp.arange(query.shape[0])
    causal = places[:, None] >= places[None, :]
    return jnp.where(causal[None], scores, -1e30)


def attend_forward(query, key, value):
    scores = masked_scores(query, key)
    top = jnp.max(scores, axis=-1, keepdims=True)
    weights = jnp.exp(scores - top)
    total = jnp.sum(weights, axis=-1, keepdims=True)
    probs = (weights / total).astype(jnp.bfloat16)
    result = jnp.einsum("hqk,khd->qhd", probs, value, preferred_element_type=jnp.float32)
    return (result.astype(jnp.bfloat16), (top + jnp.log(total))[..., 0])


def attend_backward(query, key, value, grad_result, logsum):
    scale = query.shape[-1] ** (-0.5)
    probs = jnp.exp(masked_scores(query, key) - logsum[..., None])
    grad_probs = jnp.einsum("qhd,khd->hqk", grad_result, value, preferred_element_type=jnp.float32)
    inner = jnp.sum(probs * grad_probs, axis=-1, keepdims=True)
    grad_scores = (probs * (grad_probs - inner)).astype(jnp.bfloat16) * scale
    grad_query = jnp.einsum("hqk,khd->qhd", grad_scores, key, preferred_element_type=jnp.float32)
    grad_key = jnp.einsum("hqk,qhd->khd", grad_scores, query, preferred_element_type=jnp.float32)
    grad_value = jnp.einsum(
        "hqk,qhd->khd", probs.astype(jnp.bfloat16), grad_result, preferred_element_type=jnp.float32
    )
    return jnp.stack([grad_query, grad_key, grad_value]).astype(jnp.bfloat16)


def per_device(
    hidden_in, cotangent, group_ids, group_sizes, w_qkv, w_out, w_up, w_down, gains, shifts
):
    f32 = jnp.float32
    bf16 = jnp.bfloat16
    rows = hidden_in.shape[0]
    layers = w_qkv.shape[0]
    local_width = w_qkv.shape[3]
    heads_here = local_width // HEAD_DIM
    stream = hidden_in.astype(f32)
    saved = []
    for layer in range(layers):
        normed = norm_rows(stream, gains[layer, 0], shifts[layer, 0]).astype(bf16)
        rows_all = lax.all_gather(normed, "tensor", axis=0, tiled=True)
        group_rows = rows_all.shape[0]
        seqs = group_rows // LENGTH
        qkv = jnp.einsum("td,cde->cte", rows_all, w_qkv[layer], preferred_element_type=f32).astype(
            bf16
        )
        split = qkv.reshape(3, seqs, LENGTH, heads_here, HEAD_DIM)
        attended, logsum = lax.map(
            lambda item: attend_forward(item[0], item[1], item[2]), (split[0], split[1], split[2])
        )
        attended = attended.reshape(group_rows, local_width)

        def project_out(start, count, attended=attended, layer=layer):
            return jnp.dot(attended, w_out[layer], preferred_element_type=f32)

        branch = lax.psum_scatter(
            project_out(jnp.int32(0), rows * lax.axis_size("tensor")),
            "tensor",
            scatter_dimension=0,
            tiled=True,
        )
        middle = stream + norm_rows(branch, gains[layer, 1], shifts[layer, 1])
        normed2 = norm_rows(middle, gains[layer, 2], shifts[layer, 2]).astype(bf16)
        ffn_all = lax.all_gather(normed2, "tensor", axis=0, tiled=True)
        upper = jnp.dot(ffn_all, w_up[layer], preferred_element_type=f32)
        active = gelu_tanh(upper).astype(bf16)

        def project_down(start, count, active=active, layer=layer):
            return jnp.dot(active, w_down[layer], preferred_element_type=f32)

        second = lax.psum_scatter(
            project_down(jnp.int32(0), lax.axis_size("tensor") * rows).astype(jnp.bfloat16),
            "tensor",
            scatter_dimension=0,
            tiled=True,
        ).astype(jnp.float32)
        saved.append(
            (
                stream,
                rows_all,
                qkv,
                attended,
                logsum,
                branch,
                middle,
                ffn_all,
                upper,
                active,
                second,
            )
        )
        stream = middle + norm_rows(second, gains[layer, 3], shifts[layer, 3])
    places = lax.axis_index("tensor") * rows + jnp.arange(rows)
    seq_of_row = places // LENGTH
    match = group_ids[:, None] == jnp.arange(group_sizes.shape[0])[None, :]
    counts = jnp.sum(jnp.where(match, group_sizes[None, :], 0), axis=1).astype(f32)
    seq_weight = 1.0 / counts
    owner = seq_of_row[:, None] == jnp.arange(group_ids.shape[0])[None, :]
    row_weight = jnp.sum(jnp.where(owner, seq_weight[None, :], 0.0), axis=1)
    grad_stream = cotangent.astype(f32) * row_weight[:, None]
    weight_grads = [None] * layers
    gain_grads = [None] * layers
    shift_grads = [None] * layers
    for layer in reversed(range(layers)):
        (
            stream_in,
            rows_all,
            qkv,
            attended,
            logsum,
            branch,
            middle,
            ffn_all,
            upper,
            active,
            second,
        ) = saved[layer]
        group_rows = rows_all.shape[0]
        seqs = group_rows // LENGTH
        _, pull_three = jax.vjp(norm_rows, second, gains[layer, 3], shifts[layer, 3])
        grad_second, gain_three, shift_three = pull_three(grad_stream)
        second_all = lax.all_gather(grad_second.astype(bf16), "tensor", axis=0, tiled=True)
        grad_downw = jnp.einsum("tf,td->fd", active, second_all, preferred_element_type=f32)
        grad_active = jnp.einsum("td,fd->tf", second_all, w_down[layer], preferred_element_type=f32)
        _, gelu_pull = jax.vjp(gelu_tanh, upper)
        grad_upper = gelu_pull(grad_active)[0].astype(bf16)
        grad_upw = jnp.einsum("td,tf->df", ffn_all, grad_upper, preferred_element_type=f32)

        def back_up(start, count, grad_upper=grad_upper, layer=layer):
            return jnp.einsum("tf,df->td", grad_upper, w_up[layer], preferred_element_type=f32)

        grad_normed2 = lax.psum_scatter(
            back_up(jnp.int32(0), lax.axis_size("tensor") * rows).astype(jnp.bfloat16),
            "tensor",
            scatter_dimension=0,
            tiled=True,
        ).astype(jnp.float32)
        _, pull_two = jax.vjp(norm_rows, middle, gains[layer, 2], shifts[layer, 2])
        grad_mid_part, gain_two, shift_two = pull_two(grad_normed2)
        grad_middle = grad_stream + grad_mid_part
        _, pull_one = jax.vjp(norm_rows, branch, gains[layer, 1], shifts[layer, 1])
        grad_branch, gain_one, shift_one = pull_one(grad_middle)
        branch_all = lax.all_gather(grad_branch.astype(bf16), "tensor", axis=0, tiled=True)
        grad_outw = jnp.einsum("te,td->ed", attended, branch_all, preferred_element_type=f32)
        grad_attended = jnp.einsum(
            "td,ed->te", branch_all, w_out[layer], preferred_element_type=f32
        ).astype(bf16)
        split = qkv.reshape(3, seqs, LENGTH, heads_here, HEAD_DIM)
        grad_split = grad_attended.reshape(seqs, LENGTH, heads_here, HEAD_DIM)
        grads_seq = lax.map(
            lambda item: attend_backward(item[0], item[1], item[2], item[3], item[4]),
            (split[0], split[1], split[2], grad_split, logsum),
        )
        grad_rows = jnp.moveaxis(grads_seq, 1, 0).reshape(3, group_rows, local_width)
        grad_qkvw = jnp.einsum("td,cte->cde", rows_all, grad_rows, preferred_element_type=f32)

        def back_qkv(start, count, grad_rows=grad_rows, layer=layer):
            return jnp.einsum("cte,cde->td", grad_rows, w_qkv[layer], preferred_element_type=f32)

        grad_normed = lax.psum_scatter(
            back_qkv(jnp.int32(0), lax.axis_size("tensor") * rows).astype(jnp.bfloat16),
            "tensor",
            scatter_dimension=0,
            tiled=True,
        ).astype(jnp.float32)
        _, pull_zero = jax.vjp(norm_rows, stream_in, gains[layer, 0], shifts[layer, 0])
        grad_in_part, gain_zero, shift_zero = pull_zero(grad_normed)
        grad_stream = grad_middle + grad_in_part
        gain_grads[layer] = jnp.stack([gain_zero, gain_one, gain_two, gain_three])
        shift_grads[layer] = jnp.stack([shift_zero, shift_one, shift_two, shift_three])
        weight_grads[layer] = (grad_qkvw, grad_outw, grad_upw, grad_downw)
    stacked = [
        jnp.stack([weight_grads[index][member] for index in range(layers)]) for member in range(4)
    ]
    shared = (
        lax.psum_scatter(stacked[0], "dp", scatter_dimension=2, tiled=True),
        lax.psum_scatter(stacked[1], "dp", scatter_dimension=2, tiled=True),
        lax.psum_scatter(stacked[2], "dp", scatter_dimension=1, tiled=True),
        lax.psum_scatter(stacked[3], "dp", scatter_dimension=2, tiled=True),
    )
    stacked = (
        lax.all_gather(shared[0].astype(jnp.bfloat16), "dp", axis=2, tiled=True).astype(
            jnp.float32
        ),
        lax.all_gather(shared[1].astype(jnp.bfloat16), "dp", axis=2, tiled=True).astype(
            jnp.float32
        ),
        lax.all_gather(shared[2].astype(jnp.bfloat16), "dp", axis=1, tiled=True).astype(
            jnp.float32
        ),
        lax.all_gather(shared[3].astype(jnp.bfloat16), "dp", axis=2, tiled=True).astype(
            jnp.float32
        ),
    )
    norm_sums = lax.psum((jnp.stack(gain_grads), jnp.stack(shift_grads)), ("dp", "tensor"))
    return (
        stream,
        grad_stream,
        stacked[0],
        stacked[1],
        stacked[2],
        stacked[3],
        norm_sums[0],
        norm_sums[1],
    )


def solution(mesh):
    in_specs = (
        P(("dp", "tensor"), None),
        P(("dp", "tensor"), None),
        P("dp"),
        P(),
        P(None, None, None, "tensor"),
        P(None, "tensor", None),
        P(None, None, "tensor"),
        P(None, "tensor", None),
        P(),
        P(),
    )
    out_specs = (
        P(("dp", "tensor"), None),
        P(("dp", "tensor"), None),
        P(None, None, None, "tensor"),
        P(None, "tensor", None),
        P(None, None, "tensor"),
        P(None, "tensor", None),
        P(),
        P(),
    )
    return jax.shard_map(
        per_device, mesh=mesh, in_specs=in_specs, out_specs=out_specs, check_vma=False
    )
```

profile of v0, /device:TPU:0, one launch (start us, length us, event | category | flops | bytes accessed | tf_op | source)
XLA Modules:
  0.0 1629.2 jit_solution(13445539441344188138)
XLA Ops:
  16.1 50.8 %all-gather.13.cloned.1.call-done = bf16[1088,1024]{1,0:T(8,128)(2,1)} async-done(((bf16[272,1024]{1,0:T(8,128)(2,1)}), bf16[1088,1024]{1,0:T(8,128)(2,1)}) %all-gather.13.cloned.1.call-update) | async-done | bytes 2228240 | tf_op jit(solution)/shard_map/all_gather | solution.py:69
  104.3 79.7 %reduce-scatter.13.cloned.1.call-done = f32[272,1024]{1,0:T(8,128)} async-done(((f32[1088,1024]{1,0:T(8,128)}), f32[272,1024]{1,0:T(8,128)}) %reduce-scatter.13.cloned.1.call-update) | async-done | bytes 1114128 | tf_op jit(solution)/shard_map/reduce_scatter | solution.py:84
  190.1 49.0 %all-gather.15.cloned.1.call-done = bf16[1088,1024]{1,0:T(8,128)(2,1)} async-done(((bf16[272,1024]{1,0:T(8,128)(2,1)}), bf16[1088,1024]{1,0:T(8,128)(2,1)}) %all-gather.15.cloned.1.call-update) | async-done | bytes 2228240 | tf_op jit(solution)/shard_map/all_gather | solution.py:92
  250.2 44.9 %reduce-scatter.15.cloned.1.call-done = bf16[272,1024]{1,0:T(8,128)(2,1)} async-done(((bf16[1088,1024]{1,0:T(8,128)(2,1)}), bf16[272,1024]{1,0:T(8,128)(2,1)}) %reduce-scatter.15.cloned.1.call-update) | async-done | bytes 557072 | tf_op jit(solution)/shard_map/reduce_scatter | solution.py:99
  300.8 47.9 %all-gather.17.cloned.1.call-done = bf16[1088,1024]{1,0:T(8,128)(2,1)} async-done(((bf16[272,1024]{1,0:T(8,128)(2,1)}), bf16[1088,1024]{1,0:T(8,128)(2,1)}) %all-gather.17.cloned.1.call-update) | async-done | bytes 2228240 | tf_op jit(solution)/shard_map/all_gather | solution.py:69
  389.5 79.9 %reduce-scatter.17.cloned.1.call-done = f32[272,1024]{1,0:T(8,128)} async-done(((f32[1088,1024]{1,0:T(8,128)}), f32[272,1024]{1,0:T(8,128)}) %reduce-scatter.17.cloned.1.call-update) | async-done | bytes 1114128 | tf_op jit(solution)/shard_map/reduce_scatter | solution.py:84
  485.4 37.9 %all-gather.19.cloned.1.call-done = bf16[1088,1024]{1,0:T(8,128)(2,1)} async-done(((bf16[272,1024]{1,0:T(8,128)(2,1)}), bf16[1088,1024]{1,0:T(8,128)(2,1)}) %all-gather.19.cloned.1.call-update) | async-done | bytes 2228240 | tf_op jit(solution)/shard_map/all_gather | solution.py:92
  536.4 42.9 %reduce-scatter.19.cloned.1.call-done = bf16[272,1024]{1,0:T(8,128)(2,1)} async-done(((bf16[1088,1024]{1,0:T(8,128)(2,1)}), bf16[272,1024]{1,0:T(8,128)(2,1)}) %reduce-scatter.19.cloned.1.call-update) | async-done | bytes 557072 | tf_op jit(solution)/shard_map/reduce_scatter | solution.py:99
  586.9 47.9 %all-gather.21.cloned.1.call-done = bf16[1088,1024]{1,0:T(8,128)(2,1)} async-done(((bf16[272,1024]{1,0:T(8,128)(2,1)}), bf16[1088,1024]{1,0:T(8,128)(2,1)}) %all-gather.21.cloned.1.call-update) | async-done | bytes 2228240 | tf_op jit(solution)/shard_map/all_gather | solution.py:150
  648.6 44.9 %reduce-scatter.21.cloned.1.call-done = bf16[272,1024]{1,0:T(8,128)(2,1)} async-done(((bf16[1088,1024]{1,0:T(8,128)(2,1)}), bf16[272,1024]{1,0:T(8,128)(2,1)}) %reduce-scatter.21.cloned.1.call-update) | async-done | bytes 557072 | tf_op jit(solution)/shard_map/reduce_scatter | solution.py:160
  703.1 47.8 %all-gather.23.cloned.1.call-done = bf16[1088,1024]{1,0:T(8,128)(2,1)} async-done(((bf16[272,1024]{1,0:T(8,128)(2,1)}), bf16[1088,1024]{1,0:T(8,128)(2,1)}) %all-gather.23.cloned.1.call-update) | async-done | bytes 2228240 | tf_op jit(solution)/shard_map/all_gather | solution.py:171
  834.4 44.7 %reduce-scatter.23.cloned.1.call-done = bf16[272,1024]{1,0:T(8,128)(2,1)} async-done(((bf16[1088,1024]{1,0:T(8,128)(2,1)}), bf16[272,1024]{1,0:T(8,128)(2,1)}) %reduce-scatter.23.cloned.1.call-update) | async-done | bytes 557072 | tf_op jit(solution)/shard_map/reduce_scatter | solution.py:188
  885.3 47.8 %all-gather.25.cloned.1.call-done = bf16[1088,1024]{1,0:T(8,128)(2,1)} async-done(((bf16[272,1024]{1,0:T(8,128)(2,1)}), bf16[1088,1024]{1,0:T(8,128)(2,1)}) %all-gather.25.cloned.1.call-update) | async-done | bytes 2228240 | tf_op jit(solution)/shard_map/all_gather | solution.py:150
  947.1 44.9 %reduce-scatter.25.cloned.1.call-done = bf16[272,1024]{1,0:T(8,128)(2,1)} async-done(((bf16[1088,1024]{1,0:T(8,128)(2,1)}), bf16[272,1024]{1,0:T(8,128)(2,1)}) %reduce-scatter.25.cloned.1.call-update) | async-done | bytes 557072 | tf_op jit(solution)/shard_map/reduce_scatter | solution.py:160
  1001.8 45.0 %all-gather.27.cloned.1.call-done = bf16[1088,1024]{1,0:T(8,128)(2,1)} async-done(((bf16[272,1024]{1,0:T(8,128)(2,1)}), bf16[1088,1024]{1,0:T(8,128)(2,1)}) %all-gather.27.cloned.1.call-update) | async-done | bytes 2228240 | tf_op jit(solution)/shard_map/all_gather | solution.py:171
  1110.3 29.3 %fusion.59 = bf16[4,64,1088]{2,1,0:T(8,128)(2,1)S(1)} fusion(bf16[1088,4,64]{0,2,1:T(8,128)(2,1)S(1)} %bitcast.203, f32[4,1088,1088]{1,2,0:T(8,128)} %fusion.220, f32[4,1088,1088]{1,2,0:T(8,128)} %get-tuple-element.175, f32[4,1088]{1,0:T(4,128)S(1)} %log_add_fusion), kind=kOutput, calls=%fused_computation.75 | convolution fusion | flops 653710656 | bytes 39011328 | tf_op jit(solution)/shard_map/while/body/eval_jaxpr/hqk,qhd->khd/dot_general | solution.py:49
  1140.6 28.4 %fusion.56 = bf16[4,64,1088]{2,1,0:T(8,128)(2,1)S(1)} fusion(bf16[1088,4,64]{0,2,1:T(8,128)(2,1)S(1)} %bitcast.201, f32[4,1088,1088]{1,2,0:T(8,128)} %fusion.220, f32[4,1088,1088]{1,2,0:T(8,128)} %get-tuple-element.175, f32[4,1088]{1,0:T(4,128)S(1)} %log_add_fusion), kind=kOutput, calls=%fused_computation.74 | convolution fusion | flops 653710656 | bytes 39011328 | tf_op jit(solution)/shard_map/while/body/eval_jaxpr/hqk,khd->qhd/dot_general | solution.py:48
  1187.5 54.3 %reduce-scatter.35.cloned.1.call-done = f32[2,1024,128]{2,1,0:T(8,128)} async-done(((f32[2,1024,1024]{2,1,0:T(8,128)}), f32[2,1024,128]{2,1,0:T(8,128)}) %reduce-scatter.35.cloned.1.call-update) | async-done | bytes 1048592 | tf_op jit(solution)/shard_map/reduce_scatter | solution.py:207
  1244.0 63.9 %reduce-scatter.29.cloned.1.call-done = f32[2,3,128,256]{2,3,1,0:T(8,128)} async-done(((f32[2,3,1024,256]{2,3,1,0:T(8,128)}), f32[2,3,128,256]{2,3,1,0:T(8,128)}) %reduce-scatter.29.cloned.1.call-update) | async-done | bytes 786448 | tf_op jit(solution)/shard_map/reduce_scatter | solution.py:204
  1310.1 46.0 %reduce-scatter.27.cloned.1.call-done = bf16[272,1024]{1,0:T(8,128)(2,1)} async-done(((bf16[1088,1024]{1,0:T(8,128)(2,1)}), bf16[272,1024]{1,0:T(8,128)(2,1)}) %reduce-scatter.27.cloned.1.call-update) | async-done | bytes 557072 | tf_op jit(solution)/shard_map/reduce_scatter | solution.py:188
  1384.3 36.4 %all-gather.33.cloned.1.call-done = bf16[2,1024,1024]{2,1,0:T(8,128)(2,1)} async-done(((bf16[2,128,1024]{2,1,0:T(8,128)(2,1)}), bf16[2,1024,1024]{2,1,0:T(8,128)(2,1)}) %all-gather.33.cloned.1.call-update) | async-done | bytes 4194320 | tf_op jit(solution)/shard_map/all_gather | solution.py:216
  1427.4 32.7 %all-gather.35.cloned.1.call-done = bf16[2,1024,1024]{2,1,0:T(8,128)(2,1)} async-done(((bf16[2,1024,128]{2,1,0:T(8,128)(2,1)}), bf16[2,1024,1024]{2,1,0:T(8,128)(2,1)}) %all-gather.35.cloned.1.call-update) | async-done | bytes 4194320 | tf_op jit(solution)/shard_map/all_gather | solution.py:219
  1466.8 28.5 %all-gather.29.cloned.1.call-done = bf16[2,3,1024,256]{2,3,1,0:T(8,128)(2,1)} async-done(((bf16[2,3,128,256]{2,3,1,0:T(8,128)(2,1)}), bf16[2,3,1024,256]{2,3,1,0:T(8,128)(2,1)}) %all-gather.29.cloned.1.call-update) | async-done | bytes 3145744 | tf_op jit(solution)/shard_map/all_gather | solution.py:210
  1500.6 119.0 %all-reduce.3.cloned.1.call-done = (f32[2,4,1024]{2,1,0:T(4,128)}, f32[2,4,1024]{2,1,0:T(4,128)}) async-done(((f32[2,4,1024]{2,1,0:T(4,128)}, f32[2,4,1024]{2,1,0:T(4,128)}), (f32[2,4,1024]{2,1,0:T(4,128)}, f32[2,4,1024]{2,1,0:T(4,128)})) %all-reduce.3.cloned.1.call-update) | async-done | bytes 65552 | tf_op jit(solution)/shard_map/psum | solution.py:223
  (441 shorter events, 417.7 us)
Async XLA Ops:
  15.7 168.3 %reduce-scatter.13.cloned.1.call-start = ((), (), s32[]{:S(2)}) async-start(), calls=%async_computation.13 | async-start | bytes 5570560 | tf_op jit(solution)/shard_map/reduce_scatter | solution.py:84
  104.0 135.1 %all-gather.15.cloned.1.call-start = ((), (), s32[]{:S(2)}) async-start(), calls=%async_computation.14 | async-start | bytes 2785280 | tf_op jit(solution)/shard_map/all_gather | solution.py:92
  190.1 105.1 %reduce-scatter.15.cloned.1.call-start = ((), (), s32[]{:S(2)}) async-start(), calls=%async_computation.15 | async-start | bytes 2785280 | tf_op jit(solution)/shard_map/reduce_scatter | solution.py:99
  250.2 98.5 %all-gather.17.cloned.1.call-start = ((), (), s32[]{:S(2)}) async-start(), calls=%async_computation.16 | async-start | bytes 2785280 | tf_op jit(solution)/shard_map/all_gather | solution.py:69
  300.8 168.6 %reduce-scatter.17.cloned.1.call-start = ((), (), s32[]{:S(2)}) async-start(), calls=%async_computation.17 | async-start | bytes 5570560 | tf_op jit(solution)/shard_map/reduce_scatter | solution.py:84
  389.4 133.9 %all-gather.19.cloned.1.call-start = ((), (), s32[]{:S(2)}) async-start(), calls=%async_computation.18 | async-start | bytes 2785280 | tf_op jit(solution)/shard_map/all_gather | solution.py:92
  474.3 105.0 %reduce-scatter.19.cloned.1.call-start = ((), (), s32[]{:S(2)}) async-start(), calls=%async_computation.19 | async-start | bytes 2785280 | tf_op jit(solution)/shard_map/reduce_scatter | solution.py:99
  534.4 100.4 %all-gather.21.cloned.1.call-start = ((), (), s32[]{:S(2)}) async-start(), calls=%async_computation.20 | async-start | bytes 2785280 | tf_op jit(solution)/shard_map/all_gather | solution.py:150
  586.8 106.7 %reduce-scatter.21.cloned.1.call-start = ((), (), s32[]{:S(2)}) async-start(), calls=%async_computation.21 | async-start | bytes 2785280 | tf_op jit(solution)/shard_map/reduce_scatter | solution.py:160
  648.6 102.3 %all-gather.23.cloned.1.call-start = ((), (), s32[]{:S(2)}) async-start(), calls=%async_computation.22 | async-start | bytes 2785280 | tf_op jit(solution)/shard_map/all_gather | solution.py:171
  703.0 176.1 %reduce-scatter.23.cloned.1.call-start = ((), (), s32[]{:S(2)}) async-start(), calls=%async_computation.23 | async-start | bytes 2785280 | tf_op jit(solution)/shard_map/reduce_scatter | solution.py:188
  834.1 99.0 %all-gather.25.cloned.1.call-start = ((), (), s32[]{:S(2)}) async-start(), calls=%async_computation.24 | async-start | bytes 2785280 | tf_op jit(solution)/shard_map/all_gather | solution.py:150
  885.3 106.7 %reduce-scatter.25.cloned.1.call-start = ((), (), s32[]{:S(2)}) async-start(), calls=%async_computation.25 | async-start | bytes 2785280 | tf_op jit(solution)/shard_map/reduce_scatter | solution.py:160
  947.0 99.7 %all-gather.27.cloned.1.call-start = ((), (), s32[]{:S(2)}) async-start(), calls=%async_computation.26 | async-start | bytes 2785280 | tf_op jit(solution)/shard_map/all_gather | solution.py:171
  998.9 184.6 %reduce-scatter.31.cloned.1.call-start = ((), (), s32[]{:S(2)}) async-start(), calls=%async_computation.30 | async-start | bytes 2359296 | tf_op jit(solution)/shard_map/reduce_scatter | solution.py:205
  1050.8 134.4 %reduce-scatter.33.cloned.1.call-start = ((), (), s32[]{:S(2)}) async-start(), calls=%async_computation.32 | async-start | bytes 9437184 | tf_op jit(solution)/shard_map/reduce_scatter | solution.py:206
  1063.6 178.2 %reduce-scatter.35.cloned.1.call-start = ((), (), s32[]{:S(2)}) async-start(), calls=%async_computation.34 | async-start | bytes 9437184 | tf_op jit(solution)/shard_map/reduce_scatter | solution.py:207
  1079.8 228.1 %reduce-scatter.29.cloned.1.call-start = ((), (), s32[]{:S(2)}) async-start(), calls=%async_computation.28 | async-start | bytes 7077888 | tf_op jit(solution)/shard_map/reduce_scatter | solution.py:204
  1177.0 179.1 %reduce-scatter.27.cloned.1.call-start = ((), (), s32[]{:S(2)}) async-start(), calls=%async_computation.27 | async-start | bytes 2785280 | tf_op jit(solution)/shard_map/reduce_scatter | solution.py:188
  1183.4 198.1 %all-gather.31.cloned.1.call-start = ((), (), s32[]{:S(2)}) async-start(), calls=%async_computation.31 | async-start | bytes 1179648 | tf_op jit(solution)/shard_map/all_gather | solution.py:213
  1185.2 235.6 %all-gather.33.cloned.1.call-start = ((), (), s32[]{:S(2)}) async-start(), calls=%async_computation.33 | async-start | bytes 4718592 | tf_op jit(solution)/shard_map/all_gather | solution.py:216
  1187.5 272.6 %all-gather.35.cloned.1.call-start = ((), (), s32[]{:S(2)}) async-start(), calls=%async_computation.35 | async-start | bytes 4718592 | tf_op jit(solution)/shard_map/all_gather | solution.py:219
  1244.0 251.3 %all-gather.29.cloned.1.call-start = ((), (), s32[]{:S(2)}) async-start(), calls=%async_computation.29 | async-start | bytes 3538944 | tf_op jit(solution)/shard_map/all_gather | solution.py:210
  1309.9 309.8 %all-reduce.3.cloned.1.call-start = ((), (), s32[]{:S(2)}) async-start(), calls=%async_computation.36 | async-start | bytes 131072 | tf_op jit(solution)/shard_map/psum | solution.py:223
  (121 other events, 4170.0 us)
Sparse Core Ops, SparseCore 0:
  15.8 51.0 all-gather.12
  104.1 79.8 reduce-scatter.12
  190.2 48.8 all-gather.14
  250.3 44.8 reduce-scatter.14
  300.9 47.7 all-gather.16
  389.5 79.8 reduce-scatter.16
  474.4 48.8 all-gather.18
  534.5 44.7 reduce-scatter.18
  586.9 47.7 all-gather.20
  648.7 44.8 reduce-scatter.20
  703.1 47.7 all-gather.22
  834.2 44.8 reduce-scatter.22
  885.4 47.7 all-gather.24
  947.1 44.7 reduce-scatter.24
  999.0 47.7 all-gather.26
  1050.9 40.0 reduce-scatter.30
  1095.3 71.2 reduce-scatter.32
  1170.5 71.2 reduce-scatter.34
  1246.1 61.7 reduce-scatter.28
  1310.1 45.9 reduce-scatter.26
  1384.0 36.7 all-gather.32
  1422.7 37.4 all-gather.34
  1462.4 32.8 all-gather.28
  1501.5 118.0 all-reduce.2
  (1 shorter events, 22.9 us)
where the time goes:
time: 1640 us; the launch traced here: 1630 us
  waiting for transfers between devices  1160 us (71%)
  matrix products  292 us (18%)
  other arithmetic  113 us (7%)
  local copies, waits for them, and re-layouts  38 us (2%)
  between operations  17.1 us (1%)
    reduce_scatter x2, waiting for transfers between devices, per_device(): lax.psum_scatter(project_out(jnp.int32(0), rows * lax.axis_size('tensor')...  160 us
    psum x1, waiting for transfers between devices, per_device(): lax.psum((jnp.stack(gain_grads), jnp.stack(shift_grads)), ('dp', 'tensor'))  119 us
    all_gather x2, waiting for transfers between devices, per_device(): rows_all = lax.all_gather(normed, 'tensor', axis=0, tiled=True)  98.6 us
    all_gather x2, waiting for transfers between devices, per_device(): lax.all_gather(grad_second.astype(bf16), 'tensor', axis=0, tiled=True)  95.7 us
    all_gather x2, waiting for transfers between devices, per_device(): lax.all_gather(grad_branch.astype(bf16), 'tensor', axis=0, tiled=True)  92.8 us
    reduce_scatter x2, waiting for transfers between devices, per_device(): lax.psum_scatter(back_qkv(jnp.int32(0), lax.axis_size('tensor') * rows).a...  90.7 us
    reduce_scatter x2, waiting for transfers between devices, per_device(): lax.psum_scatter(back_up(jnp.int32(0), lax.axis_size('tensor') * rows).as...  89.8 us
    reduce_scatter x2, waiting for transfers between devices, per_device(): lax.psum_scatter(project_down(jnp.int32(0), lax.axis_size('tensor') * row...  87.8 us
  transfers between devices with their start and end apart: 25, of which 23 were waited for; matrix products, arithmetic and copies ran while one was open for 10% of the time, Pallas kernels for 0%

commit v1 on v0

--- a/solution.py
+++ b/solution.py
@@ -5,6 +5,38 @@
 
 HEAD_DIM = 64
 LENGTH = 1088
+AXES = ("gh", "gl", "p", "c", "zh", "zl")
+TP = ("c", "zl")
+SHARE = ("gl", "p")
+BATCH = ("gh", "gl", "p")
+
+
+def swap_rows(values):
+    return lax.ppermute(values, ("c", "zh"), ((0, 0), (1, 2), (2, 1), (3, 3)))
+
+
+def keeps():
+    return lax.axis_index("c") == lax.axis_index("zh")
+
+
+def fetch_weight(weight):
+    shape = weight.shape
+    flat = weight.reshape(4, -1, 1024)
+    part = lax.dynamic_index_in_dim(flat, lax.axis_index(SHARE), 0, keepdims=False)
+    part = lax.ppermute(part, ("c", "zh"), ((0, 1), (3, 2)))
+    rest = lax.all_gather(part, SHARE, axis=0, tiled=True).reshape(shape)
+    return jnp.where(keeps(), weight, rest)
+
+
+def sum_weight(grad):
+    shape = grad.shape
+    flat = grad.astype(jnp.bfloat16).reshape(-1, 1024)
+    part = lax.psum_scatter(flat, BATCH, scatter_dimension=0, tiled=True)
+    other = lax.ppermute(part, ("c", "zh"), ((1, 0), (2, 3)))
+    part = (part.astype(jnp.float32) + other.astype(jnp.float32)).astype(jnp.bfloat16)
+    mate = lax.ppermute(part, "c", ((0, 1), (1, 0)))
+    part = jnp.where(keeps(), part, mate)
+    return lax.all_gather(part, BATCH, axis=0, tiled=True).reshape(shape).astype(jnp.float32)
 
 
 eps_norm = 1e-05
@@ -59,14 +91,20 @@
     f32 = jnp.float32
     bf16 = jnp.bfloat16
     rows = hidden_in.shape[0]
+    hidden_in = swap_rows(hidden_in)
+    cotangent = swap_rows(cotangent)
     layers = w_qkv.shape[0]
-    local_width = w_qkv.shape[3]
+    w_qkv = [fetch_weight(w_qkv[layer]) for layer in range(layers)]
+    w_out = [fetch_weight(w_out[layer]) for layer in range(layers)]
+    w_up = [fetch_weight(w_up[layer]) for layer in range(layers)]
+    w_down = [fetch_weight(w_down[layer]) for layer in range(layers)]
+    local_width = w_qkv[0].shape[2]
     heads_here = local_width // HEAD_DIM
     stream = hidden_in.astype(f32)
     saved = []
     for layer in range(layers):
         normed = norm_rows(stream, gains[layer, 0], shifts[layer, 0]).astype(bf16)
-        rows_all = lax.all_gather(normed, "tensor", axis=0, tiled=True)
+        rows_all = lax.all_gather(normed, TP, axis=0, tiled=True)
         group_rows = rows_all.shape[0]
         seqs = group_rows // LENGTH
         qkv = jnp.einsum("td,cde->cte", rows_all, w_qkv[layer], preferred_element_type=f32).astype(
@@ -82,14 +120,14 @@
             return jnp.dot(attended, w_out[layer], preferred_element_type=f32)
 
         branch = lax.psum_scatter(
-            project_out(jnp.int32(0), rows * lax.axis_size("tensor")),
-            "tensor",
-            scatter_dimension=0,
-            tiled=True,
-        )
+            project_out(jnp.int32(0), rows * lax.axis_size(TP)).astype(bf16),
+            TP,
+            scatter_dimension=0,
+            tiled=True,
+        ).astype(f32)
         middle = stream + norm_rows(branch, gains[layer, 1], shifts[layer, 1])
         normed2 = norm_rows(middle, gains[layer, 2], shifts[layer, 2]).astype(bf16)
-        ffn_all = lax.all_gather(normed2, "tensor", axis=0, tiled=True)
+        ffn_all = lax.all_gather(normed2, TP, axis=0, tiled=True)
         upper = jnp.dot(ffn_all, w_up[layer], preferred_element_type=f32)
         active = gelu_tanh(upper).astype(bf16)
 
@@ -97,8 +135,8 @@
             return jnp.dot(active, w_down[layer], preferred_element_type=f32)
 
         second = lax.psum_scatter(
-            project_down(jnp.int32(0), lax.axis_size("tensor") * rows).astype(jnp.bfloat16),
-            "tensor",
+            project_down(jnp.int32(0), lax.axis_size(TP) * rows).astype(jnp.bfloat16),
+            TP,
             scatter_dimension=0,
             tiled=True,
         ).astype(jnp.float32)
@@ -118,14 +156,10 @@
             )
         )
         stream = middle + norm_rows(second, gains[layer, 3], shifts[layer, 3])
-    places = lax.axis_index("tensor") * rows + jnp.arange(rows)
-    seq_of_row = places // LENGTH
-    match = group_ids[:, None] == jnp.arange(group_sizes.shape[0])[None, :]
-    counts = jnp.sum(jnp.where(match, group_sizes[None, :], 0), axis=1).astype(f32)
-    seq_weight = 1.0 / counts
-    owner = seq_of_row[:, None] == jnp.arange(group_ids.shape[0])[None, :]
-    row_weight = jnp.sum(jnp.where(owner, seq_weight[None, :], 0.0), axis=1)
-    grad_stream = cotangent.astype(f32) * row_weight[:, None]
+    ids = lax.all_gather(group_ids, "c", axis=0, tiled=True)
+    mine = lax.dynamic_index_in_dim(ids, lax.axis_index("zh"), 0, keepdims=False)
+    count = jnp.sum(jnp.where(jnp.arange(group_sizes.shape[0]) == mine, group_sizes, 0)).astype(f32)
+    grad_stream = cotangent.astype(f32) * (1.0 / count)
     weight_grads = [None] * layers
     gain_grads = [None] * layers
     shift_grads = [None] * layers
@@ -147,7 +181,7 @@
         seqs = group_rows // LENGTH
         _, pull_three = jax.vjp(norm_rows, second, gains[layer, 3], shifts[layer, 3])
         grad_second, gain_three, shift_three = pull_three(grad_stream)
-        second_all = lax.all_gather(grad_second.astype(bf16), "tensor", axis=0, tiled=True)
+        second_all = lax.all_gather(grad_second.astype(bf16), TP, axis=0, tiled=True)
         grad_downw = jnp.einsum("tf,td->fd", active, second_all, preferred_element_type=f32)
         grad_active = jnp.einsum("td,fd->tf", second_all, w_down[layer], preferred_element_type=f32)
         _, gelu_pull = jax.vjp(gelu_tanh, upper)
@@ -158,8 +192,8 @@
             return jnp.einsum("tf,df->td", grad_upper, w_up[layer], preferred_element_type=f32)
 
         grad_normed2 = lax.psum_scatter(
-            back_up(jnp.int32(0), lax.axis_size("tensor") * rows).astype(jnp.bfloat16),
-            "tensor",
+            back_up(jnp.int32(0), lax.axis_size(TP) * rows).astype(jnp.bfloat16),
+            TP,
             scatter_dimension=0,
             tiled=True,
         ).astype(jnp.float32)
@@ -168,7 +202,7 @@
         grad_middle = grad_stream + grad_mid_part
         _, pull_one = jax.vjp(norm_rows, branch, gains[layer, 1], shifts[layer, 1])
         grad_branch, gain_one, shift_one = pull_one(grad_middle)
-        branch_all = lax.all_gather(grad_branch.astype(bf16), "tensor", axis=0, tiled=True)
+        branch_all = lax.all_gather(grad_branch.astype(bf16), TP, axis=0, tiled=True)
         grad_outw = jnp.einsum("te,td->ed", attended, branch_all, preferred_element_type=f32)
         grad_attended = jnp.einsum(
             "td,ed->te", branch_all, w_out[layer], preferred_element_type=f32
@@ -186,8 +220,8 @@
             return jnp.einsum("cte,cde->td", grad_rows, w_qkv[layer], preferred_element_type=f32)
 
         grad_normed = lax.psum_scatter(
-            back_qkv(jnp.int32(0), lax.axis_size("tensor") * rows).astype(jnp.bfloat16),
-            "tensor",
+            back_qkv(jnp.int32(0), lax.axis_size(TP) * rows).astype(jnp.bfloat16),
+            TP,
             scatter_dimension=0,
             tiled=True,
         ).astype(jnp.float32)
@@ -196,34 +230,14 @@
         grad_stream = grad_middle + grad_in_part
         gain_grads[layer] = jnp.stack([gain_zero, gain_one, gain_two, gain_three])
         shift_grads[layer] = jnp.stack([shift_zero, shift_one, shift_two, shift_three])
-        weight_grads[layer] = (grad_qkvw, grad_outw, grad_upw, grad_downw)
+        weight_grads[layer] = tuple(sum_weight(value) for value in (grad_qkvw, grad_outw, grad_upw, grad_downw))
     stacked = [
         jnp.stack([weight_grads[index][member] for index in range(layers)]) for member in range(4)
     ]
-    shared = (
-        lax.psum_scatter(stacked[0], "dp", scatter_dimension=2, tiled=True),
-        lax.psum_scatter(stacked[1], "dp", scatter_dimension=2, tiled=True),
-        lax.psum_scatter(stacked[2], "dp", scatter_dimension=1, tiled=True),
-        lax.psum_scatter(stacked[3], "dp", scatter_dimension=2, tiled=True),
-    )
-    stacked = (
-        lax.all_gather(shared[0].astype(jnp.bfloat16), "dp", axis=2, tiled=True).astype(
-            jnp.float32
-        ),
-        lax.all_gather(shared[1].astype(jnp.bfloat16), "dp", axis=2, tiled=True).astype(
-            jnp.float32
-        ),
-        lax.all_gather(shared[2].astype(jnp.bfloat16), "dp", axis=1, tiled=True).astype(
-            jnp.float32
-        ),
-        lax.all_gather(shared[3].astype(jnp.bfloat16), "dp", axis=2, tiled=True).astype(
-            jnp.float32
-        ),
-    )
-    norm_sums = lax.psum((jnp.stack(gain_grads), jnp.stack(shift_grads)), ("dp", "tensor"))
+    norm_sums = lax.psum((jnp.stack(gain_grads), jnp.stack(shift_grads)), AXES)
     return (
-        stream,
-        grad_stream,
+        swap_rows(stream.astype(bf16)).astype(f32),
+        swap_rows(grad_stream.astype(bf16)).astype(f32),
         stacked[0],
         stacked[1],
         stacked[2],
@@ -234,28 +248,20 @@
 
 
 def solution(mesh):
-    in_specs = (
-        P(("dp", "tensor"), None),
-        P(("dp", "tensor"), None),
-        P("dp"),
-        P(),
-        P(None, None, None, "tensor"),
-        P(None, "tensor", None),
-        P(None, None, "tensor"),
-        P(None, "tensor", None),
-        P(),
-        P(),
-    )
-    out_specs = (
-        P(("dp", "tensor"), None),
-        P(("dp", "tensor"), None),
-        P(None, None, None, "tensor"),
-        P(None, "tensor", None),
-        P(None, None, "tensor"),
-        P(None, "tensor", None),
-        P(),
-        P(),
+    fine = jax.sharding.Mesh(mesh.devices.reshape(-1, 2, 2, 2, 2, 2), AXES)
+    dp = ("gh", "gl", "p", "c")
+    tensor = ("zh", "zl")
+    rows = P((*dp, *tensor), None)
+    weights = (
+        P(None, None, None, tensor),
+        P(None, tensor, None),
+        P(None, None, tensor),
+        P(None, tensor, None),
     )
     return jax.shard_map(
-        per_device, mesh=mesh, in_specs=in_specs, out_specs=out_specs, check_vma=False
-    )
+        per_device,
+        mesh=fine,
+        in_specs=(rows, rows, P(dp), P(), *weights, P(), P()),
+        out_specs=(rows, rows, *weights, P(), P()),
+        check_vma=False,
+    )

time: 1640 us -> 1890 us (1.15)
  waiting for transfers between devices: 1160 us -> 1220 us
  starting transfers between devices: 13.1 us -> 73 us
  blocking collectives: 0 us -> 56.6 us
  local copies, waits for them, and re-layouts: 38 us -> 86.5 us
  matrix products: 292 us -> 316 us
    reduce_scatter x12 -> x16, waiting for transfers between devices: 546 us -> 333 us  [the longest x2 90.6 us: per_device(): lax.psum_scatter(back_up(jnp.int32(0), lax.axis_size(TP) * rows).astype(j...]
    ppermute x0 -> x28, waiting for transfers between devices: none -> 170 us  [the longest x8 88.3 us: sum_weight(): other = lax.ppermute(part, ('c', 'zh'), ((1, 0), (2, 3)))]
    all_gather x12 -> x20, waiting for transfers between devices: 491 us -> 605 us  [the longest x6 176 us: sum_weight(): lax.all_gather(part, BATCH, axis=0, tiled=True).reshape(shape)]
    ppermute x0 -> x28, starting transfers between devices: none -> 69.8 us  [the longest x8 49.6 us: fetch_weight(): part = lax.ppermute(part, ('c', 'zh'), ((0, 1), (3, 2)))]
    all_gather x0 -> x4, blocking collectives: none -> 51.8 us  [the longest x2 27.3 us: fetch_weight(): rest = lax.all_gather(part, SHARE, axis=0, tiled=True).reshape(shape)]
  transfers between devices with their start and end apart: 25 -> 65, of which waited for: 23 -> 50; matrix products, arithmetic and copies ran while one was open for 10% -> 14% of each run, Pallas kernels for 0% -> 0%
where the time goes in v1:
time: 1890 us; the launch traced here: 1880 us
  waiting for transfers between devices  1220 us (65%)
  matrix products  316 us (17%)
  other arithmetic  107 us (6%)
  local copies, waits for them, and re-layouts  86.5 us (5%)
  starting transfers between devices  73 us (4%)
  blocking collectives  56.6 us (3%)
    all_gather x6, waiting for transfers between devices, sum_weight(): lax.all_gather(part, BATCH, axis=0, tiled=True).reshape(shape)  176 us
    psum x1, waiting for transfers between devices, per_device(): norm_sums = lax.psum((jnp.stack(gain_grads), jnp.stack(shift_grads)), AXES)  116 us
    all_gather x6, waiting for transfers between devices, fetch_weight(): rest = lax.all_gather(part, SHARE, axis=0, tiled=True).reshape(shape)  104 us
    all_gather x2, waiting for transfers between devices, per_device(): ffn_all = lax.all_gather(normed2, TP, axis=0, tiled=True)  96.1 us
    all_gather x2, waiting for transfers between devices, per_device(): lax.all_gather(grad_second.astype(bf16), TP, axis=0, tiled=True)  92.7 us
    reduce_scatter x2, waiting for transfers between devices, per_device(): lax.psum_scatter(back_up(jnp.int32(0), lax.axis_size(TP) * rows).astype(j...  90.6 us
    ppermute x8, waiting for transfers between devices, sum_weight(): other = lax.ppermute(part, ('c', 'zh'), ((1, 0), (2, 3)))  88.3 us
    all_gather x2, waiting for transfers between devices, per_device(): rows_all = lax.all_gather(normed, TP, axis=0, tiled=True)  87.5 us
  transfers between devices with their start and end apart: 65, of which 50 were waited for; matrix products, arithmetic and copies ran while one was open for 14% of the time, Pallas kernels for 0%

profile of v1, /device:TPU:0, one launch (start us, length us, event | category | flops | bytes accessed | tf_op | source)
XLA Modules:
  0.0 1880.7 jit_solution(12590580112284078300)
XLA Ops:
  68.5 43.2 %all-gather.23.cloned.1.call-done = bf16[1088,1024]{1,0:T(8,128)(2,1)} async-done(((bf16[272,1024]{1,0:T(8,128)(2,1)}), bf16[1088,1024]{1,0:T(8,128)(2,1)}) %all-gather.23.cloned.1.call-update) | async-done | bytes 2228240 | tf_op jit(solution)/shard_map/all_gather | solution.py:107
  241.5 48.0 %all-gather.25.cloned.1.call-done = bf16[1088,1024]{1,0:T(8,128)(2,1)} async-done(((bf16[272,1024]{1,0:T(8,128)(2,1)}), bf16[1088,1024]{1,0:T(8,128)(2,1)}) %all-gather.25.cloned.1.call-update) | async-done | bytes 2228240 | tf_op jit(solution)/shard_map/all_gather | solution.py:130
  296.3 30.8 %all-gather.29.cloned.1.call-done = bf16[1024,1024]{1,0:T(8,128)(2,1)} async-done(((bf16[256,1024]{1,0:T(8,128)(2,1)}), bf16[1024,1024]{1,0:T(8,128)(2,1)}) %all-gather.29.cloned.1.call-update) | async-done | bytes 2097168 | tf_op jit(solution)/shard_map/all_gather | solution.py:27
  422.6 44.3 %all-gather.33.cloned.1.call-done = bf16[1088,1024]{1,0:T(8,128)(2,1)} async-done(((bf16[272,1024]{1,0:T(8,128)(2,1)}), bf16[1088,1024]{1,0:T(8,128)(2,1)}) %all-gather.33.cloned.1.call-update) | async-done | bytes 2228240 | tf_op jit(solution)/shard_map/all_gather | solution.py:107
  531.5 26.5 %reduce-scatter.21.cloned.1.call-done = bf16[272,1024]{1,0:T(8,128)(2,1)} async-done(((bf16[1088,1024]{1,0:T(8,128)(2,1)}), bf16[272,1024]{1,0:T(8,128)(2,1)}) %reduce-scatter.21.cloned.1.call-update) | async-done | bytes 557072 | tf_op jit(solution)/shard_map/reduce_scatter | solution.py:122
  594.9 48.0 %all-gather.35.cloned.1.call-done = bf16[1088,1024]{1,0:T(8,128)(2,1)} async-done(((bf16[272,1024]{1,0:T(8,128)(2,1)}), bf16[1088,1024]{1,0:T(8,128)(2,1)}) %all-gather.35.cloned.1.call-update) | async-done | bytes 2228240 | tf_op jit(solution)/shard_map/all_gather | solution.py:130
  649.8 30.9 %all-gather.39.cloned.1.call-done = bf16[1024,1024]{1,0:T(8,128)(2,1)} async-done(((bf16[256,1024]{1,0:T(8,128)(2,1)}), bf16[1024,1024]{1,0:T(8,128)(2,1)}) %all-gather.39.cloned.1.call-update) | async-done | bytes 2097168 | tf_op jit(solution)/shard_map/all_gather | solution.py:27
  699.1 39.4 %reduce-scatter.23.cloned.1.call-done = bf16[272,1024]{1,0:T(8,128)(2,1)} async-done(((bf16[1088,1024]{1,0:T(8,128)(2,1)}), bf16[272,1024]{1,0:T(8,128)(2,1)}) %reduce-scatter.23.cloned.1.call-update) | async-done | bytes 557072 | tf_op jit(solution)/shard_map/reduce_scatter | solution.py:137
  744.9 46.6 %all-gather.41.cloned.1.call-done = bf16[1088,1024]{1,0:T(8,128)(2,1)} async-done(((bf16[272,1024]{1,0:T(8,128)(2,1)}), bf16[1088,1024]{1,0:T(8,128)(2,1)}) %all-gather.41.cloned.1.call-update) | async-done | bytes 2228240 | tf_op jit(solution)/shard_map/all_gather | solution.py:184
  804.9 45.3 %reduce-scatter.25.cloned.1.call-done = bf16[272,1024]{1,0:T(8,128)(2,1)} async-done(((bf16[1088,1024]{1,0:T(8,128)(2,1)}), bf16[272,1024]{1,0:T(8,128)(2,1)}) %reduce-scatter.25.cloned.1.call-update) | async-done | bytes 557072 | tf_op jit(solution)/shard_map/reduce_scatter | solution.py:194
  859.5 45.6 %all-gather.43.cloned.1.call-done = bf16[1088,1024]{1,0:T(8,128)(2,1)} async-done(((bf16[272,1024]{1,0:T(8,128)(2,1)}), bf16[1088,1024]{1,0:T(8,128)(2,1)}) %all-gather.43.cloned.1.call-update) | async-done | bytes 2228240 | tf_op jit(solution)/shard_map/all_gather | solution.py:205
  930.2 27.3 %fusion.62 = bf16[4,64,1088]{2,1,0:T(8,128)(2,1)S(1)} fusion(bf16[1088,4,64]{0,2,1:T(8,128)(2,1)S(1)} %bitcast.217, f32[4,1088,1088]{1,2,0:T(8,128)} %fusion.227, f32[4,1088,1088]{1,2,0:T(8,128)} %get-tuple-element.167, f32[4,1088]{1,0:T(4,128)S(1)} %log_add_fusion.1), kind=kOutput, calls=%fused_computation.78 | convolution fusion | flops 653710656 | bytes 39011328 | tf_op jit(solution)/shard_map/while/body/eval_jaxpr/hqk,khd->qhd/dot_general | solution.py:80
  957.5 28.0 %fusion.65 = bf16[4,64,1088]{2,1,0:T(8,128)(2,1)} fusion(bf16[1088,4,64]{0,2,1:T(8,128)(2,1)S(1)} %bitcast.219, f32[4,1088,1088]{1,2,0:T(8,128)} %fusion.227, f32[4,1088,1088]{1,2,0:T(8,128)} %get-tuple-element.167, f32[4,1088]{1,0:T(4,128)S(1)} %log_add_fusion.1), kind=kOutput, calls=%fused_computation.79 | convolution fusion | flops 653710656 | bytes 39011328 | tf_op jit(solution)/shard_map/while/body/eval_jaxpr/hqk,qhd->khd/dot_general | solution.py:81
  995.1 45.0 %reduce-scatter.27.cloned.1.call-done = bf16[272,1024]{1,0:T(8,128)(2,1)} async-done(((bf16[1088,1024]{1,0:T(8,128)(2,1)}), bf16[272,1024]{1,0:T(8,128)(2,1)}) %reduce-scatter.27.cloned.1.call-update) | async-done | bytes 557072 | tf_op jit(solution)/shard_map/reduce_scatter | solution.py:222
  1046.4 46.1 %all-gather.45.cloned.1.call-done = bf16[1088,1024]{1,0:T(8,128)(2,1)} async-done(((bf16[272,1024]{1,0:T(8,128)(2,1)}), bf16[1088,1024]{1,0:T(8,128)(2,1)}) %all-gather.45.cloned.1.call-update) | async-done | bytes 2228240 | tf_op jit(solution)/shard_map/all_gather | solution.py:184
  1106.4 45.3 %reduce-scatter.29.cloned.1.call-done = bf16[272,1024]{1,0:T(8,128)(2,1)} async-done(((bf16[1088,1024]{1,0:T(8,128)(2,1)}), bf16[272,1024]{1,0:T(8,128)(2,1)}) %reduce-scatter.29.cloned.1.call-update) | async-done | bytes 557072 | tf_op jit(solution)/shard_map/reduce_scatter | solution.py:194
  1229.7 28.8 %fusion.59 = bf16[4,64,1088]{2,1,0:T(8,128)(2,1)} fusion(bf16[1088,4,64]{0,2,1:T(8,128)(2,1)S(1)} %bitcast.215, f32[4,1088,1088]{1,2,0:T(8,128)} %fusion.228, f32[4,1088,1088]{1,2,0:T(8,128)} %get-tuple-element.165, f32[4,1088]{1,0:T(4,128)S(1)} %log_add_fusion), kind=kOutput, calls=%fused_computation.77 | convolution fusion | flops 653710656 | bytes 39011328 | tf_op jit(solution)/shard_map/while/body/eval_jaxpr/hqk,qhd->khd/dot_general | solution.py:81
  1260.6 27.7 %fusion.56 = bf16[4,64,1088]{2,1,0:T(8,128)(2,1)S(1)} fusion(bf16[1088,4,64]{0,2,1:T(8,128)(2,1)S(1)} %bitcast.213, f32[4,1088,1088]{1,2,0:T(8,128)} %fusion.228, f32[4,1088,1088]{1,2,0:T(8,128)} %get-tuple-element.165, f32[4,1088]{1,0:T(4,128)S(1)} %log_add_fusion), kind=kOutput, calls=%fused_computation.76 | convolution fusion | flops 653710656 | bytes 39011328 | tf_op jit(solution)/shard_map/while/body/eval_jaxpr/hqk,khd->qhd/dot_general | solution.py:80
  1522.8 30.8 %all-gather.55.cloned.1.call-done = bf16[1024,1024]{1,0:T(8,128)(2,1)} async-done(((bf16[256,1024]{1,0:T(8,128)(2,1)}), bf16[1024,1024]{1,0:T(8,128)(2,1)}) %all-gather.55.cloned.1.call-update) | async-done | bytes 2097168 | tf_op jit(solution)/shard_map/all_gather | solution.py:39
  1553.6 37.8 %all-gather.53.cloned.1.call-done = bf16[1024,1024]{1,0:T(8,128)(2,1)} async-done(((bf16[256,1024]{1,0:T(8,128)(2,1)}), bf16[1024,1024]{1,0:T(8,128)(2,1)}) %all-gather.53.cloned.1.call-update) | async-done | bytes 2097168 | tf_op jit(solution)/shard_map/all_gather | solution.py:39
  1600.5 27.9 %all-gather.59.cloned.1.call-done = bf16[1024,1024]{1,0:T(8,128)(2,1)} async-done(((bf16[256,1024]{1,0:T(8,128)(2,1)}), bf16[1024,1024]{1,0:T(8,128)(2,1)}) %all-gather.59.cloned.1.call-update) | async-done | bytes 2097168 | tf_op jit(solution)/shard_map/all_gather | solution.py:39
  1628.4 37.8 %all-gather.57.cloned.1.call-done = bf16[1024,1024]{1,0:T(8,128)(2,1)} async-done(((bf16[256,1024]{1,0:T(8,128)(2,1)}), bf16[1024,1024]{1,0:T(8,128)(2,1)}) %all-gather.57.cloned.1.call-update) | async-done | bytes 2097168 | tf_op jit(solution)/shard_map/all_gather | solution.py:39
  1684.1 29.9 %reduce-scatter.31.cloned.1.call-done = bf16[272,1024]{1,0:T(8,128)(2,1)} async-done(((bf16[1088,1024]{1,0:T(8,128)(2,1)}), bf16[272,1024]{1,0:T(8,128)(2,1)}) %reduce-scatter.31.cloned.1.call-update) | async-done | bytes 557072 | tf_op jit(solution)/shard_map/reduce_scatter | solution.py:222
  1754.9 116.0 %all-reduce.4.cloned.1.call-done = (f32[2,4,1024]{2,1,0:T(4,128)}, f32[2,4,1024]{2,1,0:T(4,128)}) async-done(((f32[2,4,1024]{2,1,0:T(4,128)}, f32[2,4,1024]{2,1,0:T(4,128)}), (f32[2,4,1024]{2,1,0:T(4,128)}, f32[2,4,1024]{2,1,0:T(4,128)})) %all-reduce.4.cloned.1.call-update) | async-done | bytes 65552 | tf_op jit(solution)/shard_map/psum | solution.py:237
  (577 shorter events, 885.9 us)
Async XLA Ops:
  28.2 176.4 %reduce-scatter.17.cloned.1.call-start = ((), (), s32[]{:S(2)}) async-start(), calls=%async_computation.18 | async-start | bytes 2785280 | tf_op jit(solution)/shard_map/reduce_scatter | solution.py:122
  211.9 115.2 %all-gather.29.cloned.1.call-start = ((), (), s32[]{:S(2)}) async-start(), calls=%async_computation.21 | async-start | bytes 2621440 | tf_op jit(solution)/shard_map/all_gather | solution.py:27
  227.2 157.1 %reduce-scatter.19.cloned.1.call-start = ((), (), s32[]{:S(2)}) async-start(), calls=%async_computation.22 | async-start | bytes 2785280 | tf_op jit(solution)/shard_map/reduce_scatter | solution.py:137
  390.2 167.7 %reduce-scatter.21.cloned.1.call-start = ((), (), s32[]{:S(2)}) async-start(), calls=%async_computation.25 | async-start | bytes 2785280 | tf_op jit(solution)/shard_map/reduce_scatter | solution.py:122
  531.2 111.7 %all-gather.35.cloned.1.call-start = ((), (), s32[]{:S(2)}) async-start(), calls=%async_computation.26 | async-start | bytes 2785280 | tf_op jit(solution)/shard_map/all_gather | solution.py:130
  563.5 117.2 %all-gather.39.cloned.1.call-start = ((), (), s32[]{:S(2)}) async-start(), calls=%async_computation.28 | async-start | bytes 2621440 | tf_op jit(solution)/shard_map/all_gather | solution.py:27
  573.8 164.7 %reduce-scatter.23.cloned.1.call-start = ((), (), s32[]{:S(2)}) async-start(), calls=%async_computation.29 | async-start | bytes 2785280 | tf_op jit(solution)/shard_map/reduce_scatter | solution.py:137
  859.0 181.2 %reduce-scatter.27.cloned.1.call-start = ((), (), s32[]{:S(2)}) async-start(), calls=%async_computation.33 | async-start | bytes 2785280 | tf_op jit(solution)/shard_map/reduce_scatter | solution.py:222
  1157.2 141.7 %reduce-scatter.35.cloned.1.call-start = ((), (), s32[]{:S(2)}) async-start(), calls=%async_computation.40 | async-start | bytes 1966080 | tf_op jit(solution)/shard_map/reduce_scatter | solution.py:34
  1166.8 150.7 %reduce-scatter.43.cloned.1.call-start = ((), (), s32[]{:S(2)}) async-start(), calls=%async_computation.46 | async-start | bytes 2621440 | tf_op jit(solution)/shard_map/reduce_scatter | solution.py:34
  1173.6 163.0 %reduce-scatter.41.cloned.1.call-start = ((), (), s32[]{:S(2)}) async-start(), calls=%async_computation.44 | async-start | bytes 2621440 | tf_op jit(solution)/shard_map/reduce_scatter | solution.py:34
  1180.2 176.5 %reduce-scatter.47.cloned.1.call-start = ((), (), s32[]{:S(2)}) async-start(), calls=%async_computation.50 | async-start | bytes 2621440 | tf_op jit(solution)/shard_map/reduce_scatter | solution.py:34
  1188.0 204.1 %reduce-scatter.45.cloned.1.call-start = ((), (), s32[]{:S(2)}) async-start(), calls=%async_computation.48 | async-start | bytes 2621440 | tf_op jit(solution)/shard_map/reduce_scatter | solution.py:34
  1195.7 225.0 %reduce-scatter.39.cloned.1.call-start = ((), (), s32[]{:S(2)}) async-start(), calls=%async_computation.43 | async-start | bytes 655360 | tf_op jit(solution)/shard_map/reduce_scatter | solution.py:34
  1200.1 253.7 %reduce-scatter.33.cloned.1.call-start = ((), (), s32[]{:S(2)}) async-start(), calls=%async_computation.38 | async-start | bytes 1966080 | tf_op jit(solution)/shard_map/reduce_scatter | solution.py:34
  1298.9 189.3 %all-gather.51.cloned.1.call-start = ((), (), s32[]{:S(2)}) async-start(), calls=%async_computation.41 | async-start | bytes 1966080 | tf_op jit(solution)/shard_map/all_gather | solution.py:39
  1317.4 199.0 %reduce-scatter.37.cloned.1.call-start = ((), (), s32[]{:S(2)}) async-start(), calls=%async_computation.42 | async-start | bytes 655360 | tf_op jit(solution)/shard_map/reduce_scatter | solution.py:34
  1322.2 231.4 %all-gather.55.cloned.1.call-start = ((), (), s32[]{:S(2)}) async-start(), calls=%async_computation.47 | async-start | bytes 2621440 | tf_op jit(solution)/shard_map/all_gather | solution.py:39
  1336.5 254.9 %all-gather.53.cloned.1.call-start = ((), (), s32[]{:S(2)}) async-start(), calls=%async_computation.45 | async-start | bytes 2621440 | tf_op jit(solution)/shard_map/all_gather | solution.py:39
  1356.7 271.8 %all-gather.59.cloned.1.call-start = ((), (), s32[]{:S(2)}) async-start(), calls=%async_computation.51 | async-start | bytes 2621440 | tf_op jit(solution)/shard_map/all_gather | solution.py:39
  1376.8 289.4 %all-gather.57.cloned.1.call-start = ((), (), s32[]{:S(2)}) async-start(), calls=%async_computation.49 | async-start | bytes 2621440 | tf_op jit(solution)/shard_map/all_gather | solution.py:39
  1413.9 300.1 %reduce-scatter.31.cloned.1.call-start = ((), (), s32[]{:S(2)}) async-start(), calls=%async_computation.37 | async-start | bytes 2785280 | tf_op jit(solution)/shard_map/reduce_scatter | solution.py:222
  1419.0 327.7 %all-gather.49.cloned.1.call-start = ((), (), s32[]{:S(2)}) async-start(), calls=%async_computation.39 | async-start | bytes 1966080 | tf_op jit(solution)/shard_map/all_gather | solution.py:39
  1600.5 270.4 %all-reduce.4.cloned.1.call-start = ((), (), s32[]{:S(2)}) async-start(), calls=%async_computation.52 | async-start | bytes 131072 | tf_op jit(solution)/shard_map/psum | solution.py:237
  (163 other events, 5589.3 us)
Sparse Core Ops, SparseCore 0:
  23.7 38.4 all-gather.20
  64.3 47.4 all-gather.22
  153.7 50.9 reduce-scatter.16
  243.5 46.0 all-gather.24
  291.8 35.2 all-gather.28
  334.5 49.6 reduce-scatter.18
  421.0 45.9 all-gather.32
  507.0 50.8 reduce-scatter.20
  596.9 46.0 all-gather.34
  645.4 35.2 all-gather.38
  688.1 50.4 reduce-scatter.22
  744.8 46.7 all-gather.40
  805.0 45.1 reduce-scatter.24
  859.1 46.0 all-gather.42
  995.1 44.9 reduce-scatter.26
  1046.5 45.9 all-gather.44
  1106.4 45.1 reduce-scatter.28
  1157.3 45.9 all-gather.46
  1518.3 35.2 all-gather.54
  1556.1 35.2 all-gather.52
  1593.1 35.2 all-gather.58
  1630.9 35.2 all-gather.56
  1669.1 44.8 reduce-scatter.30
  1752.8 118.0 all-reduce.3
  (13 shorter events, 417.0 us)

commit v2 on v1

v2 whole, which is shorter than its diff:
```python
import functools

import jax
import jax.numpy as jnp
from jax import lax
from jax.experimental import pallas as pl
from jax.experimental.pallas import tpu as pltpu
from jax.sharding import PartitionSpec as P

HEAD_DIM = 64
LENGTH = 1088
AXES = ("gh", "gl", "p", "c", "zh", "zl")
f32 = jnp.float32
bf16 = jnp.bfloat16
MESH = pl.DeviceIdType.MESH
eps_norm = 1e-05
TILE = 256


def centre(values):
    mean = jnp.mean(values, axis=-1, keepdims=True)
    centred = values - mean
    spread = jnp.mean(centred * centred, axis=-1, keepdims=True)
    rate = lax.rsqrt(spread + eps_norm)
    return centred * rate, rate


def norm_rows(values, gain, shift):
    return centre(values)[0] * gain + shift


def norm_pull(values, gain, grad):
    hat, rate = centre(values)
    scaled = grad * gain
    along = jnp.mean(scaled * hat, axis=-1, keepdims=True)
    level = jnp.mean(scaled, axis=-1, keepdims=True)
    return (
        rate * (scaled - level - hat * along),
        jnp.sum(grad * hat, axis=0, keepdims=True),
        jnp.sum(grad, axis=0, keepdims=True),
    )


def dot_nt(left, right):
    return lax.dot_general(left, right, (((1,), (1,)), ((), ())), preferred_element_type=f32)


def dot_tn(left, right):
    return lax.dot_general(left, right, (((0,), (0,)), ((), ())), preferred_element_type=f32)


def dot_nn(left, right):
    return jnp.dot(left, right, preferred_element_type=f32)


def cut_rows(rows):
    first = (rows // 2 + 15) // 16 * 16
    return ((0, first), (first, rows - first))


def greet():
    mate = {"c": 1 - lax.axis_index("c")}
    near = {"zl": 1 - lax.axis_index("zl")}
    barrier = pltpu.get_barrier_semaphore()
    for other in (mate, near):
        pl.semaphore_signal(barrier, inc=1, device_id=other, device_id_type=MESH)
    pl.semaphore_wait(barrier, 2)
    return mate, near


def remote(source, target, send, receive, device):
    return pltpu.make_async_remote_copy(
        src_ref=source,
        dst_ref=target,
        send_sem=send,
        recv_sem=receive,
        device_id=device,
        device_id_type=MESH,
    )


def tiles(width, body):
    def step(index, carry):
        body(pl.ds(pl.multiple_of(index * TILE, TILE), TILE))
        return carry

    lax.fori_loop(0, width // TILE, step, 0)


def exchange(rows, mate, near, held, work, first, sums, send, receive):
    own = pl.ds(0, rows)
    parts = cut_rows(rows)
    copies = [remote(held.at[own], held.at[pl.ds(rows, rows)], send.at[0], receive.at[0], mate)]
    copies[0].start()
    along = []
    for index, (start, size) in enumerate(parts):
        place = pl.ds(2 * rows + 2 * start, size)
        copy = remote(held.at[pl.ds(start, size)], held.at[place], send.at[1 + index], receive.at[1 + index], near)
        copy.start()
        along.append(copy)

    def keep(row, columns, value):
        first[pl.ds(row, value.shape[0]), columns] = value

    work(0, rows, keep)
    copies[0].wait_recv()

    def keep_mate(row, columns, value):
        sums[0, pl.ds(row - rows, value.shape[0]), columns] = value.astype(bf16)

    work(rows, rows, keep_mate)
    back = remote(sums.at[0], sums.at[1], send.at[3], receive.at[3], mate)
    back.start()
    copies.append(back)
    final = []
    for index, (start, size) in enumerate(parts):
        place = 2 * rows + 2 * start
        along[index].wait_recv()
        relay = remote(
            held.at[pl.ds(place, size)], held.at[pl.ds(place + size, size)], send.at[4 + index], receive.at[4 + index], mate
        )
        relay.start()
        relay.wait_recv()

        def keep_far(row, columns, value, place=place, start=start, size=size):
            first[pl.ds(rows + start, size), columns] = value[:size]
            sums[2, pl.ds(start, size), columns] = value[size:].astype(bf16)

        work(place, 2 * size, keep_far)
        part = pl.ds(start, size)
        cross = remote(sums.at[2, part], sums.at[3, part], send.at[6 + index], receive.at[6 + index], mate)
        cross.start()
        cross.wait_recv()
        sums[4, part, :] = (first[pl.ds(rows + start, size), :] + sums[3, part, :].astype(f32)).astype(bf16)
        last = remote(sums.at[4, part], sums.at[5, part], send.at[8 + index], receive.at[8 + index], near)
        last.start()
        final.append(last)
        copies += [relay, cross]

    def finish():
        back.wait_recv()
        for copy in final:
            copy.wait_recv()
        for copy in copies + along + final:
            copy.wait_send()

    return finish


def gelu_and_slope(values):
    rate, cubic = 0.7978845608028654, 0.044715
    square = values * values
    bend = jnp.tanh(rate * values * (1.0 + cubic * square))
    half = 0.5 * (1.0 + bend)
    slope = half + 0.5 * values * (1.0 - bend * bend) * (rate * (1.0 + 3.0 * cubic * square))
    return values * half, slope


def ffn_forward_kernel(
    layer, middle, gains, shifts, w_up, w_down, second, stream, held_out, active_out, slope_out,
    held, active, slope, up, down, first, sums, send, receive, local,
):
    rows = middle.shape[0]
    loads = [pltpu.make_async_copy(w_up, up, local.at[0]), pltpu.make_async_copy(w_down, down, local.at[1])]
    for copy in loads:
        copy.start()
    mate, near = greet()
    held[pl.ds(0, rows), :] = norm_rows(middle[...], gains[2:3, :], shifts[2:3, :]).astype(bf16)
    for copy in loads:
        copy.wait()

    def work(start, size, sink):
        here = pl.ds(start, size)

        def step(columns):
            upper = dot_nn(held[here, :], up[:, columns])
            value, bend = gelu_and_slope(upper)
            active[here, columns] = value.astype(bf16)
            slope[here, columns] = bend.astype(bf16)

        tiles(up.shape[1], step)

        def step_down(columns):
            sink(start, columns, dot_nn(active[here, :], down[:, columns]))

        tiles(down.shape[1], step_down)

    finish = exchange(rows, mate, near, held, work, first, sums, send, receive)
    stores = [
        pltpu.make_async_copy(held, held_out, local.at[2]),
        pltpu.make_async_copy(active, active_out, local.at[3]),
        pltpu.make_async_copy(slope, slope_out, local.at[4]),
    ]
    for copy in stores:
        copy.start()
    finish()
    total = first[pl.ds(0, rows), :] + sums[1].astype(f32) + sums[5].astype(f32)
    second[...] = total
    stream[...] = middle[...] + norm_rows(total, gains[3:4, :], shifts[3:4, :])
    for copy in stores:
        copy.wait()


def vmem(count):
    return [pl.BlockSpec(memory_space=pltpu.VMEM)] * count


def anywhere(count):
    return [pl.BlockSpec(memory_space=pl.ANY)] * count


def sums_scratch(rows, width):
    return [
        pltpu.VMEM((2 * rows, width), f32),
        pltpu.VMEM((6, rows, width), bf16),
        pltpu.SemaphoreType.DMA((10,)),
        pltpu.SemaphoreType.DMA((10,)),
    ]


def ffn_forward(middle, gains, shifts, w_up, w_down):
    rows, width = middle.shape
    hidden = w_up.shape[1]
    shape = jax.ShapeDtypeStruct
    return pl.pallas_call(
        functools.partial(ffn_forward_kernel, 0),
        out_shape=(
            shape((rows, width), f32),
            shape((rows, width), f32),
            shape((4 * rows, width), bf16),
            shape((4 * rows, hidden), bf16),
            shape((4 * rows, hidden), bf16),
        ),
        in_specs=vmem(3) + anywhere(2),
        out_specs=vmem(2) + anywhere(3),
        scratch_shapes=[
            pltpu.VMEM((4 * rows, width), bf16),
            pltpu.VMEM((4 * rows, hidden), bf16),
            pltpu.VMEM((4 * rows, hidden), bf16),
            pltpu.VMEM(w_up.shape, bf16),
            pltpu.VMEM(w_down.shape, bf16),
            *sums_scratch(rows, width),
            pltpu.SemaphoreType.DMA((5,)),
        ],
        compiler_params=pltpu.CompilerParams(collective_id=0, has_side_effects=True, vmem_limit_bytes=56 << 20),
        cost_estimate=pl.CostEstimate(flops=16 * rows * width * hidden, bytes_accessed=24 << 20, transcendentals=4 * rows * hidden),
    )(middle, gains, shifts, w_up, w_down)


def ffn_backward_kernel(
    layer, grad, second, middle, gains, shifts, held_in, active_in, slope_in, w_up, w_down,
    grad_middle, sums_out, grad_up, grad_down,
    held, past, active, slope, pushed, up, down, outcome, first, sums, send, receive, local,
):
    rows = middle.shape[0]
    loads = [
        pltpu.make_async_copy(w_down, down, local.at[0]),
        pltpu.make_async_copy(w_up, up, local.at[1]),
        pltpu.make_async_copy(slope_in, slope, local.at[2]),
        pltpu.make_async_copy(active_in, active, local.at[3]),
        pltpu.make_async_copy(held_in, past, local.at[4]),
    ]
    for copy in loads:
        copy.start()
    mate, near = greet()
    pulled, gain_three, shift_three = norm_pull(second[...], gains[3:4, :], grad[...])
    held[pl.ds(0, rows), :] = pulled.astype(bf16)
    for copy in loads:
        copy.wait()

    def work(start, size, sink):
        here = pl.ds(start, size)

        def step(columns):
            value = dot_nt(held[here, :], down[columns, :])
            pushed[here, columns] = (value * slope[here, columns].astype(f32)).astype(bf16)

        tiles(down.shape[0], step)

        def step_up(columns):
            sink(start, columns, dot_nt(pushed[here, :], up[columns, :]))

        tiles(up.shape[0], step_up)

    finish = exchange(rows, mate, near, held, work, first, sums, send, receive)

    def step_down(columns):
        outcome[0, columns, :] = dot_tn(active[:, columns], held[...]).astype(bf16)

    tiles(down.shape[0], step_down)
    out_down = pltpu.make_async_copy(outcome.at[0], grad_down, local.at[0])
    out_down.start()

    def step_up(columns):
        outcome[1, columns, :] = dot_tn(past[:, columns], pushed[...]).astype(bf16)

    tiles(up.shape[0], step_up)
    out_up = pltpu.make_async_copy(outcome.at[1], grad_up, local.at[1])
    out_up.start()
    finish()
    total = first[pl.ds(0, rows), :] + sums[1].astype(f32) + sums[5].astype(f32)
    pulled, gain_two, shift_two = norm_pull(middle[...], gains[2:3, :], total)
    grad_middle[...] = grad[...] + pulled
    sums_out[0:1, :] = gain_two
    sums_out[1:2, :] = shift_two
    sums_out[2:3, :] = gain_three
    sums_out[3:4, :] = shift_three
    out_down.wait()
    out_up.wait()


def ffn_backward(grad, second, middle, gains, shifts, held, active, slope, w_up, w_down):
    rows, width = middle.shape
    hidden = w_up.shape[1]
    shape = jax.ShapeDtypeStruct
    return pl.pallas_call(
        functools.partial(ffn_backward_kernel, 0),
        out_shape=(
            shape((rows, width), f32),
            shape((4, width), f32),
            shape(w_up.shape, bf16),
            shape(w_down.shape, bf16),
        ),
        in_specs=vmem(5) + anywhere(5),
        out_specs=vmem(2) + anywhere(2),
        scratch_shapes=[
            pltpu.VMEM((4 * rows, width), bf16),
            pltpu.VMEM((4 * rows, width), bf16),
            pltpu.VMEM((4 * rows, hidden), bf16),
            pltpu.VMEM((4 * rows, hidden), bf16),
            pltpu.VMEM((4 * rows, hidden), bf16),
            pltpu.VMEM(w_up.shape, bf16),
            pltpu.VMEM(w_down.shape, bf16),
            pltpu.VMEM((2, width, hidden), bf16),
            *sums_scratch(rows, width),
            pltpu.SemaphoreType.DMA((5,)),
        ],
        compiler_params=pltpu.CompilerParams(collective_id=1, has_side_effects=True, vmem_limit_bytes=56 << 20),
        cost_estimate=pl.CostEstimate(flops=32 * rows * width * hidden, bytes_accessed=32 << 20, transcendentals=0),
    )(grad, second, middle, gains, shifts, held, active, slope, w_up, w_down)


def places(rows):
    c, zl = lax.axis_index("c"), lax.axis_index("zl")

    def at(core, part):
        return pl.multiple_of((2 * core + part) * rows, 16)

    return at(c, zl), at(1 - c, zl), at(c, 1 - zl), at(1 - c, 1 - zl)


def gather(rows, mate, near, held, arrived, send, receive):
    own, others, along, across = places(rows)
    parts = cut_rows(rows)
    here = pl.ds(own, rows)
    copies = [remote(held.at[here], held.at[here], send.at[0], receive.at[0], mate)]
    copies[0].start()
    for index, (start, size) in enumerate(parts):
        part = pl.ds(pl.multiple_of(own + start, 16), size)
        copy = remote(held.at[part], held.at[part], send.at[1 + index], receive.at[1 + index], near)
        copy.start()
        copies.append(copy)
    arrived(own, rows)
    copies[0].wait_recv()
    arrived(others, rows)
    for index, (start, size) in enumerate(parts):
        copies[1 + index].wait_recv()
        first = pl.multiple_of(along + start, 16)
        part = pl.ds(first, size)
        relay = remote(held.at[part], held.at[part], send.at[4 + index], receive.at[4 + index], mate)
        relay.start()
        copies.append(relay)
        arrived(first, size)
        relay.wait_recv()
        arrived(pl.multiple_of(across + start, 16), size)

    def finish():
        for copy in copies:
            copy.wait_send()

    return finish


def scatter(rows, mate, near, project, first, sums, send, receive):
    own, others, along, across = places(rows)
    parts = cut_rows(rows)
    copies, crossing, final = [], [], []
    for index, (start, size) in enumerate(parts):
        part = pl.ds(start, size)

        def keep_far(columns, value, part=part):
            sums[2, part, columns] = value.astype(bf16)

        project(pl.multiple_of(across + start, 16), size, keep_far)
        cross = remote(sums.at[2, part], sums.at[3, part], send.at[6 + index], receive.at[6 + index], mate)
        cross.start()
        crossing.append(cross)
    for index, (start, size) in enumerate(parts):
        part = pl.ds(start, size)

        def keep_near(columns, value, start=start, size=size):
            first[pl.ds(rows + start, size), columns] = value

        project(pl.multiple_of(along + start, 16), size, keep_near)
        crossing[index].wait_recv()
        sums[4, part, :] = (first[pl.ds(rows + start, size), :] + sums[3, part, :].astype(f32)).astype(bf16)
        last = remote(sums.at[4, part], sums.at[5, part], send.at[8 + index], receive.at[8 + index], near)
        last.start()
        final.append(last)

    def keep_mate(columns, value):
        sums[0, :, columns] = value.astype(bf16)

    project(others, rows, keep_mate)
    back = remote(sums.at[0], sums.at[1], send.at[3], receive.at[3], mate)
    back.start()

    def keep(columns, value):
        first[pl.ds(0, rows), columns] = value

    project(own, rows, keep)

    def finish():
        back.wait_recv()
        for copy in final:
            copy.wait_recv()
        for copy in [back] + crossing + final:
            copy.wait_send()

    return finish


def head_lanes(shape, half):
    lane = lax.broadcasted_iota(jnp.int32, shape, len(shape) - 1)
    return (lane < HEAD_DIM) if half == 0 else (lane >= HEAD_DIM)


def masked(scores, start, first_key):
    query = lax.broadcasted_iota(jnp.int32, scores.shape, 0) + start
    key = lax.broadcasted_iota(jnp.int32, scores.shape, 1) + first_key
    return jnp.where(key <= query, scores, -1e30)


def spans(rows, high):
    if not high:
        return ((0, 2 * rows, True),)
    free = 2 * rows // 128 * 128
    return ((0, free, False), (free, 4 * rows - free, True))


def attend_block(rows, start, high, qkv, attended, lse):
    width = attended.shape[1]
    here = pl.ds(start, rows)
    lane = lax.broadcasted_iota(jnp.int32, (rows, 128), 1)
    tops = jnp.zeros((rows, 128), f32)
    for pair in range(width // 128):
        columns = slice(pair * 128, pair * 128 + 128)
        query = qkv[here, columns] * bf16(HEAD_DIM ** (-0.5))
        results = []
        for half in range(2):
            only = jnp.where(head_lanes(query.shape, half), query, 0)
            scores = []
            for begin, size, mask in spans(rows, high):
                part = dot_nt(only, qkv[pl.ds(begin, size), width + pair * 128 : width + pair * 128 + 128])
                scores.append(masked(part, start, begin) if mask else part)
            top = functools.reduce(jnp.maximum, [jnp.max(part, axis=-1, keepdims=True) for part in scores])
            total, result = 0.0, 0.0
            for (begin, size, _), part in zip(spans(rows, high), scores):
                weights = jnp.exp(part - top)
                total = total + jnp.sum(weights, axis=-1, keepdims=True)
                values = qkv[pl.ds(begin, size), 2 * width + pair * 128 : 2 * width + pair * 128 + 128]
                result = result + dot_nn(weights.astype(bf16), values)
            results.append(result / total)
            tops = jnp.where(lane == 2 * pair + half, top + jnp.log(total), tops)
        attended[here, columns] = jnp.where(head_lanes((rows, 128), 0), results[0], results[1]).astype(bf16)
    lse[here, :] = tops


def attention_forward_kernel(
    layer, stream, gains, shifts, w_qkv, w_out, branch, middle, held_out, qkv_out, attended_out, lse_out,
    held, qkv, attended, lse, weight, project, first, sums, send, receive, local,
):
    rows = stream.shape[0]
    width = attended.shape[1]
    loads = [
        pltpu.make_async_copy(w_qkv.at[index], weight.at[:, pl.ds(index * width, width)], local.at[index]) for index in range(3)
    ]
    loads.append(pltpu.make_async_copy(w_out, project, local.at[3]))
    for copy in loads:
        copy.start()
    mate, near = greet()
    own, others, along, across = places(rows)
    held[pl.ds(own, rows), :] = norm_rows(stream[...], gains[0:1, :], shifts[0:1, :]).astype(bf16)
    for copy in loads:
        copy.wait()

    def arrived(start, size):
        here = pl.ds(start, size)

        def step(columns):
            qkv[here, columns] = dot_nn(held[here, :], weight[:, columns]).astype(bf16)

        tiles(3 * width, step)

    sent = gather(rows, mate, near, held, arrived, send, receive)
    stores = [pltpu.make_async_copy(held, held_out, local.at[0]), pltpu.make_async_copy(qkv, qkv_out, local.at[1])]
    for copy in stores:
        copy.start()
    zl = lax.axis_index("zl")

    def at(quarter):
        return pl.multiple_of(quarter * rows, 16)

    attend_block(rows, at(3 - zl), True, qkv, attended, lse)
    attend_block(rows, at(1 - zl), False, qkv, attended, lse)
    done = []

    def term(start, size, sink):
        if size == rows and not done:
            done.append(True)
            attend_block(rows, at(2 + zl), True, qkv, attended, lse)
            attend_block(rows, at(zl), False, qkv, attended, lse)
        here = pl.ds(start, size)

        def step(columns):
            sink(columns, dot_nn(attended[here, :], project[:, columns]))

        tiles(project.shape[1], step)

    finish = scatter(rows, mate, near, term, first, sums, send, receive)
    late = [pltpu.make_async_copy(attended, attended_out, local.at[2]), pltpu.make_async_copy(lse, lse_out, local.at[3])]
    for copy in late:
        copy.start()
    finish()
    total = first[pl.ds(0, rows), :] + sums[1].astype(f32) + sums[5].astype(f32)
    branch[...] = total
    middle[...] = stream[...] + norm_rows(total, gains[1:2, :], shifts[1:2, :])
    sent()
    for copy in stores + late:
        copy.wait()


def attention_forward(stream, gains, shifts, w_qkv, w_out):
    rows, model = stream.shape
    width = w_out.shape[0]
    shape = jax.ShapeDtypeStruct
    return pl.pallas_call(
        functools.partial(attention_forward_kernel, 0),
        out_shape=(
            shape((rows, model), f32),
            shape((rows, model), f32),
            shape((4 * rows, model), bf16),
            shape((4 * rows, 3 * width), bf16),
            shape((4 * rows, width), bf16),
            shape((4 * rows, 128), f32),
        ),
        in_specs=vmem(3) + anywhere(2),
        out_specs=vmem(2) + anywhere(4),
        scratch_shapes=[
            pltpu.VMEM((4 * rows, model), bf16),
            pltpu.VMEM((4 * rows, 3 * width), bf16),
            pltpu.VMEM((4 * rows, width), bf16),
            pltpu.VMEM((4 * rows, 128), f32),
            pltpu.VMEM((model, 3 * width), bf16),
            pltpu.VMEM(w_out.shape, bf16),
            *sums_scratch(rows, model),
            pltpu.SemaphoreType.DMA((4,)),
        ],
        compiler_params=pltpu.CompilerParams(collective_id=2, has_side_effects=True, vmem_limit_bytes=56 << 20),
        cost_estimate=pl.CostEstimate(flops=24 * rows * model * width, bytes_accessed=16 << 20, transcendentals=16 * rows * rows * 4),
    )(stream, gains, shifts, w_qkv, w_out)


def attend_block_back(rows, start, high, qkv, attended_grad, lse, inner, grad_query, grad_key, grad_value):
    width = attended_grad.shape[1]
    here = pl.ds(start, rows)
    scale = HEAD_DIM ** (-0.5)
    for pair in range(width // 128):
        columns = slice(pair * 128, pair * 128 + 128)
        query = qkv[here, columns] * bf16(scale)
        above = attended_grad[here, columns]
        result = 0.0
        for half in range(2):
            head = 2 * pair + half
            only = jnp.where(head_lanes(query.shape, half), query, 0)
            grad = jnp.where(head_lanes(query.shape, half), above, 0)
            for begin, size, mask in spans(rows, high):
                keys = pl.ds(begin, size)
                key = qkv[keys, width + pair * 128 : width + pair * 128 + 128]
                value = qkv[keys, 2 * width + pair * 128 : 2 * width + pair * 128 + 128]
                scores = dot_nt(only, key)
                if mask:
                    scores = masked(scores, start, begin)
                probs = jnp.exp(scores - lse[here, head : head + 1])
                grad_probs = dot_nt(grad, value)
                grad_scores = (probs * (grad_probs - inner[here, head : head + 1])).astype(bf16)
                key_only = jnp.where(head_lanes(key.shape, half), key, 0)
                result = result + dot_nn(grad_scores, key_only)
                grad_key[keys, columns] += dot_tn(grad_scores, only)
                grad_value[keys, columns] += dot_tn(probs.astype(bf16), grad)
        grad_query[here, columns] = (result * scale).astype(bf16)


def attention_backward_kernel(
    layer, grad, branch, stream, gains, shifts, held_in, qkv_in, attended_in, lse_in, w_qkv, w_out,
    grad_stream, sums_out, grad_qkv, grad_out,
    held, past, qkv, attended, lse, inner, above, pushed, grad_key, grad_value, weight, project, outcome, outcome_out,
    first, sums, send, receive, local,
):
    rows = stream.shape[0]
    width = attended.shape[1]
    model = stream.shape[1]
    loads = [
        pltpu.make_async_copy(w_out, project, local.at[3]),
        pltpu.make_async_copy(attended_in, attended, local.at[4]),
        pltpu.make_async_copy(qkv_in, qkv, local.at[5]),
        pltpu.make_async_copy(lse_in, lse, local.at[6]),
        *[pltpu.make_async_copy(w_qkv.at[index], weight.at[:, pl.ds(index * width, width)], local.at[index]) for index in range(3)],
        pltpu.make_async_copy(held_in, past, local.at[7]),
    ]
    for copy in loads:
        copy.start()
    mate, near = greet()
    own, others, along, across = places(rows)
    pulled, gain_one, shift_one = norm_pull(branch[...], gains[1:2, :], grad[...])
    held[pl.ds(own, rows), :] = pulled.astype(bf16)
    grad_key[...] = jnp.zeros_like(grad_key)
    grad_value[...] = jnp.zeros_like(grad_value)
    for copy in loads:
        copy.wait()
    zl = lax.axis_index("zl")

    def at(quarter):
        return pl.multiple_of(quarter * rows, 16)

    blocks = []

    def arrived(start, size):
        here = pl.ds(start, size)
        value = dot_nt(held[here, :], project[...]).astype(bf16)
        above[here, :] = value
        product = value.astype(f32) * attended[here, :].astype(f32)
        lane = lax.broadcasted_iota(jnp.int32, (size, 128), 1)
        tile = jnp.zeros((size, 128), f32)
        for pair in range(width // 128):
            part = product[:, pair * 128 : pair * 128 + 128]
            for half in range(2):
                one = jnp.sum(jnp.where(head_lanes(part.shape, half), part, 0.0), axis=-1, keepdims=True)
                tile = jnp.where(lane == 2 * pair + half, one, tile)
        inner[here, :] = tile
        blocks.append(size)
        if len(blocks) == 2:
            back(2 + zl, True)
            back(zl, False)

    def back(quarter, high):
        attend_block_back(rows, at(quarter), high, qkv, above, lse, inner, pushed, grad_key, grad_value)

    sent = gather(rows, mate, near, held, arrived, send, receive)
    back(3 - zl, True)
    back(1 - zl, False)
    pushed[:, pl.ds(width, width)] = grad_key[...].astype(bf16)
    pushed[:, pl.ds(2 * width, width)] = grad_value[...].astype(bf16)

    def term(start, size, sink):
        here = pl.ds(start, size)

        def step(columns):
            sink(columns, dot_nt(pushed[here, :], weight[columns, :]))

        tiles(model, step)

    finish = scatter(rows, mate, near, term, first, sums, send, receive)

    def step_out(columns):
        outcome_out[:, columns] = dot_tn(attended[...], held[:, columns]).astype(bf16)

    tiles(model, step_out)
    out = pltpu.make_async_copy(outcome_out, grad_out, local.at[0])
    out.start()

    def step_qkv(columns):
        outcome[columns, :] = dot_tn(past[:, columns], pushed[...]).astype(bf16)

    tiles(model, step_qkv)
    outs = [out]
    for index in range(3):
        copy = pltpu.make_async_copy(outcome.at[:, pl.ds(index * width, width)], grad_qkv.at[index], local.at[1 + index])
        copy.start()
        outs.append(copy)
    finish()
    total = first[pl.ds(0, rows), :] + sums[1].astype(f32) + sums[5].astype(f32)
    pulled, gain_zero, shift_zero = norm_pull(stream[...], gains[0:1, :], total)
    grad_stream[...] = grad[...] + pulled
    sums_out[0:1, :] = gain_zero
    sums_out[1:2, :] = shift_zero
    sums_out[2:3, :] = gain_one
    sums_out[3:4, :] = shift_one
    sent()
    for copy in outs:
        copy.wait()


def attention_backward(grad, branch, stream, gains, shifts, held, qkv, attended, lse, w_qkv, w_out):
    rows, model = stream.shape
    width = w_out.shape[0]
    shape = jax.ShapeDtypeStruct
    return pl.pallas_call(
        functools.partial(attention_backward_kernel, 0),
        out_shape=(
            shape((rows, model), f32),
            shape((4, model), f32),
            shape(w_qkv.shape, bf16),
            shape(w_out.shape, bf16),
        ),
        in_specs=vmem(5) + anywhere(6),
        out_specs=vmem(2) + anywhere(2),
        scratch_shapes=[
            pltpu.VMEM((4 * rows, model), bf16),
            pltpu.VMEM((4 * rows, model), bf16),
            pltpu.VMEM((4 * rows, 3 * width), bf16),
            pltpu.VMEM((4 * rows, width), bf16),
            pltpu.VMEM((4 * rows, 128), f32),
            pltpu.VMEM((4 * rows, 128), f32),
            pltpu.VMEM((4 * rows, width), bf16),
            pltpu.VMEM((4 * rows, 3 * width), bf16),
            pltpu.VMEM((4 * rows, width), f32),
            pltpu.VMEM((4 * rows, width), f32),
            pltpu.VMEM((model, 3 * width), bf16),
            pltpu.VMEM(w_out.shape, bf16),
            pltpu.VMEM((model, 3 * width), bf16),
            pltpu.VMEM(w_out.shape, bf16),
            *sums_scratch(rows, model),
            pltpu.SemaphoreType.DMA((8,)),
        ],
        compiler_params=pltpu.CompilerParams(collective_id=3, has_side_effects=True, vmem_limit_bytes=56 << 20),
        cost_estimate=pl.CostEstimate(flops=60 * rows * model * width, bytes_accessed=24 << 20, transcendentals=16 * rows * rows * 4),
    )(grad, branch, stream, gains, shifts, held, qkv, attended, lse, w_qkv, w_out)


TP = ("c", "zl")
SHARE = ("gl", "p")
BATCH = ("gh", "gl", "p")


def swap_rows(values):
    return lax.ppermute(values, ("c", "zh"), ((0, 0), (1, 2), (2, 1), (3, 3)))


def keeps():
    return lax.axis_index("c") == lax.axis_index("zh")


def fetch_weight(weight):
    shape = weight.shape
    flat = weight.reshape(4, -1, 1024)
    part = lax.dynamic_index_in_dim(flat, lax.axis_index(SHARE), 0, keepdims=False)
    part = lax.ppermute(part, ("c", "zh"), ((0, 1), (3, 2)))
    rest = lax.all_gather(part, SHARE, axis=0, tiled=True).reshape(shape)
    return jnp.where(keeps(), weight, rest)


def sum_weight(grad):
    shape = grad.shape
    flat = grad.astype(jnp.bfloat16).reshape(-1, 1024)
    part = lax.psum_scatter(flat, BATCH, scatter_dimension=0, tiled=True)
    other = lax.ppermute(part, ("c", "zh"), ((1, 0), (2, 3)))
    part = (part.astype(jnp.float32) + other.astype(jnp.float32)).astype(jnp.bfloat16)
    mate = lax.ppermute(part, "c", ((0, 1), (1, 0)))
    part = jnp.where(keeps(), part, mate)
    return lax.all_gather(part, BATCH, axis=0, tiled=True).reshape(shape).astype(jnp.float32)


def per_device(hidden_in, cotangent, group_ids, group_sizes, w_qkv, w_out, w_up, w_down, gains, shifts):
    layers = w_qkv.shape[0]
    hidden_in = swap_rows(hidden_in)
    cotangent = swap_rows(cotangent)
    weights = [[fetch_weight(value[layer]) for value in (w_qkv, w_out, w_up, w_down)] for layer in range(layers)]
    stream = hidden_in.astype(f32)
    saved = []
    for layer in range(layers):
        qkv, out, up, down = weights[layer]
        branch, middle, *kept = attention_forward(stream, gains[layer], shifts[layer], qkv, out)
        second, later, *kept_ffn = ffn_forward(middle, gains[layer], shifts[layer], up, down)
        saved.append((stream, branch, kept, middle, second, kept_ffn))
        stream = later
    ids = lax.all_gather(group_ids, "c", axis=0, tiled=True)
    mine = lax.dynamic_index_in_dim(ids, lax.axis_index("zh"), 0, keepdims=False)
    count = jnp.sum(jnp.where(jnp.arange(group_sizes.shape[0]) == mine, group_sizes, 0)).astype(f32)
    grad = cotangent.astype(f32) * (1.0 / count)
    weight_grads, norm_grads = [None] * layers, [None] * layers
    for layer in reversed(range(layers)):
        qkv, out, up, down = weights[layer]
        before, branch, kept, middle, second, kept_ffn = saved[layer]
        grad, sums_ffn, grad_up, grad_down = ffn_backward(
            grad, second, middle, gains[layer], shifts[layer], *kept_ffn, up, down
        )
        grad, sums_att, grad_qkv, grad_out = attention_backward(
            grad, branch, before, gains[layer], shifts[layer], *kept, qkv, out
        )
        weight_grads[layer] = [sum_weight(value) for value in (grad_qkv, grad_out, grad_up, grad_down)]
        norm_grads[layer] = jnp.concatenate([sums_att, sums_ffn])
    norm_sums = lax.psum(jnp.stack(norm_grads), AXES).reshape(layers, 4, 2, -1)
    return (
        swap_rows(stream.astype(bf16)).astype(f32),
        swap_rows(grad.astype(bf16)).astype(f32),
        *[jnp.stack([weight_grads[layer][member] for layer in range(layers)]) for member in range(4)],
        norm_sums[:, :, 0],
        norm_sums[:, :, 1],
    )


def solution(mesh):
    fine = jax.sharding.Mesh(mesh.devices.reshape(-1, 2, 2, 2, 2, 2), AXES)
    dp = ("gh", "gl", "p", "c")
    tensor = ("zh", "zl")
    rows = P((*dp, *tensor), None)
    weights = (
        P(None, None, None, tensor),
        P(None, tensor, None),
        P(None, None, tensor),
        P(None, tensor, None),
    )
    return jax.shard_map(
        per_device,
        mesh=fine,
        in_specs=(rows, rows, P(dp), P(), *weights, P(), P()),
        out_specs=(rows, rows, *weights, P(), P()),
        check_vma=False,
    )
```

time: 1890 us -> 1170 us (0.62)
  waiting for transfers between devices: 1220 us -> 620 us
  Pallas kernels: 0 us -> 322 us
  matrix products: 316 us -> 0 us
  other arithmetic: 107 us -> 48.4 us
  local copies, waits for them, and re-layouts: 86.5 us -> 40.1 us
    all_gather x8 -> x0, waiting for transfers between devices: 325 us -> none  [the longest x2 96.1 us: per_device(): ffn_all = lax.all_gather(normed2, TP, axis=0, tiled=True)]
    pallas_call x0 -> x8, Pallas kernels: none -> 322 us  [the longest x2 95.1 us: attention_backward(): pl.pallas_call(functools.partial(attention_backward_kernel, 0), out_shape...]
    dot_general x36 -> x0, matrix products: 316 us -> none  [the longest x2 56.8 us: attend_backward(): jnp.einsum('hqk,qhd->khd', grad_scores, query, preferred_element_type=jnp...]
    reduce_scatter x8 -> x0, waiting for transfers between devices: 280 us -> none  [the longest x2 90.6 us: per_device(): lax.psum_scatter(back_up(jnp.int32(0), lax.axis_size(TP) * rows).astype(j...]
    reduce_scatter x8, waiting for transfers between devices: 53.4 us -> 137 us  [sum_weight(): part = lax.psum_scatter(flat, BATCH, scatter_dimension=0, tiled=True)]
    all_gather x6, waiting for transfers between devices: 104 us -> 43.3 us  [fetch_weight(): rest = lax.all_gather(part, SHARE, axis=0, tiled=True).reshape(shape)]
    reduce_sum x33 -> x0, other arithmetic: 57.7 us -> none  [the longest x13 21.7 us: norm_rows(): return centred * lax.rsqrt(spread + eps_norm) * gain + shift]
    ppermute x8, waiting for transfers between devices: 72.3 us -> 36.4 us  [fetch_weight(): part = lax.ppermute(part, ('c', 'zh'), ((0, 1), (3, 2)))]
  transfers between devices with their start and end apart: 65 -> 49, of which waited for: 50 -> 36; matrix products, arithmetic and copies ran while one was open for 14% -> 6% of each run, Pallas kernels for 0% -> 4%
where the time goes in v2:
time: 1170 us
  waiting for transfers between devices  620 us (53%)
  Pallas kernels  322 us (28%)
  starting transfers between devices  65.1 us (6%)
  blocking collectives  52.1 us (4%)
  other arithmetic  48.4 us (4%)
  local copies, waits for them, and re-layouts  40.1 us (3%)
  between operations  16.7 us (1%)
    all_gather x6, waiting for transfers between devices, sum_weight(): lax.all_gather(part, BATCH, axis=0, tiled=True).reshape(shape)  168 us
    reduce_scatter x8, waiting for transfers between devices, sum_weight(): part = lax.psum_scatter(flat, BATCH, scatter_dimension=0, tiled=True)  137 us
    psum x1, waiting for transfers between devices, per_device(): norm_sums = lax.psum(jnp.stack(norm_grads), AXES).reshape(layers, 4, 2, -1)  123 us
    ppermute x8, waiting for transfers between devices, sum_weight(): other = lax.ppermute(part, ('c', 'zh'), ((1, 0), (2, 3)))  97.2 us
    pallas_call x2, Pallas kernels, attention_backward(): pl.pallas_call(functools.partial(attention_backward_kernel, 0), out_shape...  95.1 us
    pallas_call x2, Pallas kernels, attention_forward(): pl.pallas_call(functools.partial(attention_forward_kernel, 0), out_shape=...  87.9 us
    pallas_call x2, Pallas kernels, ffn_backward(): pl.pallas_call(functools.partial(ffn_backward_kernel, 0), out_shape=(shap...  71.9 us
    pallas_call x2, Pallas kernels, ffn_forward(): pl.pallas_call(functools.partial(ffn_forward_kernel, 0), out_shape=(shape...  67.5 us
  transfers between devices with their start and end apart: 49, of which 36 were waited for; matrix products, arithmetic and copies ran while one was open for 6% of the time, Pallas kernels for 4%

profile of v2, /device:TPU:0, one launch (start us, length us, event | category | flops | bytes accessed | tf_op | source)
XLA Modules:
  0.0 1165.2 jit_solution(13677555183226754082)
XLA Ops:
  153.7 47.3 %shard_map.161 = (f32[272,1024]{1,0:T(8,128)}, f32[272,1024]{1,0:T(8,128)}, bf16[1088,1024]{1,0:T(8,128)(2,1)}, bf16[1088,768]{1,0:T(8,128)(2,1)}, bf16[1088,256]{1,0:T(8,128)(2,1)}, /*index=5*/f32[1088,128]{1,0:T(8,128)}) custom-call(f32[272,1024]{1,0:T(8,128)} %convert_element_type.121.stream, f32[4,1024]{1,0:T(4,128)} %get-tuple-element.106.gains, ...), custom_call_target="tpu_custom_call" | custom-call | flops 1711276032 | bytes 16777216 | tf_op jit(solution)/shard_map/pallas_call | solution.py:547
  212.0 37.0 %all-gather.23.cloned.1.call-done = bf16[1024,1024]{1,0:T(8,128)(2,1)} async-done(((bf16[256,1024]{1,0:T(8,128)(2,1)}), bf16[1024,1024]{1,0:T(8,128)(2,1)}) %all-gather.23.cloned.1.call-update) | async-done | bytes 2097168 | tf_op jit(solution)/shard_map/all_gather | solution.py:759
  253.6 34.5 %shard_map.162 = (f32[272,1024]{1,0:T(8,128)}, f32[272,1024]{1,0:T(8,128)}, bf16[1088,1024]{1,0:T(8,128)(2,1)}, bf16[1088,1024]{1,0:T(8,128)(2,1)}, bf16[1088,1024]{1,0:T(8,128)(2,1)}) custom-call(f32[272,1024]{1,0:T(8,128)} %get-tuple-element.46.middle, f32[4,1024]{1,0:T(4,128)} %get-tuple-element.106.gains, f32[4,1024]{1,0:T(4,128)} %get-tuple-element.103.shifts, ...), custom_call_target="tpu_custom_call" | custom-call | flops 4563402752 | bytes 25165824 | tf_op jit(solution)/shard_map/pallas_call | solution.py:225
  288.1 40.6 %shard_map.163 = (f32[272,1024]{1,0:T(8,128)}, f32[272,1024]{1,0:T(8,128)}, bf16[1088,1024]{1,0:T(8,128)(2,1)}, bf16[1088,768]{1,0:T(8,128)(2,1)}, bf16[1088,256]{1,0:T(8,128)(2,1)}, /*index=5*/f32[1088,128]{1,0:T(8,128)}) custom-call(f32[272,1024]{1,0:T(8,128)} %get-tuple-element.47.stream, f32[4,1024]{1,0:T(4,128)} %get-tuple-element.107.gains, ...), custom_call_target="tpu_custom_call" | custom-call | flops 1711276032 | bytes 16777216 | tf_op jit(solution)/shard_map/pallas_call | solution.py:547
  328.7 33.0 %shard_map.164 = (f32[272,1024]{1,0:T(8,128)}, f32[272,1024]{1,0:T(8,128)}, bf16[1088,1024]{1,0:T(8,128)(2,1)}, bf16[1088,1024]{1,0:T(8,128)(2,1)}, bf16[1088,1024]{1,0:T(8,128)(2,1)}) custom-call(f32[272,1024]{1,0:T(8,128)} %get-tuple-element.48.middle, f32[4,1024]{1,0:T(4,128)} %get-tuple-element.107.gains, f32[4,1024]{1,0:T(4,128)} %get-tuple-element.102.shifts, ...), custom_call_target="tpu_custom_call" | custom-call | flops 4563402752 | bytes 25165824 | tf_op jit(solution)/shard_map/pallas_call | solution.py:225
  361.8 36.3 %shard_map.165 = (f32[272,1024]{1,0:T(8,128)}, f32[4,1024]{1,0:T(4,128)}, bf16[1024,1024]{1,0:T(8,128)(2,1)}, bf16[1024,1024]{1,0:T(8,128)(2,1)}) custom-call(f32[272,1024]{1,0:T(8,128)} %convert_multiply_fusion.grad, f32[272,1024]{1,0:T(8,128)} %get-tuple-element.50.second, f32[272,1024]{1,0:T(8,128)} %get-tuple-element.48.middle, ...), custom_call_target="tpu_custom_call" | custom-call | flops 9126805504 | bytes 33554432 | tf_op jit(solution)/shard_map/pallas_call | solution.py:316
  398.1 47.6 %shard_map.166 = (f32[272,1024]{1,0:T(8,128)}, f32[4,1024]{1,0:T(4,128)}, bf16[3,1024,256]{2,1,0:T(8,128)(2,1)}, bf16[256,1024]{1,0:T(8,128)(2,1)}) custom-call(f32[272,1024]{1,0:T(8,128)} %get-tuple-element.54.grad, f32[272,1024]{1,0:T(8,128)} %get-tuple-element.55.branch, f32[272,1024]{1,0:T(8,128)} %get-tuple-element.47.stream, ...), custom_call_target="tpu_custom_call" | custom-call | flops 4278190080 | bytes 25165824 | tf_op jit(solution)/shard_map/pallas_call | solution.py:708
  445.7 35.6 %shard_map.167 = (f32[272,1024]{1,0:T(8,128)}, f32[4,1024]{1,0:T(4,128)}, bf16[1024,1024]{1,0:T(8,128)(2,1)}, bf16[1024,1024]{1,0:T(8,128)(2,1)}) custom-call(f32[272,1024]{1,0:T(8,128)} %get-tuple-element.60.grad, f32[272,1024]{1,0:T(8,128)} %get-tuple-element.61.second, f32[272,1024]{1,0:T(8,128)} %get-tuple-element.46.middle, ...), custom_call_target="tpu_custom_call" | custom-call | flops 9126805504 | bytes 33554432 | tf_op jit(solution)/shard_map/pallas_call | solution.py:316
  481.3 47.5 %shard_map.168 = (f32[272,1024]{1,0:T(8,128)}, f32[4,1024]{1,0:T(4,128)}, bf16[3,1024,256]{2,1,0:T(8,128)(2,1)}, bf16[256,1024]{1,0:T(8,128)(2,1)}) custom-call(f32[272,1024]{1,0:T(8,128)} %get-tuple-element.65.grad, f32[272,1024]{1,0:T(8,128)} %get-tuple-element.66.branch, f32[272,1024]{1,0:T(8,128)} %convert_element_type.121.stream, ...), custom_call_target="tpu_custom_call" | custom-call | flops 4278190080 | bytes 25165824 | tf_op jit(solution)/shard_map/pallas_call | solution.py:708
  538.5 24.2 %reduce-scatter.9.cloned.1.call-done = bf16[192,1024]{1,0:T(8,128)(2,1)} async-done(((bf16[768,1024]{1,0:T(8,128)(2,1)}), bf16[192,1024]{1,0:T(8,128)(2,1)}) %reduce-scatter.9.cloned.1.call-update) | async-done | bytes 393232 | tf_op jit(solution)/shard_map/reduce_scatter | solution.py:766
  615.9 19.4 %reduce-scatter.19.cloned.1.call-done = bf16[256,1024]{1,0:T(8,128)(2,1)} async-done(((bf16[1024,1024]{1,0:T(8,128)(2,1)}), bf16[256,1024]{1,0:T(8,128)(2,1)}) %reduce-scatter.19.cloned.1.call-update) | async-done | bytes 524304 | tf_op jit(solution)/shard_map/reduce_scatter | solution.py:766
  636.6 16.5 %collective-permute-done.22 = bf16[256,1024]{1,0:T(8,128)(2,1)S(1)} collective-permute-done((bf16[256,1024]{1,0:T(8,128)(2,1)}, bf16[256,1024]{1,0:T(8,128)(2,1)S(1)}, u32[]{:S(2)}, u32[]{:S(2)}) %collective-permute-start.22) | collective-permute-done | bytes 524320 | tf_op jit(solution)/shard_map/ppermute | solution.py:767
  657.3 16.4 %reduce-scatter.17.cloned.1.call-done = bf16[256,1024]{1,0:T(8,128)(2,1)} async-done(((bf16[1024,1024]{1,0:T(8,128)(2,1)}), bf16[256,1024]{1,0:T(8,128)(2,1)}) %reduce-scatter.17.cloned.1.call-update) | async-done | bytes 524304 | tf_op jit(solution)/shard_map/reduce_scatter | solution.py:766
  675.0 16.5 %collective-permute-done.20 = bf16[256,1024]{1,0:T(8,128)(2,1)S(1)} collective-permute-done((bf16[256,1024]{1,0:T(8,128)(2,1)}, bf16[256,1024]{1,0:T(8,128)(2,1)S(1)}, u32[]{:S(2)}, u32[]{:S(2)}) %collective-permute-start.20) | collective-permute-done | bytes 524320 | tf_op jit(solution)/shard_map/ppermute | solution.py:767
  713.2 16.5 %collective-permute-done.26 = bf16[256,1024]{1,0:T(8,128)(2,1)S(1)} collective-permute-done((bf16[256,1024]{1,0:T(8,128)(2,1)}, bf16[256,1024]{1,0:T(8,128)(2,1)S(1)}, u32[]{:S(2)}, u32[]{:S(2)}) %collective-permute-start.26) | collective-permute-done | bytes 524320 | tf_op jit(solution)/shard_map/ppermute | solution.py:767
  733.8 16.4 %reduce-scatter.21.cloned.1.call-done = bf16[256,1024]{1,0:T(8,128)(2,1)} async-done(((bf16[1024,1024]{1,0:T(8,128)(2,1)}), bf16[256,1024]{1,0:T(8,128)(2,1)}) %reduce-scatter.21.cloned.1.call-update) | async-done | bytes 524304 | tf_op jit(solution)/shard_map/reduce_scatter | solution.py:766
  751.5 16.5 %collective-permute-done.24 = bf16[256,1024]{1,0:T(8,128)(2,1)S(1)} collective-permute-done((bf16[256,1024]{1,0:T(8,128)(2,1)}, bf16[256,1024]{1,0:T(8,128)(2,1)S(1)}, u32[]{:S(2)}, u32[]{:S(2)}) %collective-permute-start.24) | collective-permute-done | bytes 524320 | tf_op jit(solution)/shard_map/ppermute | solution.py:767
  779.2 123.4 %all-reduce.3.cloned.1.call-done = f32[2,4,2,1024]{3,1,0,2:T(4,128)} async-done(((f32[2,4,2,1024]{3,1,0,2:T(4,128)}), f32[2,4,2,1024]{3,1,0,2:T(4,128)}) %all-reduce.3.cloned.1.call-update) | async-done | bytes 65552 | tf_op jit(solution)/shard_map/psum | solution.py:803
  906.3 24.9 %reduce-scatter.15.cloned.1.call-done = bf16[64,1024]{1,0:T(8,128)(2,1)} async-done(((bf16[256,1024]{1,0:T(8,128)(2,1)}), bf16[64,1024]{1,0:T(8,128)(2,1)}) %reduce-scatter.15.cloned.1.call-update) | async-done | bytes 131088 | tf_op jit(solution)/shard_map/reduce_scatter | solution.py:766
  972.9 29.4 %all-gather.27.cloned.1.call-done = bf16[768,1024]{1,0:T(8,128)(2,1)} async-done(((bf16[192,1024]{1,0:T(8,128)(2,1)}), bf16[768,1024]{1,0:T(8,128)(2,1)}) %all-gather.27.cloned.1.call-update) | async-done | bytes 1572880 | tf_op jit(solution)/shard_map/all_gather | solution.py:771
  1008.2 31.8 %all-gather.31.cloned.1.call-done = bf16[1024,1024]{1,0:T(8,128)(2,1)} async-done(((bf16[256,1024]{1,0:T(8,128)(2,1)}), bf16[1024,1024]{1,0:T(8,128)(2,1)}) %all-gather.31.cloned.1.call-update) | async-done | bytes 2097168 | tf_op jit(solution)/shard_map/all_gather | solution.py:771
  1039.9 37.8 %all-gather.29.cloned.1.call-done = bf16[1024,1024]{1,0:T(8,128)(2,1)} async-done(((bf16[256,1024]{1,0:T(8,128)(2,1)}), bf16[1024,1024]{1,0:T(8,128)(2,1)}) %all-gather.29.cloned.1.call-update) | async-done | bytes 2097168 | tf_op jit(solution)/shard_map/all_gather | solution.py:771
  1083.8 30.9 %all-gather.35.cloned.1.call-done = bf16[1024,1024]{1,0:T(8,128)(2,1)} async-done(((bf16[256,1024]{1,0:T(8,128)(2,1)}), bf16[1024,1024]{1,0:T(8,128)(2,1)}) %all-gather.35.cloned.1.call-update) | async-done | bytes 2097168 | tf_op jit(solution)/shard_map/all_gather | solution.py:771
  1114.7 37.2 %all-gather.33.cloned.1.call-done = bf16[1024,1024]{1,0:T(8,128)(2,1)} async-done(((bf16[256,1024]{1,0:T(8,128)(2,1)}), bf16[1024,1024]{1,0:T(8,128)(2,1)}) %all-gather.33.cloned.1.call-update) | async-done | bytes 2097168 | tf_op jit(solution)/shard_map/all_gather | solution.py:771
  (208 shorter events, 331.5 us)
Async XLA Ops:
  7.2 136.8 %all-gather.19.cloned.1.call-start = ((), (), s32[]{:S(2)}) async-start(), calls=%async_computation.11 | async-start | bytes 1966080 | tf_op jit(solution)/shard_map/all_gather | solution.py:759
  24.6 123.3 %all-gather.13.cloned.1.call-start = ((), (), s32[]{:S(2)}) async-start(), calls=%async_computation.8 | async-start | bytes 1966080 | tf_op jit(solution)/shard_map/all_gather | solution.py:759
  37.1 164.0 %all-gather.15.cloned.1.call-start = ((), (), s32[]{:S(2)}) async-start(), calls=%async_computation.9 | async-start | bytes 2621440 | tf_op jit(solution)/shard_map/all_gather | solution.py:759
  52.8 148.2 %all-gather.21.cloned.1.call-start = ((), (), s32[]{:S(2)}) async-start(), calls=%async_computation.12 | async-start | bytes 2621440 | tf_op jit(solution)/shard_map/all_gather | solution.py:759
  65.8 146.1 %all-gather.17.cloned.1.call-start = ((), (), s32[]{:S(2)}) async-start(), calls=%async_computation.10 | async-start | bytes 2621440 | tf_op jit(solution)/shard_map/all_gather | solution.py:759
  80.8 168.3 %all-gather.23.cloned.1.call-start = ((), (), s32[]{:S(2)}) async-start(), calls=%async_computation.13 | async-start | bytes 2621440 | tf_op jit(solution)/shard_map/all_gather | solution.py:759
  93.8 468.8 %reduce-scatter.9.cloned.1.call-start = ((), (), s32[]{:S(2)}) async-start(), calls=%async_computation.14 | async-start | bytes 1966080 | tf_op jit(solution)/shard_map/reduce_scatter | solution.py:766
  532.7 64.5 %reduce-scatter.11.cloned.1.call-start = ((), (), s32[]{:S(2)}) async-start(), calls=%async_computation.16 | async-start | bytes 1966080 | tf_op jit(solution)/shard_map/reduce_scatter | solution.py:766
  535.0 100.4 %reduce-scatter.19.cloned.1.call-start = ((), (), s32[]{:S(2)}) async-start(), calls=%async_computation.22 | async-start | bytes 2621440 | tf_op jit(solution)/shard_map/reduce_scatter | solution.py:766
  535.7 137.9 %reduce-scatter.17.cloned.1.call-start = ((), (), s32[]{:S(2)}) async-start(), calls=%async_computation.20 | async-start | bytes 2621440 | tf_op jit(solution)/shard_map/reduce_scatter | solution.py:766
  536.3 175.6 %reduce-scatter.23.cloned.1.call-start = ((), (), s32[]{:S(2)}) async-start(), calls=%async_computation.26 | async-start | bytes 2621440 | tf_op jit(solution)/shard_map/reduce_scatter | solution.py:766
  537.1 213.1 %reduce-scatter.21.cloned.1.call-start = ((), (), s32[]{:S(2)}) async-start(), calls=%async_computation.24 | async-start | bytes 2621440 | tf_op jit(solution)/shard_map/reduce_scatter | solution.py:766
  537.6 240.2 %reduce-scatter.13.cloned.1.call-start = ((), (), s32[]{:S(2)}) async-start(), calls=%async_computation.18 | async-start | bytes 655360 | tf_op jit(solution)/shard_map/reduce_scatter | solution.py:766
  538.4 364.3 %all-reduce.3.cloned.1.call-start = ((), (), s32[]{:S(2)}) async-start(), calls=%async_computation.28 | async-start | bytes 131072 | tf_op jit(solution)/shard_map/psum | solution.py:803
  564.7 366.5 %reduce-scatter.15.cloned.1.call-start = ((), (), s32[]{:S(2)}) async-start(), calls=%async_computation.19 | async-start | bytes 655360 | tf_op jit(solution)/shard_map/reduce_scatter | solution.py:766
  565.3 404.9 %all-gather.25.cloned.1.call-start = ((), (), s32[]{:S(2)}) async-start(), calls=%async_computation.15 | async-start | bytes 1966080 | tf_op jit(solution)/shard_map/all_gather | solution.py:771
  581.4 421.0 %all-gather.27.cloned.1.call-start = ((), (), s32[]{:S(2)}) async-start(), calls=%async_computation.17 | async-start | bytes 1966080 | tf_op jit(solution)/shard_map/all_gather | solution.py:771
  615.9 424.0 %all-gather.31.cloned.1.call-start = ((), (), s32[]{:S(2)}) async-start(), calls=%async_computation.23 | async-start | bytes 2621440 | tf_op jit(solution)/shard_map/all_gather | solution.py:771
  657.2 420.4 %all-gather.29.cloned.1.call-start = ((), (), s32[]{:S(2)}) async-start(), calls=%async_computation.21 | async-start | bytes 2621440 | tf_op jit(solution)/shard_map/all_gather | solution.py:771
  695.6 419.1 %all-gather.35.cloned.1.call-start = ((), (), s32[]{:S(2)}) async-start(), calls=%async_computation.27 | async-start | bytes 2621440 | tf_op jit(solution)/shard_map/all_gather | solution.py:771
  733.8 418.1 %all-gather.33.cloned.1.call-start = ((), (), s32[]{:S(2)}) async-start(), calls=%async_computation.25 | async-start | bytes 2621440 | tf_op jit(solution)/shard_map/all_gather | solution.py:771
  772.2 131.9 %collective-permute-start.11 = (bf16[272,1024]{1,0:T(8,128)(2,1)S(1)}, bf16[272,1024]{1,0:T(8,128)(2,1)S(1)}, u32[]{:S(2)}, u32[]{:S(2)}) collective-permute-start(bf16[272,1024]{1,0:T(8,128)(2,1)S(1)} %convert_element_type.126), channel_id=1, source_target_pairs={{0,0},{2,4},{4,2},{6,6},{1,1},{3,5},{5,3},{7,7},{8,8},{10,12},{12,... | collective-permute-start | bytes 1671176 | tf_op jit(solution)/shard_map/ppermute | solution.py:747
  773.0 132.2 %collective-permute-start.9 = (bf16[272,1024]{1,0:T(8,128)(2,1)S(1)}, bf16[272,1024]{1,0:T(8,128)(2,1)S(1)}, u32[]{:S(2)}, u32[]{:S(2)}) collective-permute-start(bf16[272,1024]{1,0:T(8,128)(2,1)S(1)} %convert_element_type.122), channel_id=1, source_target_pairs={{0,0},{2,4},{4,2},{6,6},{1,1},{3,5},{5,3},{7,7},{8,8},{10,12},{12,... | collective-permute-start | bytes 1671176 | tf_op jit(solution)/shard_map/ppermute | solution.py:747
  777.8 154.7 %collective-permute-start.16 = (bf16[64,1024]{1,0:T(8,128)(2,1)}, bf16[64,1024]{1,0:T(8,128)(2,1)S(1)}, u32[]{:S(2)}, u32[]{:S(2)}) collective-permute-start(bf16[64,1024]{1,0:T(8,128)(2,1)} %reduce-scatter.13.cloned.1.call-done), channel_id=1, source_target_pairs={{2,0},{4,6},{3,1},{5,7},{10,8},{12,14},{11,9},{13,15},{18,16},{20,... | collective-permute-start | bytes 393224 | tf_op jit(solution)/shard_map/ppermute | solution.py:767
  (44 other events, 771.3 us)
Sparse Core Ops, SparseCore 0:
  24.7 37.0 all-gather.18
  64.2 30.9 all-gather.12
  97.7 38.1 all-gather.14
  138.1 36.7 all-gather.20
  176.6 35.2 all-gather.16
  213.7 35.2 all-gather.22
  532.8 29.7 reduce-scatter.8
  566.2 30.9 reduce-scatter.10
  600.1 35.1 reduce-scatter.18
  638.4 35.1 reduce-scatter.16
  676.6 35.1 reduce-scatter.22
  715.0 35.1 reduce-scatter.20
  753.0 24.7 reduce-scatter.12
  784.8 117.8 all-reduce.2
  905.6 25.5 reduce-scatter.14
  932.9 37.2 all-gather.24
  972.4 29.8 all-gather.26
  1004.6 35.2 all-gather.30
  1042.3 35.2 all-gather.28
  1079.4 35.2 all-gather.34
  1116.6 35.2 all-gather.32

commit v3 on v2

v3 whole, which is shorter than its diff:
```python
import functools
import types

import jax
import jax.numpy as jnp
from jax import lax
from jax.experimental import pallas as pl
from jax.experimental.pallas import tpu as pltpu
from jax.sharding import PartitionSpec as P

HEAD_DIM = 64
AXES = ("gh", "gl", "p", "c", "zh", "zl")
f32 = jnp.float32
bf16 = jnp.bfloat16
MESH = pl.DeviceIdType.MESH
VMEM, ANY = pltpu.VMEM, pl.ANY
eps_norm = 1e-05
TILE = 256


def centre(values):
    mean = jnp.mean(values, axis=-1, keepdims=True)
    centred = values - mean
    spread = jnp.mean(centred * centred, axis=-1, keepdims=True)
    rate = lax.rsqrt(spread + eps_norm)
    return centred * rate, rate


def norm_rows(values, gain, shift):
    return centre(values)[0] * gain + shift


def norm_pull(values, gain, grad):
    hat, rate = centre(values)
    scaled = grad * gain
    along = jnp.mean(scaled * hat, axis=-1, keepdims=True)
    level = jnp.mean(scaled, axis=-1, keepdims=True)
    return (
        rate * (scaled - level - hat * along),
        jnp.sum(grad * hat, axis=0, keepdims=True),
        jnp.sum(grad, axis=0, keepdims=True),
    )


def dot_nt(left, right):
    return lax.dot_general(left, right, (((1,), (1,)), ((), ())), preferred_element_type=f32)


def dot_tn(left, right):
    return lax.dot_general(left, right, (((0,), (0,)), ((), ())), preferred_element_type=f32)


def dot_nn(left, right):
    return jnp.dot(left, right, preferred_element_type=f32)


def cut_rows(rows):
    first = (rows // 2 + 15) // 16 * 16
    return ((0, first), (first, rows - first))


def flipped(*names):
    return {name: 1 - lax.axis_index(name) for name in names}


def greet(*others):
    barrier = pltpu.get_barrier_semaphore()
    for names in others:
        pl.semaphore_signal(barrier, inc=1, device_id=flipped(*names), device_id_type=MESH)
    pl.semaphore_wait(barrier, len(others))


GROUP = (("c",), ("zl",))
ACROSS = (("p",), ("gl",), ("gl", "p"))
FETCH = (("zh",), *ACROSS)


def remote(source, target, send, receive, device):
    return pltpu.make_async_remote_copy(
        src_ref=source,
        dst_ref=target,
        send_sem=send,
        recv_sem=receive,
        device_id=device,
        device_id_type=MESH,
    )


def tiles(width, body):
    def step(index, carry):
        body(pl.ds(pl.multiple_of(index * TILE, TILE), TILE))
        return carry

    lax.fori_loop(0, width // TILE, step, 0)


def exchange(rows, held, work, first, sums, send, receive):
    mate, near = flipped("c"), flipped("zl")
    own = pl.ds(0, rows)
    parts = cut_rows(rows)
    copies = [remote(held.at[own], held.at[pl.ds(rows, rows)], send.at[0], receive.at[0], mate)]
    copies[0].start()
    along = []
    for index, (start, size) in enumerate(parts):
        place = pl.ds(2 * rows + 2 * start, size)
        copy = remote(held.at[pl.ds(start, size)], held.at[place], send.at[1 + index], receive.at[1 + index], near)
        copy.start()
        along.append(copy)

    def keep(row, columns, value):
        first[pl.ds(row, value.shape[0]), columns] = value

    work(0, rows, keep)
    copies[0].wait_recv()

    def keep_mate(row, columns, value):
        sums[0, pl.ds(row - rows, value.shape[0]), columns] = value.astype(bf16)

    work(rows, rows, keep_mate)
    back = remote(sums.at[0], sums.at[1], send.at[3], receive.at[3], mate)
    back.start()
    copies.append(back)
    final = []
    for index, (start, size) in enumerate(parts):
        place = 2 * rows + 2 * start
        along[index].wait_recv()
        relay = remote(
            held.at[pl.ds(place, size)], held.at[pl.ds(place + size, size)], send.at[4 + index], receive.at[4 + index], mate
        )
        relay.start()
        relay.wait_recv()

        def keep_far(row, columns, value, place=place, start=start, size=size):
            first[pl.ds(rows + start, size), columns] = value[:size]
            sums[2, pl.ds(start, size), columns] = value[size:].astype(bf16)

        work(place, 2 * size, keep_far)
        part = pl.ds(start, size)
        cross = remote(sums.at[2, part], sums.at[3, part], send.at[6 + index], receive.at[6 + index], mate)
        cross.start()
        cross.wait_recv()
        sums[4, part, :] = (first[pl.ds(rows + start, size), :] + sums[3, part, :].astype(f32)).astype(bf16)
        last = remote(sums.at[4, part], sums.at[5, part], send.at[8 + index], receive.at[8 + index], near)
        last.start()
        final.append(last)
        copies += [relay, cross]

    def finish():
        back.wait_recv()
        for copy in final:
            copy.wait_recv()
        for copy in copies + along + final:
            copy.wait_send()

    return finish


def run(body, number, inputs, outputs, scratch, flops, transcendentals=0):
    names = [*inputs, *outputs, *scratch]

    def kernel(*refs):
        body(types.SimpleNamespace(**dict(zip(names, refs))))

    moved = sum(value.size * value.dtype.itemsize for value, _ in inputs.values())
    results = pl.pallas_call(
        kernel,
        out_shape=tuple(jax.ShapeDtypeStruct(shape, kind) for shape, kind, _ in outputs.values()),
        in_specs=[pl.BlockSpec(memory_space=memory) for _, memory in inputs.values()],
        out_specs=tuple(pl.BlockSpec(memory_space=memory) for _, _, memory in outputs.values()),
        scratch_shapes=list(scratch.values()),
        compiler_params=pltpu.CompilerParams(collective_id=number, has_side_effects=True, vmem_limit_bytes=58 << 20),
        cost_estimate=pl.CostEstimate(flops=flops, bytes_accessed=moved, transcendentals=transcendentals),
    )(*[value for value, _ in inputs.values()])
    return types.SimpleNamespace(**dict(zip(outputs, results)))


def semaphores(count):
    return pltpu.SemaphoreType.DMA((count,))


def group_scratch(rows, width):
    return {
        "first": VMEM((2 * rows, width), f32),
        "sums": VMEM((6, rows, width), bf16),
        "send": semaphores(10),
        "receive": semaphores(10),
    }


def pick(ref, rows):
    return ref.at[:, rows, :] if len(ref.shape) == 3 else ref.at[rows, :]


def part_shape(shape, parts):
    return (*shape[:-2], shape[-2] // parts, shape[-1])


def holds():
    return lax.axis_index("c") == lax.axis_index("zh")


class Fetching:
    copies = 4

    def __init__(self, source, target, send, receive, local):
        self.source, self.target, self.send, self.receive, self.local = source, target, send, receive, local
        self.size = source.shape[-2] // 4

    def rows_of(self, names=()):
        gl, p = [(1 - lax.axis_index(name)) if name in names else lax.axis_index(name) for name in ("gl", "p")]
        return pl.ds(pl.multiple_of((2 * gl + p) * self.size, 16), self.size)

    def along(self):
        rows = self.rows_of()
        return remote(
            pick(self.source, rows), pick(self.target, rows), self.send.at[0], self.receive.at[0], flipped("zh")
        )

    def share(self):
        rows = pick(self.target, self.rows_of())
        return [
            remote(rows, rows, self.send.at[1 + slot], self.receive.at[1 + slot], flipped(*names))
            for slot, names in enumerate(ACROSS)
        ]

    def step_along(self):
        @pl.when(holds())
        def _():
            self.along().start()
            pltpu.make_async_copy(self.source, self.target, self.local.at[0]).start()

    def step_share(self):
        @pl.when(jnp.logical_not(holds()))
        def _():
            self.along().wait_recv()
            for copy in self.share():
                copy.start()

    def step_end(self):
        @pl.when(holds())
        def _():
            self.along().wait_send()
            pltpu.make_async_copy(self.source, self.target, self.local.at[0]).wait()

        @pl.when(jnp.logical_not(holds()))
        def _():
            for copy in self.share():
                copy.wait()


def fetch_jobs(refs, names, layer):
    return [
        Fetching(
            getattr(refs, name + "_from").at[layer], getattr(refs, name + "_to"), getattr(refs, name + "_send"),
            getattr(refs, name + "_receive"), getattr(refs, name + "_local"),
        )
        for name in names
    ]


def fetch_inputs(weights):
    return {name + "_from": (value, ANY) for name, value in weights.items()}


def fetch_outputs(weights):
    return {name + "_to": (value.shape[1:], bf16, ANY) for name, value in weights.items()}


def fetch_scratch(weights):
    result = {}
    for name in weights:
        result[name + "_send"] = semaphores(4)
        result[name + "_receive"] = semaphores(4)
        result[name + "_local"] = semaphores(1)
    return result


def every(jobs, step):
    for job in jobs:
        getattr(job, step)()


def head(hidden_in, weight, weights):
    def body(r):
        greet(("c",), ("c", "zh"), *FETCH)
        jobs = fetch_jobs(r, weights, 0)
        jobs[0].step_along()
        swap = remote(r.hidden, r.landed, r.send.at[0], r.receive.at[0], flipped("c", "zh"))
        scale = remote(r.weight, r.other, r.send.at[1], r.receive.at[1], flipped("c"))
        scale.start()

        @pl.when(jnp.logical_not(holds()))
        def _():
            swap.start()

        every(jobs[1:], "step_along")
        every(jobs, "step_share")

        @pl.when(holds())
        def _():
            r.stream[...] = r.hidden[...].astype(f32)

        scale.wait()
        r.scale[...] = jnp.where(holds(), r.weight[...], r.other[...])

        @pl.when(jnp.logical_not(holds()))
        def _():
            swap.wait()
            r.stream[...] = r.landed[...].astype(f32)

        every(jobs, "step_end")

    return run(
        body,
        0,
        {"hidden": (hidden_in, VMEM), "weight": (weight, VMEM), **fetch_inputs(weights)},
        {"stream": (hidden_in.shape, f32, VMEM), "scale": (weight.shape, f32, VMEM), **fetch_outputs(weights)},
        {
            "landed": VMEM(hidden_in.shape, bf16),
            "other": VMEM(weight.shape, f32),
            "send": semaphores(2),
            "receive": semaphores(2),
            **fetch_scratch(weights),
        },
        1 << 20,
    )


def gelu_and_slope(values):
    rate, cubic = 0.7978845608028654, 0.044715
    square = values * values
    bend = jnp.tanh(rate * values * (1.0 + cubic * square))
    half = 0.5 * (1.0 + bend)
    slope = half + 0.5 * values * (1.0 - bend * bend) * (rate * (1.0 + 3.0 * cubic * square))
    return values * half, slope


def ffn_forward(layer, middle, gains, shifts, w_up, w_down, weights):
    rows, width = middle.shape
    hidden = w_up.shape[1]

    def body(r):
        loads = [pltpu.make_async_copy(r.w_up, r.up, r.local.at[0]), pltpu.make_async_copy(r.w_down, r.down, r.local.at[1])]
        for copy in loads:
            copy.start()
        greet(*GROUP, *(FETCH if weights else ()))
        jobs = fetch_jobs(r, weights, layer + 1)
        held, active, slope = r.held, r.active, r.slope
        held[pl.ds(0, rows), :] = norm_rows(r.middle[...], r.gains[layer, 2:3, :], r.shifts[layer, 2:3, :]).astype(bf16)
        for copy in loads:
            copy.wait()
        calls = []

        def work(start, size, sink):
            calls.append(start)
            if len(calls) == 1:
                every(jobs, "step_along")
            here = pl.ds(start, size)

            def step(columns):
                upper = dot_nn(held[here, :], r.up[:, columns])
                value, bend = gelu_and_slope(upper)
                active[here, columns] = value.astype(bf16)
                slope[here, columns] = bend.astype(bf16)

            tiles(hidden, step)

            def step_down(columns):
                sink(start, columns, dot_nn(active[here, :], r.down[:, columns]))

            tiles(width, step_down)

        finish = exchange(rows, held, work, r.first, r.sums, r.send, r.receive)
        stores = [
            pltpu.make_async_copy(held, r.held_out, r.local.at[2]),
            pltpu.make_async_copy(active, r.active_out, r.local.at[3]),
            pltpu.make_async_copy(slope, r.slope_out, r.local.at[4]),
        ]
        for copy in stores:
            copy.start()
        every(jobs, "step_share")
        finish()
        total = r.first[pl.ds(0, rows), :] + r.sums[1].astype(f32) + r.sums[5].astype(f32)
        r.second[...] = total
        r.stream[...] = r.middle[...] + norm_rows(total, r.gains[layer, 3:4, :], r.shifts[layer, 3:4, :])
        every(jobs, "step_end")
        for copy in stores:
            copy.wait()

    return run(
        body,
        3 + layer,
        {
            "middle": (middle, VMEM), "gains": (gains, VMEM), "shifts": (shifts, VMEM), "w_up": (w_up, ANY), "w_down": (w_down, ANY),
            **fetch_inputs(weights),
        },
        {
            "second": ((rows, width), f32, VMEM), "stream": ((rows, width), f32, VMEM),
            "held_out": ((4 * rows, width), bf16, ANY), "active_out": ((4 * rows, hidden), bf16, ANY),
            "slope_out": ((4 * rows, hidden), bf16, ANY), **fetch_outputs(weights),
        },
        {
            "held": VMEM((4 * rows, width), bf16), "active": VMEM((4 * rows, hidden), bf16), "slope": VMEM((4 * rows, hidden), bf16),
            "up": VMEM(w_up.shape, bf16), "down": VMEM(w_down.shape, bf16), **group_scratch(rows, width), "local": semaphores(5),
            **fetch_scratch(weights),
        },
        16 * rows * width * hidden,
        4 * rows * hidden,
    )


def ffn_backward(layer, grad, saved, gains, shifts, w_up, w_down):
    middle = saved.middle
    rows, width = middle.shape
    hidden = w_up.shape[1]

    def body(r):
        held, active, slope, pushed, past = r.held, r.active, r.slope, r.pushed, r.past
        loads = [
            pltpu.make_async_copy(r.w_down, r.down, r.local.at[0]),
            pltpu.make_async_copy(r.w_up, r.up, r.local.at[1]),
            pltpu.make_async_copy(r.slope_in, slope, r.local.at[2]),
            pltpu.make_async_copy(r.active_in, active, r.local.at[3]),
            pltpu.make_async_copy(r.held_in, past, r.local.at[4]),
        ]
        for copy in loads:
            copy.start()
        greet(*GROUP)
        pulled, gain_three, shift_three = norm_pull(r.second[...], r.gains[layer, 3:4, :], r.grad[...])
        held[pl.ds(0, rows), :] = pulled.astype(bf16)
        for copy in loads:
            copy.wait()

        def work(start, size, sink):
            here = pl.ds(start, size)

            def step(columns):
                value = dot_nt(held[here, :], r.down[columns, :])
                pushed[here, columns] = (value * slope[here, columns].astype(f32)).astype(bf16)

            tiles(hidden, step)

            def step_up(columns):
                sink(start, columns, dot_nt(pushed[here, :], r.up[columns, :]))

            tiles(width, step_up)

        finish = exchange(rows, held, work, r.first, r.sums, r.send, r.receive)

        def step_down(columns):
            r.outcome[0, columns, :] = dot_tn(active[:, columns], held[...]).astype(bf16)

        tiles(hidden, step_down)
        out_down = pltpu.make_async_copy(r.outcome.at[0], r.grad_down, r.local.at[0])
        out_down.start()

        def step_up(columns):
            r.outcome[1, columns, :] = dot_tn(past[:, columns], pushed[...]).astype(bf16)

        tiles(width, step_up)
        out_up = pltpu.make_async_copy(r.outcome.at[1], r.grad_up, r.local.at[1])
        out_up.start()
        finish()
        total = r.first[pl.ds(0, rows), :] + r.sums[1].astype(f32) + r.sums[5].astype(f32)
        pulled, gain_two, shift_two = norm_pull(r.middle[...], r.gains[layer, 2:3, :], total)
        r.grad_middle[...] = r.grad[...] + pulled
        for index, value in enumerate((gain_two, shift_two, gain_three, shift_three)):
            r.norms[index : index + 1, :] = value
        out_down.wait()
        out_up.wait()

    return run(
        body,
        5 + layer,
        {
            "grad": (grad, VMEM), "second": (saved.second, VMEM), "middle": (middle, VMEM), "gains": (gains, VMEM),
            "shifts": (shifts, VMEM), "held_in": (saved.held_out, ANY), "active_in": (saved.active_out, ANY),
            "slope_in": (saved.slope_out, ANY), "w_up": (w_up, ANY), "w_down": (w_down, ANY),
        },
        {
            "grad_middle": ((rows, width), f32, VMEM), "norms": ((4, width), f32, VMEM),
            "grad_up": (w_up.shape, bf16, ANY), "grad_down": (w_down.shape, bf16, ANY),
        },
        {
            "held": VMEM((4 * rows, width), bf16), "past": VMEM((4 * rows, width), bf16),
            "active": VMEM((4 * rows, hidden), bf16), "slope": VMEM((4 * rows, hidden), bf16),
            "pushed": VMEM((4 * rows, hidden), bf16), "up": VMEM(w_up.shape, bf16), "down": VMEM(w_down.shape, bf16),
            "outcome": VMEM((2, width, hidden), bf16), **group_scratch(rows, width), "local": semaphores(5),
        },
        32 * rows * width * hidden,
    )


def places(rows):
    c, zl = lax.axis_index("c"), lax.axis_index("zl")

    def at(core, part):
        return pl.multiple_of((2 * core + part) * rows, 16)

    return at(c, zl), at(1 - c, zl), at(c, 1 - zl), at(1 - c, 1 - zl)


def gather(rows, held, arrived, send, receive):
    mate, near = flipped("c"), flipped("zl")
    own, others, along, across = places(rows)
    parts = cut_rows(rows)
    here = pl.ds(own, rows)
    copies = [remote(held.at[here], held.at[here], send.at[0], receive.at[0], mate)]
    copies[0].start()
    for index, (start, size) in enumerate(parts):
        part = pl.ds(pl.multiple_of(own + start, 16), size)
        copy = remote(held.at[part], held.at[part], send.at[1 + index], receive.at[1 + index], near)
        copy.start()
        copies.append(copy)
    arrived(own, rows)
    copies[0].wait_recv()
    arrived(others, rows)
    for index, (start, size) in enumerate(parts):
        copies[1 + index].wait_recv()
        first = pl.multiple_of(along + start, 16)
        part = pl.ds(first, size)
        relay = remote(held.at[part], held.at[part], send.at[4 + index], receive.at[4 + index], mate)
        relay.start()
        copies.append(relay)
        arrived(first, size)
        relay.wait_recv()
        arrived(pl.multiple_of(across + start, 16), size)

    def finish():
        for copy in copies:
            copy.wait_send()

    return finish


def scatter(rows, project, first, sums, send, receive):
    mate, near = flipped("c"), flipped("zl")
    own, others, along, across = places(rows)
    parts = cut_rows(rows)
    copies, crossing, final = [], [], []
    for index, (start, size) in enumerate(parts):
        part = pl.ds(start, size)

        def keep_far(columns, value, part=part):
            sums[2, part, columns] = value.astype(bf16)

        project(pl.multiple_of(across + start, 16), size, keep_far)
        cross = remote(sums.at[2, part], sums.at[3, part], send.at[6 + index], receive.at[6 + index], mate)
        cross.start()
        crossing.append(cross)
    for index, (start, size) in enumerate(parts):
        part = pl.ds(start, size)

        def keep_near(columns, value, start=start, size=size):
            first[pl.ds(rows + start, size), columns] = value

        project(pl.multiple_of(along + start, 16), size, keep_near)
        crossing[index].wait_recv()
        sums[4, part, :] = (first[pl.ds(rows + start, size), :] + sums[3, part, :].astype(f32)).astype(bf16)
        last = remote(sums.at[4, part], sums.at[5, part], send.at[8 + index], receive.at[8 + index], near)
        last.start()
        final.append(last)

    def keep_mate(columns, value):
        sums[0, :, columns] = value.astype(bf16)

    project(others, rows, keep_mate)
    back = remote(sums.at[0], sums.at[1], send.at[3], receive.at[3], mate)
    back.start()

    def keep(columns, value):
        first[pl.ds(0, rows), columns] = value

    project(own, rows, keep)

    def finish():
        back.wait_recv()
        for copy in final:
            copy.wait_recv()
        for copy in [back] + crossing + final:
            copy.wait_send()

    return finish


def head_lanes(shape, half):
    lane = lax.broadcasted_iota(jnp.int32, shape, len(shape) - 1)
    return (lane < HEAD_DIM) if half == 0 else (lane >= HEAD_DIM)


def masked(scores, start, first_key):
    query = lax.broadcasted_iota(jnp.int32, scores.shape, 0) + start
    key = lax.broadcasted_iota(jnp.int32, scores.shape, 1) + first_key
    return jnp.where(key <= query, scores, -1e30)


def spans(rows, high):
    if not high:
        return ((0, 2 * rows, True),)
    free = 2 * rows // 128 * 128
    return ((0, free, False), (free, 4 * rows - free, True))


def attend_block(rows, start, high, qkv, attended, lse):
    width = attended.shape[1]
    here = pl.ds(start, rows)
    lane = lax.broadcasted_iota(jnp.int32, (rows, 128), 1)
    tops = jnp.zeros((rows, 128), f32)
    for pair in range(width // 128):
        columns = slice(pair * 128, pair * 128 + 128)
        query = qkv[here, columns] * bf16(HEAD_DIM ** (-0.5))
        results = []
        for half in range(2):
            only = jnp.where(head_lanes(query.shape, half), query, 0)
            scores = []
            for begin, size, mask in spans(rows, high):
                part = dot_nt(only, qkv[pl.ds(begin, size), width + pair * 128 : width + pair * 128 + 128])
                scores.append(masked(part, start, begin) if mask else part)
            top = functools.reduce(jnp.maximum, [jnp.max(part, axis=-1, keepdims=True) for part in scores])
            total, result = 0.0, 0.0
            for (begin, size, _), part in zip(spans(rows, high), scores):
                weights = jnp.exp(part - top)
                total = total + jnp.sum(weights, axis=-1, keepdims=True)
                values = qkv[pl.ds(begin, size), 2 * width + pair * 128 : 2 * width + pair * 128 + 128]
                result = result + dot_nn(weights.astype(bf16), values)
            results.append(result / total)
            tops = jnp.where(lane == 2 * pair + half, top + jnp.log(total), tops)
        attended[here, columns] = jnp.where(head_lanes((rows, 128), 0), results[0], results[1]).astype(bf16)
    lse[here, :] = tops


def attention_forward(layer, stream, gains, shifts, w_qkv, w_out, weights):
    rows, model = stream.shape
    width = w_out.shape[0]

    def body(r):
        held, qkv, attended, lse, weight = r.held, r.qkv, r.attended, r.lse, r.weight
        loads = [
            pltpu.make_async_copy(r.w_qkv.at[index], weight.at[:, pl.ds(index * width, width)], r.local.at[index])
            for index in range(3)
        ]
        loads.append(pltpu.make_async_copy(r.w_out, r.out, r.local.at[3]))
        for copy in loads:
            copy.start()
        greet(*GROUP, *(FETCH if weights else ()))
        jobs = fetch_jobs(r, weights, layer)
        own = places(rows)[0]
        held[pl.ds(own, rows), :] = norm_rows(r.stream[...], r.gains[layer, 0:1, :], r.shifts[layer, 0:1, :]).astype(bf16)
        for copy in loads:
            copy.wait()
        calls = []

        def arrived(start, size):
            calls.append(start)
            if len(calls) == 1:
                every(jobs, "step_along")
            here = pl.ds(start, size)

            def step(columns):
                qkv[here, columns] = dot_nn(held[here, :], weight[:, columns]).astype(bf16)

            tiles(3 * width, step)

        sent = gather(rows, held, arrived, r.send, r.receive)
        stores = [pltpu.make_async_copy(held, r.held_out, r.local.at[0]), pltpu.make_async_copy(qkv, r.qkv_out, r.local.at[1])]
        for copy in stores:
            copy.start()
        zl = lax.axis_index("zl")

        def attend(quarter, high):
            attend_block(rows, pl.multiple_of(quarter * rows, 16), high, qkv, attended, lse)

        attend(3 - zl, True)
        attend(1 - zl, False)
        done = []

        def term(start, size, sink):
            if size == rows and not done:
                done.append(True)
                if jobs:
                    jobs[0].step_share()
                attend(2 + zl, True)
                every(jobs[1:], "step_share")
                attend(zl, False)
            here = pl.ds(start, size)

            def step(columns):
                sink(columns, dot_nn(attended[here, :], r.out[:, columns]))

            tiles(model, step)

        finish = scatter(rows, term, r.first, r.sums, r.send, r.receive)
        late = [pltpu.make_async_copy(attended, r.attended_out, r.local.at[2]), pltpu.make_async_copy(lse, r.lse_out, r.local.at[3])]
        for copy in late:
            copy.start()
        finish()
        total = r.first[pl.ds(0, rows), :] + r.sums[1].astype(f32) + r.sums[5].astype(f32)
        r.branch[...] = total
        r.middle[...] = r.stream[...] + norm_rows(total, r.gains[layer, 1:2, :], r.shifts[layer, 1:2, :])
        sent()
        every(jobs, "step_end")
        for copy in stores + late:
            copy.wait()

    return run(
        body,
        1 + layer,
        {
            "stream": (stream, VMEM), "gains": (gains, VMEM), "shifts": (shifts, VMEM), "w_qkv": (w_qkv, ANY), "w_out": (w_out, ANY),
            **fetch_inputs(weights),
        },
        {
            "branch": ((rows, model), f32, VMEM), "middle": ((rows, model), f32, VMEM),
            "held_out": ((4 * rows, model), bf16, ANY), "qkv_out": ((4 * rows, 3 * width), bf16, ANY),
            "attended_out": ((4 * rows, width), bf16, ANY), "lse_out": ((4 * rows, 128), f32, ANY), **fetch_outputs(weights),
        },
        {
            "held": VMEM((4 * rows, model), bf16), "qkv": VMEM((4 * rows, 3 * width), bf16), "attended": VMEM((4 * rows, width), bf16),
            "lse": VMEM((4 * rows, 128), f32), "weight": VMEM((model, 3 * width), bf16), "out": VMEM(w_out.shape, bf16),
            **group_scratch(rows, model), "local": semaphores(4), **fetch_scratch(weights),
        },
        24 * rows * model * width,
        64 * rows * rows,
    )


def attend_block_back(rows, start, high, qkv, attended_grad, lse, inner, grad_query, grad_key, grad_value):
    width = attended_grad.shape[1]
    here = pl.ds(start, rows)
    scale = HEAD_DIM ** (-0.5)
    for pair in range(width // 128):
        columns = slice(pair * 128, pair * 128 + 128)
        query = qkv[here, columns] * bf16(scale)
        above = attended_grad[here, columns]
        result = 0.0
        for half in range(2):
            head = 2 * pair + half
            only = jnp.where(head_lanes(query.shape, half), query, 0)
            grad = jnp.where(head_lanes(query.shape, half), above, 0)
            for begin, size, mask in spans(rows, high):
                keys = pl.ds(begin, size)
                key = qkv[keys, width + pair * 128 : width + pair * 128 + 128]
                value = qkv[keys, 2 * width + pair * 128 : 2 * width + pair * 128 + 128]
                scores = dot_nt(only, key)
                if mask:
                    scores = masked(scores, start, begin)
                probs = jnp.exp(scores - lse[here, head : head + 1])
                grad_probs = dot_nt(grad, value)
                grad_scores = (probs * (grad_probs - inner[here, head : head + 1])).astype(bf16)
                key_only = jnp.where(head_lanes(key.shape, half), key, 0)
                result = result + dot_nn(grad_scores, key_only)
                grad_key[keys, columns] += dot_tn(grad_scores, only)
                grad_value[keys, columns] += dot_tn(probs.astype(bf16), grad)
        grad_query[here, columns] = (result * scale).astype(bf16)


def attention_backward(layer, grad, stream, saved, gains, shifts, w_qkv, w_out):
    rows, model = stream.shape
    width = w_out.shape[0]

    def body(r):
        held, past, qkv, attended, lse, inner, above = r.held, r.past, r.qkv, r.attended, r.lse, r.inner, r.above
        pushed, grad_key, grad_value, weight = r.pushed, r.grad_key, r.grad_value, r.weight
        loads = [
            pltpu.make_async_copy(r.w_out, r.out, r.local.at[3]),
            pltpu.make_async_copy(r.attended_in, attended, r.local.at[4]),
            pltpu.make_async_copy(r.qkv_in, qkv, r.local.at[5]),
            pltpu.make_async_copy(r.lse_in, lse, r.local.at[6]),
            *[
                pltpu.make_async_copy(r.w_qkv.at[index], weight.at[:, pl.ds(index * width, width)], r.local.at[index])
                for index in range(3)
            ],
            pltpu.make_async_copy(r.held_in, past, r.local.at[7]),
        ]
        for copy in loads:
            copy.start()
        greet(*GROUP)
        own = places(rows)[0]
        pulled, gain_one, shift_one = norm_pull(r.branch[...], r.gains[layer, 1:2, :], r.grad[...])
        held[pl.ds(own, rows), :] = pulled.astype(bf16)
        grad_key[...] = jnp.zeros_like(grad_key)
        grad_value[...] = jnp.zeros_like(grad_value)
        for copy in loads:
            copy.wait()
        zl = lax.axis_index("zl")

        def back(quarter, high):
            attend_block_back(
                rows, pl.multiple_of(quarter * rows, 16), high, qkv, above, lse, inner, pushed, grad_key, grad_value
            )

        blocks = []

        def arrived(start, size):
            here = pl.ds(start, size)
            value = dot_nt(held[here, :], r.out[...]).astype(bf16)
            above[here, :] = value
            product = value.astype(f32) * attended[here, :].astype(f32)
            lane = lax.broadcasted_iota(jnp.int32, (size, 128), 1)
            tile = jnp.zeros((size, 128), f32)
            for pair in range(width // 128):
                part = product[:, pair * 128 : pair * 128 + 128]
                for half in range(2):
                    one = jnp.sum(jnp.where(head_lanes(part.shape, half), part, 0.0), axis=-1, keepdims=True)
                    tile = jnp.where(lane == 2 * pair + half, one, tile)
            inner[here, :] = tile
            blocks.append(size)
            if len(blocks) == 2:
                back(2 + zl, True)
                back(zl, False)

        sent = gather(rows, held, arrived, r.send, r.receive)
        back(3 - zl, True)
        back(1 - zl, False)
        pushed[:, pl.ds(width, width)] = grad_key[...].astype(bf16)
        pushed[:, pl.ds(2 * width, width)] = grad_value[...].astype(bf16)

        def term(start, size, sink):
            here = pl.ds(start, size)

            def step(columns):
                sink(columns, dot_nt(pushed[here, :], weight[columns, :]))

            tiles(model, step)

        finish = scatter(rows, term, r.first, r.sums, r.send, r.receive)

        def step_out(columns):
            r.outcome_out[:, columns] = dot_tn(attended[...], held[:, columns]).astype(bf16)

        tiles(model, step_out)
        outs = [pltpu.make_async_copy(r.outcome_out, r.grad_out, r.local.at[0])]
        outs[0].start()

        def step_qkv(columns):
            r.outcome[columns, :] = dot_tn(past[:, columns], pushed[...]).astype(bf16)

        tiles(model, step_qkv)
        for index in range(3):
            copy = pltpu.make_async_copy(r.outcome.at[:, pl.ds(index * width, width)], r.grad_qkv.at[index], r.local.at[1 + index])
            copy.start()
            outs.append(copy)
        finish()
        total = r.first[pl.ds(0, rows), :] + r.sums[1].astype(f32) + r.sums[5].astype(f32)
        pulled, gain_zero, shift_zero = norm_pull(r.stream[...], r.gains[layer, 0:1, :], total)
        r.grad_stream[...] = r.grad[...] + pulled
        for index, value in enumerate((gain_zero, shift_zero, gain_one, shift_one)):
            r.norms[index : index + 1, :] = value
        sent()
        for copy in outs:
            copy.wait()

    return run(
        body,
        7 + layer,
        {
            "grad": (grad, VMEM), "branch": (saved.branch, VMEM), "stream": (stream, VMEM), "gains": (gains, VMEM),
            "shifts": (shifts, VMEM), "held_in": (saved.held_out, ANY), "qkv_in": (saved.qkv_out, ANY),
            "attended_in": (saved.attended_out, ANY), "lse_in": (saved.lse_out, ANY), "w_qkv": (w_qkv, ANY), "w_out": (w_out, ANY),
        },
        {
            "grad_stream": ((rows, model), f32, VMEM), "norms": ((4, model), f32, VMEM),
            "grad_qkv": (w_qkv.shape, bf16, ANY), "grad_out": (w_out.shape, bf16, ANY),
        },
        {
            "held": VMEM((4 * rows, model), bf16), "past": VMEM((4 * rows, model), bf16), "qkv": VMEM((4 * rows, 3 * width), bf16),
            "attended": VMEM((4 * rows, width), bf16), "lse": VMEM((4 * rows, 128), f32), "inner": VMEM((4 * rows, 128), f32),
            "above": VMEM((4 * rows, width), bf16), "pushed": VMEM((4 * rows, 3 * width), bf16),
            "grad_key": VMEM((4 * rows, width), f32), "grad_value": VMEM((4 * rows, width), f32),
            "weight": VMEM((model, 3 * width), bf16), "out": VMEM(w_out.shape, bf16), "outcome": VMEM((model, 3 * width), bf16),
            "outcome_out": VMEM(w_out.shape, bf16), **group_scratch(rows, model), "local": semaphores(8),
        },
        60 * rows * model * width,
        64 * rows * rows,
    )


SUM_COPIES = 11


class Summing:
    def __init__(self, source, target, land, mine, part, cross, send, receive, local):
        self.source, self.target = source, target
        self.land, self.mine, self.part, self.cross = land, mine, part, cross
        self.send, self.receive, self.local = send, receive, local
        self.size = source.shape[-2] // 4

    def rows_of(self, names=()):
        gl, p = [(1 - lax.axis_index(name)) if name in names else lax.axis_index(name) for name in ("gl", "p")]
        return pl.ds(pl.multiple_of((2 * gl + p) * self.size, 16), self.size)

    def copy(self, slot, source, target, device):
        return remote(source, target, self.send.at[slot], self.receive.at[slot], device)

    def spread(self):
        return [
            self.copy(slot, pick(self.source, self.rows_of(names)), self.land.at[slot], flipped(*names))
            for slot, names in enumerate(ACROSS)
        ]

    def keep(self):
        return pltpu.make_async_copy(pick(self.source, self.rows_of()), self.mine, self.local.at[0])

    def along(self):
        return self.copy(3, self.part, self.cross, flipped("zh"))

    def place(self):
        return pltpu.make_async_copy(self.part, pick(self.target, self.rows_of()), self.local.at[1])

    def share(self):
        own = pick(self.target, self.rows_of())
        return [self.copy(4 + slot, self.part, own, flipped(*names)) for slot, names in enumerate((*ACROSS, ("c",)))]

    def relays(self):
        rows = [pick(self.target, self.rows_of(names)) for names in ACROSS]
        return [self.copy(8 + slot, part, part, flipped("c")) for slot, part in enumerate(rows)]

    def step_spread(self):
        every(self.spread(), "start")
        self.keep().start()

    def step_add(self):
        self.keep().wait()
        every(self.spread(), "wait_recv")
        total = self.mine[...].astype(f32)
        for slot in range(3):
            total = total + self.land[slot].astype(f32)
        self.part[...] = total.astype(bf16)

        @pl.when(jnp.logical_not(holds()))
        def _():
            self.along().start()

    def step_share(self):
        @pl.when(holds())
        def _():
            self.along().wait_recv()
            self.part[...] = (self.part[...].astype(f32) + self.cross[...].astype(f32)).astype(bf16)
            every(self.share(), "start")
            self.place().start()

    def step_relay(self):
        @pl.when(holds())
        def _():
            for copy, relay in zip(self.share()[:3], self.relays()):
                copy.wait_recv()
                relay.start()

    def step_end(self):
        every(self.spread(), "wait_send")

        @pl.when(holds())
        def _():
            every(self.share() + self.relays(), "wait_send")
            self.place().wait()

        @pl.when(jnp.logical_not(holds()))
        def _():
            self.along().wait_send()
            every([self.share()[3]] + self.relays(), "wait_recv")


def summing_scratch(name, shape):
    part = part_shape(shape, 4)
    return {
        name + "_land": VMEM((3, *part), bf16),
        name + "_mine": VMEM(part, bf16),
        name + "_part": VMEM(part, bf16),
        name + "_cross": VMEM(part, bf16),
        name + "_send": semaphores(SUM_COPIES),
        name + "_receive": semaphores(SUM_COPIES),
        name + "_local": semaphores(2),
    }


CUBE = ("c", "zl", "p", "gl", "zh")


def tail(grads, norms, mixed, grad_in):
    def body(r):
        jobs = [
            Summing(*[getattr(r, name + end) for end in ("_from", "_to", "_land", "_mine", "_part", "_cross", "_send", "_receive", "_local")])
            for name in grads
        ]
        greet(*GROUP, *FETCH, ("c", "zh"))
        swaps = []
        for index, (source, low, landed) in enumerate(((r.mixed, r.low_mixed, r.land_mixed), (r.grad_in, r.low_grad, r.land_grad))):
            low[...] = source[...].astype(bf16)
            swaps.append(remote(low, landed, r.send.at[index], r.receive.at[index], flipped("c", "zh")))

        @pl.when(jnp.logical_not(holds()))
        def _():
            every(swaps, "start")

        total = r.norms[...]
        for index, name in enumerate(CUBE):
            r.norms_out[...] = total
            copy = remote(r.norms_out, r.land.at[index], r.send.at[2 + index], r.receive.at[2 + index], flipped(name))
            copy.start()
            if index == 0:
                every(jobs[:2], "step_spread")
            copy.wait()
            total = total + r.land[index]
        r.norms_out[...] = total
        count = len(jobs)
        for index in range(count + 3):
            if index < count:
                jobs[index].step_add()
                every(jobs[index + 2 : index + 3], "step_spread")
            if 0 <= index - 1 < count:
                jobs[index - 1].step_share()
            if 0 <= index - 2 < count:
                jobs[index - 2].step_relay()
            if 0 <= index - 3 < count:
                jobs[index - 3].step_end()

        @pl.when(holds())
        def _():
            r.mixed_out[...] = r.mixed[...]
            r.grad_out[...] = r.grad_in[...]

        @pl.when(jnp.logical_not(holds()))
        def _():
            every(swaps, "wait")
            r.mixed_out[...] = r.land_mixed[...].astype(f32)
            r.grad_out[...] = r.land_grad[...].astype(f32)

    scratch = {
        "land": VMEM((len(CUBE), *norms.shape), f32),
        "send": semaphores(2 + len(CUBE)),
        "receive": semaphores(2 + len(CUBE)),
        **{name: VMEM(mixed.shape, bf16) for name in ("low_mixed", "land_mixed", "low_grad", "land_grad")},
    }
    for name, value in grads.items():
        scratch.update(summing_scratch(name, value.shape))
    return run(
        body,
        9,
        {
            **{name + "_from": (value, ANY) for name, value in grads.items()},
            "norms": (norms, VMEM), "mixed": (mixed, VMEM), "grad_in": (grad_in, VMEM),
        },
        {
            **{name + "_to": (value.shape, bf16, ANY) for name, value in grads.items()},
            "norms_out": (norms.shape, f32, VMEM), "mixed_out": (mixed.shape, f32, VMEM), "grad_out": (mixed.shape, f32, VMEM),
        },
        scratch,
        1 << 20,
    )


def per_device(hidden_in, cotangent, group_ids, group_sizes, w_qkv, w_out, w_up, w_down, gains, shifts):
    layers = w_qkv.shape[0]
    size = jnp.sum(jnp.where(jnp.arange(group_sizes.shape[0]) == group_ids[0], group_sizes, 0))
    weight = jnp.full((8, 128), 1.0 / size.astype(f32), f32)
    start = head(hidden_in, weight, {"qkv": w_qkv, "out": w_out})
    stream, qkv, out = start.stream, start.qkv_to, start.out_to
    attentions, ffns = [], []
    for layer in range(layers):
        last = layer + 1 == layers
        att = attention_forward(layer, stream, gains, shifts, qkv, out, {"up": w_up, "down": w_down})
        ffn = ffn_forward(layer, att.middle, gains, shifts, att.up_to, att.down_to, {} if last else {"qkv": w_qkv, "out": w_out})
        ffn.middle = att.middle
        attentions.append((stream, att, qkv, out))
        ffns.append((ffn, att.up_to, att.down_to))
        stream = ffn.stream
        if not last:
            qkv, out = ffn.qkv_to, ffn.out_to
    cotangent = lax.ppermute(cotangent, ("c", "zh"), ((0, 0), (1, 2), (2, 1), (3, 3)))
    grad = cotangent.astype(f32) * start.scale[0, 0]
    grads, norms = {}, [None] * layers
    for layer in reversed(range(layers)):
        back = ffn_backward(layer, grad, ffns[layer][0], gains, shifts, *ffns[layer][1:])
        before, att, qkv, out = attentions[layer]
        deep = attention_backward(layer, back.grad_middle, before, att, gains, shifts, qkv, out)
        grad = deep.grad_stream
        for name, value in (("up", back.grad_up), ("down", back.grad_down), ("qkv", deep.grad_qkv), ("out", deep.grad_out)):
            grads[f"{name}{layer}"] = value
        norms[layer] = jnp.concatenate([deep.norms, back.norms])
    total = tail(grads, jnp.concatenate(norms), stream, grad)

    def stacked(name):
        whole = jnp.stack([getattr(total, f"{name}{layer}_to") for layer in range(layers)]).astype(f32)
        return lax.psum(whole, "gh") if lax.axis_size("gh") > 1 else whole

    sums = total.norms_out.reshape(layers, 4, 2, -1)
    if lax.axis_size("gh") > 1:
        sums = lax.psum(sums, "gh")
    return (
        total.mixed_out, total.grad_out, stacked("qkv"), stacked("out"), stacked("up"), stacked("down"), sums[:, :, 0], sums[:, :, 1]
    )


def solution(mesh):
    fine = jax.sharding.Mesh(mesh.devices.reshape(-1, 2, 2, 2, 2, 2), AXES)
    dp = ("gh", "gl", "p", "c")
    tensor = ("zh", "zl")
    rows = P((*dp, *tensor), None)
    weights = (
        P(None, None, None, tensor),
        P(None, tensor, None),
        P(None, None, tensor),
        P(None, tensor, None),
    )
    return jax.shard_map(
        per_device,
        mesh=fine,
        in_specs=(rows, rows, P(dp), P(), *weights, P(), P()),
        out_specs=(rows, rows, *weights, P(), P()),
        check_vma=False,
    )
```

time: 1170 us -> 882 us (0.75)
  waiting for transfers between devices: 620 us -> 0.01 us
  Pallas kernels: 322 us -> 842 us
  starting transfers between devices: 65.1 us -> 1.71 us
  blocking collectives: 52.1 us -> 0 us
  local copies, waits for them, and re-layouts: 40.1 us -> 8.27 us
  other arithmetic: 48.4 us -> 17.1 us
  between operations: 16.7 us -> 2.61 us
    pallas_call x8 -> x10, Pallas kernels: 322 us -> 842 us  [run(): pl.pallas_call(kernel, out_shape=tuple((jax.ShapeDtypeStruct(shape, kind)...]
    all_gather x12 -> x0, waiting for transfers between devices: 211 us -> none  [the longest x6 168 us: sum_weight(): lax.all_gather(part, BATCH, axis=0, tiled=True).reshape(shape)]
    ppermute x28 -> x1, waiting for transfers between devices: 145 us -> 0.01 us  [per_device(): lax.ppermute(cotangent, ('c', 'zh'), ((0, 0), (1, 2), (2, 1), (3, 3)))]
    reduce_scatter x8 -> x0, waiting for transfers between devices: 137 us -> none  [sum_weight(): part = lax.psum_scatter(flat, BATCH, scatter_dimension=0, tiled=True)]
    psum x1 -> x0, waiting for transfers between devices: 123 us -> none  [per_device(): norm_sums = lax.psum(jnp.stack(norm_grads), AXES).reshape(layers, 4, 2, -1)]
    ppermute x28 -> x1, starting transfers between devices: 64.3 us -> 1.71 us  [per_device(): lax.ppermute(cotangent, ('c', 'zh'), ((0, 0), (1, 2), (2, 1), (3, 3)))]
    all_gather x4 -> x0, blocking collectives: 50.3 us -> none  [the longest x2 26.3 us: sum_weight(): lax.all_gather(part, BATCH, axis=0, tiled=True).reshape(shape)]
    select_n x12 -> x0, other arithmetic: 17.4 us -> none  [the longest x4 12.3 us: fetch_weight(): return jnp.where(keeps(), weight, rest)]
  transfers between devices with their start and end apart: 49 -> 1, of which waited for: 36 -> 0; matrix products, arithmetic and copies ran while one was open for 6% -> 0% of each run, Pallas kernels for 4% -> 52%
where the time goes in v3:
time: 882 us; the launch traced here: 872 us
  Pallas kernels  842 us (95%)
  other arithmetic  17.1 us (2%)
    pallas_call x10, Pallas kernels, run(): pl.pallas_call(kernel, out_shape=tuple((jax.ShapeDtypeStruct(shape, kind)...  842 us
  transfers between devices with their start and end apart: 1, of which 0 were waited for; matrix products, arithmetic and copies ran while one was open for 0% of the time, Pallas kernels for 52%

profile of v3, /device:TPU:0, one launch (start us, length us, event | category | flops | bytes accessed | tf_op | source)
XLA Modules:
  0.0 871.8 jit_solution(2151004153976238678)
XLA Ops:
  0.6 1.7 collective-permute-start
  3.0 1.3 fusion
  5.6 71.2 %shard_map.161 = (f32[272,1024]{1,0:T(8,128)}, f32[8,128]{1,0:T(8,128)}, bf16[3,1024,256]{2,1,0:T(8,128)(2,1)}, bf16[256,1024]{1,0:T(8,128)(2,1)}) custom-call(bf16[272,1024]{1,0:T(8,128)(2,1)} %refs_0_.1, f32[8,128]{1,0:T(8,128)} %broadcast_in_dim.8.refs_1_, bf16[2,3,1024,256]{3,2,1,0:T(8,128)(2,1)} %refs_5_.4, bf16[2,256,1024]{2,1,0:T(8,128)(2,1)} %refs_6_.4), custom_call_target="tpu_custom_call" | custom-call | flops 1048576 | bytes 4755456 | tf_op jit(solution)/shard_map/pallas_call | solution.py:165
  76.8 1.2 slice.9
  78.0 134.0 %shard_map.162 = (f32[272,1024]{1,0:T(8,128)}, f32[272,1024]{1,0:T(8,128)}, bf16[1088,1024]{1,0:T(8,128)(2,1)}, bf16[1088,768]{1,0:T(8,128)(2,1)}, bf16[1088,256...) custom-call(f32[272,1024]{1,0:T(8,128)} %get-tuple-element.68.refs_0_.refs_2_, ...), custom_call_target="tpu_custom_call" | custom-call | flops 1711276032 | bytes 11665408 | tf_op jit(solution)/shard_map/pallas_call | solution.py:165
  212.0 69.9 %shard_map.163 = (f32[272,1024]{1,0:T(8,128)}, f32[272,1024]{1,0:T(8,128)}, bf16[1088,1024]{1,0:T(8,128)(2,1)}, bf16[1088,1024]{1,0:T(8,128)(2,1)}, bf16[1088,10...) custom-call(f32[272,1024]{1,0:T(8,128)} %get-tuple-element.71.refs_0_.refs_2_, ...), custom_call_target="tpu_custom_call" | custom-call | flops 4563402752 | bytes 9568256 | tf_op jit(solution)/shard_map/pallas_call | solution.py:165
  281.9 133.2 %shard_map.164 = (f32[272,1024]{1,0:T(8,128)}, f32[272,1024]{1,0:T(8,128)}, bf16[1088,1024]{1,0:T(8,128)(2,1)}, bf16[1088,768]{1,0:T(8,128)(2,1)}, bf16[1088,256...) custom-call(f32[272,1024]{1,0:T(8,128)} %get-tuple-element.74.refs_0_.refs_2_, ...), custom_call_target="tpu_custom_call" | custom-call | flops 1711276032 | bytes 11665408 | tf_op jit(solution)/shard_map/pallas_call | solution.py:165
  415.1 44.5 %shard_map.165 = (f32[272,1024]{1,0:T(8,128)}, f32[272,1024]{1,0:T(8,128)}, bf16[1088,1024]{1,0:T(8,128)(2,1)}, bf16[1088,1024]{1,0:T(8,128)(2,1)}, bf16[1088,1024]{1,0:T(8,128)(2,1)}) custom-call(f32[272,1024]{1,0:T(8,128)} %get-tuple-element.77.refs_0_.refs_2_, f32[2,4,1024]{2,1,0:T(4,128)} %refs_3_.9, f32[2,4,1024]{2,1,0:T(4,128)} %refs_4_.7, ...), custom_call_target="tpu_custom_call" | custom-call | flops 4563402752 | bytes 5373952 | tf_op jit(solution)/shard_map/pallas_call | solution.py:165
  459.7 1.8 convert_multiply_fusion.refs_0_
  461.4 35.8 %shard_map.166 = (f32[272,1024]{1,0:T(8,128)}, f32[4,1024]{1,0:T(4,128)}, bf16[1024,1024]{1,0:T(8,128)(2,1)}, bf16[1024,1024]{1,0:T(8,128)(2,1)}) custom-call(f32[272,1024]{1,0:T(8,128)} %convert_multiply_fusion.refs_0_, f32[272,1024]{1,0:T(8,128)} %get-tuple-element.80.refs_1_, f32[272,1024]{1,0:T(8,128)} %get-tuple-element.77.refs_0_.refs_2_, ...), custom_call_target="tpu_custom_call" | custom-call | flops 9126805504 | bytes 14286848 | tf_op jit(solution)/shard_map/pallas_call | solution.py:165
  497.3 47.6 %shard_map.167 = (f32[272,1024]{1,0:T(8,128)}, f32[4,1024]{1,0:T(4,128)}, bf16[3,1024,256]{2,1,0:T(8,128)(2,1)}, bf16[256,1024]{1,0:T(8,128)(2,1)}) custom-call(f32[272,1024]{1,0:T(8,128)} %get-tuple-element.86.refs_0_, f32[272,1024]{1,0:T(8,128)} %get-tuple-element.87.refs_1_, f32[272,1024]{1,0:T(8,128)} %get-tuple-element.74.refs_0_.refs_2_, ...), custom_call_target="tpu_custom_call" | custom-call | flops 4278190080 | bytes 10518528 | tf_op jit(solution)/shard_map/pallas_call | solution.py:165
  544.9 35.8 %shard_map.168 = (f32[272,1024]{1,0:T(8,128)}, f32[4,1024]{1,0:T(4,128)}, bf16[1024,1024]{1,0:T(8,128)(2,1)}, bf16[1024,1024]{1,0:T(8,128)(2,1)}) custom-call(f32[272,1024]{1,0:T(8,128)} %get-tuple-element.94.refs_0_, f32[272,1024]{1,0:T(8,128)} %get-tuple-element.95.refs_1_, f32[272,1024]{1,0:T(8,128)} %get-tuple-element.71.refs_0_.refs_2_, ...), custom_call_target="tpu_custom_call" | custom-call | flops 9126805504 | bytes 14286848 | tf_op jit(solution)/shard_map/pallas_call | solution.py:165
  580.7 47.4 %shard_map.169 = (f32[272,1024]{1,0:T(8,128)}, f32[4,1024]{1,0:T(4,128)}, bf16[3,1024,256]{2,1,0:T(8,128)(2,1)}, bf16[256,1024]{1,0:T(8,128)(2,1)}) custom-call(f32[272,1024]{1,0:T(8,128)} %get-tuple-element.101.refs_0_, f32[272,1024]{1,0:T(8,128)} %get-tuple-element.102.refs_1_, f32[272,1024]{1,0:T(8,128)} %get-tuple-element.68.refs_0_.refs_2_, ...), custom_call_target="tpu_custom_call" | custom-call | flops 4278190080 | bytes 10518528 | tf_op jit(solution)/shard_map/pallas_call | solution.py:165
  628.2 1.4 pad_maximum_fusion.refs_8_
  629.6 222.6 %shard_map.170 = (bf16[1024,1024]{1,0:T(8,128)(2,1)}, bf16[1024,1024]{1,0:T(8,128)(2,1)}, bf16[3,1024,256]{2,1,0:T(8,128)(2,1)}, bf16[256,1024]{1,0:T(8,128)(2,1...) custom-call(bf16[1024,1024]{1,0:T(8,128)(2,1)} %get-tuple-element.84, ...), custom_call_target="tpu_custom_call" | custom-call | flops 1048576 | bytes 14876672 | tf_op jit(solution)/shard_map/pallas_call | solution.py:165
  852.1 1.0 reshape.19
  853.2 0.6 copy_bitcast_fusion
  853.9 2.7 maximum_convert_fusion.3
  856.6 3.6 maximum_convert_fusion.2
  860.8 0.9 copy-done.2
  862.3 6.5 maximum_convert_fusion
  868.7 1.0 copy.27
  869.7 0.7 copy-done.6
  870.4 1.0 copy.28
  (23 shorter events, 1.9 us)
Async XLA Ops:
  0.6 459.0 %collective-permute-start = (bf16[272,1024]{1,0:T(8,128)(2,1)}, bf16[272,1024]{1,0:T(8,128)(2,1)S(1)}, u32[]{:S(2)}, u32[]{:S(2)}) collective-permute-start(bf16[272,1024]{1,0:T(8,128)(2,1)} %param.11), channel_id=1, source_target_pairs={{0,0},{2,4},{4,2},{6,6},{1,1},{3,5},{5,3},{7,7},{8,8},{10,12},{12,... | collective-permute-start | bytes 1671176 | tf_op jit(solution)/shard_map/ppermute | solution.py:1069
  580.7 47.5 %copy-start.8 = (f32[4,1024]{1,0:T(4,128)S(1)}, f32[4,1024]{1,0:T(4,128)}, u32[]{:S(2)}) copy-start(f32[4,1024]{1,0:T(4,128)} %get-tuple-element.112) | copy-start | bytes 49156
  580.7 47.5 %copy-start.9 = (f32[4,1024]{1,0:T(4,128)S(1)}, f32[4,1024]{1,0:T(4,128)}, u32[]{:S(2)}) copy-start(f32[4,1024]{1,0:T(4,128)} %get-tuple-element.111) | copy-start | bytes 49156
  580.7 47.5 %copy-start.10 = (f32[4,1024]{1,0:T(4,128)S(1)}, f32[4,1024]{1,0:T(4,128)}, u32[]{:S(2)}) copy-start(f32[4,1024]{1,0:T(4,128)} %get-tuple-element.110) | copy-start | bytes 49156
  852.1 4.4 copy-start.4
  852.1 4.4 copy-start.5
  856.5 3.6 copy-start
  856.5 4.2 copy-start.1
  856.5 5.1 copy-start.2
  856.6 5.7 copy-start.3
  862.3 6.5 copy-start.7
  868.7 1.6 copy-start.6

commit v4 on v3

--- a/solution.py
+++ b/solution.py
@@ -192,7 +192,7 @@
 
 
 def part_shape(shape, parts):
-    return (*shape[:-2], shape[-2] // parts, shape[-1])
+    return (*shape[:-2], int(shape[-2] / parts), shape[-1])
 
 
 def holds():
@@ -202,8 +202,8 @@
 class Fetching:
     copies = 4
 
-    def __init__(self, source, target, send, receive, local):
-        self.source, self.target, self.send, self.receive, self.local = source, target, send, receive, local
+    def __init__(self, source, target, send, receive):
+        self.source, self.target, self.send, self.receive = source, target, send, receive
         self.size = source.shape[-2] // 4
 
     def rows_of(self, names=()):
@@ -227,7 +227,6 @@
         @pl.when(holds())
         def _():
             self.along().start()
-            pltpu.make_async_copy(self.source, self.target, self.local.at[0]).start()
 
     def step_share(self):
         @pl.when(jnp.logical_not(holds()))
@@ -240,7 +239,6 @@
         @pl.when(holds())
         def _():
             self.along().wait_send()
-            pltpu.make_async_copy(self.source, self.target, self.local.at[0]).wait()
 
         @pl.when(jnp.logical_not(holds()))
         def _():
@@ -252,7 +250,7 @@
     return [
         Fetching(
             getattr(refs, name + "_from").at[layer], getattr(refs, name + "_to"), getattr(refs, name + "_send"),
-            getattr(refs, name + "_receive"), getattr(refs, name + "_local"),
+            getattr(refs, name + "_receive"),
         )
         for name in names
     ]
@@ -271,13 +269,229 @@
     for name in weights:
         result[name + "_send"] = semaphores(4)
         result[name + "_receive"] = semaphores(4)
-        result[name + "_local"] = semaphores(1)
     return result
+
+
+class Loading:
+    def __init__(self, own, fetched, target, semaphore):
+        self.ways = [pltpu.make_async_copy(source, target, semaphore) for source in (own, fetched)]
+
+    def start(self):
+        pl.when(holds())(self.ways[0].start)
+        pl.when(jnp.logical_not(holds()))(self.ways[1].start)
+
+    def wait(self):
+        pl.when(holds())(self.ways[0].wait)
+        pl.when(jnp.logical_not(holds()))(self.ways[1].wait)
 
 
 def every(jobs, step):
     for job in jobs:
         getattr(job, step)()
+
+
+ORDERS = (("p", "gl"), ("gl", "p"))
+
+
+class Halves:
+    def copy(self, slot, source, target, name):
+        return remote(source, target, self.send.at[slot], self.receive.at[slot], flipped(name))
+
+    def at(self, half, first, second=None):
+        start = (4 * half + 2 * first) * self.size
+        if second is None:
+            return pl.ds(pl.multiple_of(start, 16), 2 * self.size)
+        return pl.ds(pl.multiple_of(start + second * self.size, 16), self.size)
+
+
+class Scattering(Halves):
+    def __init__(self, source, out, land, mine, more, part, send, receive, local):
+        self.source, self.out = source, out
+        self.land, self.mine, self.more, self.part = land, mine, more, part
+        self.send, self.receive, self.local = send, receive, local
+        self.size = source.shape[-2] // 8
+
+    def spread(self, half):
+        name = ORDERS[half][0]
+        return self.copy(half, pick(self.source, self.at(half, 1 - lax.axis_index(name))), self.land.at[half], name)
+
+    def keep(self, half):
+        rows = self.at(half, lax.axis_index(ORDERS[half][0]))
+        return pltpu.make_async_copy(pick(self.source, rows), self.mine.at[half], self.local.at[half])
+
+    def second(self, index):
+        return pl.ds(pl.multiple_of(index * self.size, 16), self.size)
+
+    def fold(self, half):
+        name = ORDERS[half][1]
+        return self.copy(2 + half, pick(self.mine.at[half], self.second(1 - lax.axis_index(name))), self.more.at[half], name)
+
+    def store(self):
+        return pltpu.make_async_copy(self.part, self.out, self.local.at[2])
+
+    def step_spread(self):
+        for half in range(2):
+            self.spread(half).start()
+            self.keep(half).start()
+
+    def step_fold(self):
+        for half in range(2):
+            self.keep(half).wait()
+            self.spread(half).wait_recv()
+            self.mine[half] = (self.mine[half].astype(f32) + self.land[half].astype(f32)).astype(bf16)
+            self.fold(half).start()
+
+    def step_add(self):
+        for half in range(2):
+            self.fold(half).wait_recv()
+            own = pick(self.mine.at[half], self.second(lax.axis_index(ORDERS[half][1])))
+            total = own[...].astype(f32) + self.more[half].astype(f32)
+            pick(self.part, pl.ds(half * self.size, self.size))[...] = total.astype(bf16)
+        self.store().start()
+
+    def step_end(self):
+        for half in range(2):
+            self.spread(half).wait_send()
+            self.fold(half).wait_send()
+        self.store().wait()
+
+
+class Sharing(Halves):
+    def __init__(self, part, target, mine, cross, send, receive, local):
+        self.part, self.target, self.mine, self.cross = part, target, mine, cross
+        self.send, self.receive, self.local = send, receive, local
+        self.size = target.shape[-2] // 8
+
+    def place_of(self, half):
+        return [lax.axis_index(name) for name in ORDERS[half]]
+
+    def along(self):
+        return self.copy(0, self.part, self.cross, "zh")
+
+    def load(self):
+        return pltpu.make_async_copy(self.part, self.mine, self.local.at[0])
+
+    def place(self, half):
+        own = pick(self.target, self.at(half, *self.place_of(half)))
+        return pltpu.make_async_copy(self.own(half), own, self.local.at[1 + half])
+
+    def own(self, half):
+        return pick(self.mine, pl.ds(half * self.size, self.size))
+
+    def direct(self, half, axis):
+        own = pick(self.target, self.at(half, *self.place_of(half)))
+        return self.copy(1 + 2 * half + axis, self.own(half), own, ORDERS[half][axis])
+
+    def relay(self, half):
+        first, second = self.place_of(half)
+        rows = pick(self.target, self.at(half, first, 1 - second))
+        return self.copy(5 + half, rows, rows, ORDERS[half][0])
+
+    def mate(self, half, index):
+        first = self.place_of(half)[0]
+        rows = pick(self.target, self.at(half, first if index == 0 else 1 - first))
+        return self.copy(7 + 2 * half + index, rows, rows, "c")
+
+    def step_along(self):
+        pl.when(holds())(self.load().start)
+        pl.when(jnp.logical_not(holds()))(self.along().start)
+
+    def step_share(self):
+        @pl.when(holds())
+        def _():
+            self.load().wait()
+            self.along().wait_recv()
+            self.mine[...] = (self.mine[...].astype(f32) + self.cross[...].astype(f32)).astype(bf16)
+            for half in range(2):
+                self.direct(half, 1).start()
+                self.direct(half, 0).start()
+                self.place(half).start()
+
+    def step_relay(self):
+        @pl.when(holds())
+        def _():
+            for half in range(2):
+                self.direct(half, 1).wait_recv()
+                self.relay(half).start()
+                self.place(half).wait()
+                self.mate(half, 0).start()
+
+    def step_mate(self):
+        @pl.when(holds())
+        def _():
+            for half in range(2):
+                self.direct(half, 0).wait_recv()
+                self.relay(half).wait_recv()
+                self.mate(half, 1).start()
+
+    def step_end(self):
+        @pl.when(holds())
+        def _():
+            for half in range(2):
+                self.direct(half, 0).wait_send()
+                self.direct(half, 1).wait_send()
+                self.relay(half).wait_send()
+                self.mate(half, 0).wait_send()
+                self.mate(half, 1).wait_send()
+
+        @pl.when(jnp.logical_not(holds()))
+        def _():
+            self.along().wait_send()
+            for half in range(2):
+                self.mate(half, 0).wait_recv()
+                self.mate(half, 1).wait_recv()
+
+
+SPREAD = ("from", "part", "land", "mine", "more", "sum", "send", "receive", "local")
+SHARE = ("part", "to", "own", "cross", "along_send", "along_receive", "along_local")
+
+
+def scatter_jobs(refs, names):
+    return [Scattering(*[getattr(refs, f"{name}_{end}") for end in SPREAD]) for name in names]
+
+
+def scatter_inputs(grads):
+    return {name + "_from": (value, ANY) for name, value in grads.items()}
+
+
+def scatter_outputs(grads):
+    return {name + "_part": (part_shape(value.shape, 4), bf16, ANY) for name, value in grads.items()}
+
+
+def scatter_scratch(grads):
+    result = {}
+    for name, value in grads.items():
+        result[name + "_land"] = VMEM((2, *part_shape(value.shape, 4)), bf16)
+        result[name + "_mine"] = VMEM((2, *part_shape(value.shape, 4)), bf16)
+        result[name + "_more"] = VMEM((2, *part_shape(value.shape, 8)), bf16)
+        result[name + "_sum"] = VMEM(part_shape(value.shape, 4), bf16)
+        result[name + "_send"] = semaphores(4)
+        result[name + "_receive"] = semaphores(4)
+        result[name + "_local"] = semaphores(3)
+    return result
+
+
+def share_jobs(refs, names):
+    return [Sharing(*[getattr(refs, f"{name}_{end}") for end in SHARE]) for name in names]
+
+
+def share_inputs(parts):
+    return {name + "_part": (value, ANY) for name, value in parts.items()}
+
+
+def share_outputs(parts):
+    return {name + "_to": (part_shape(value.shape, 1 / 4), bf16, ANY) for name, value in parts.items()}
+
+
+def share_scratch(parts):
+    result = {}
+    for name, value in parts.items():
+        result[name + "_own"] = VMEM(value.shape, bf16)
+        result[name + "_cross"] = VMEM(value.shape, bf16)
+        result[name + "_along_send"] = semaphores(11)
+        result[name + "_along_receive"] = semaphores(11)
+        result[name + "_along_local"] = semaphores(3)
+    return result
 
 
 def head(hidden_in, weight, weights):
@@ -335,12 +549,12 @@
     return values * half, slope
 
 
-def ffn_forward(layer, middle, gains, shifts, w_up, w_down, weights):
+def ffn_forward(layer, middle, gains, shifts, w_up, w_down, own_up, own_down, weights):
     rows, width = middle.shape
     hidden = w_up.shape[1]
 
     def body(r):
-        loads = [pltpu.make_async_copy(r.w_up, r.up, r.local.at[0]), pltpu.make_async_copy(r.w_down, r.down, r.local.at[1])]
+        loads = [Loading(r.own_up.at[layer], r.w_up, r.up, r.local.at[0]), Loading(r.own_down.at[layer], r.w_down, r.down, r.local.at[1])]
         for copy in loads:
             copy.start()
         greet(*GROUP, *(FETCH if weights else ()))
@@ -391,7 +605,7 @@
         body,
         3 + layer,
         {
-            "middle": (middle, VMEM), "gains": (gains, VMEM), "shifts": (shifts, VMEM), "w_up": (w_up, ANY), "w_down": (w_down, ANY),
+            "middle": (middle, VMEM), "gains": (gains, VMEM), "shifts": (shifts, VMEM), "w_up": (w_up, ANY), "w_down": (w_down, ANY), "own_up": (own_up, ANY), "own_down": (own_down, ANY),
             **fetch_inputs(weights),
         },
         {
@@ -409,7 +623,7 @@
     )
 
 
-def ffn_backward(layer, grad, saved, gains, shifts, w_up, w_down):
+def ffn_backward(layer, grad, saved, gains, shifts, w_up, w_down, own_up, own_down, grads, parts):
     middle = saved.middle
     rows, width = middle.shape
     hidden = w_up.shape[1]
@@ -417,21 +631,30 @@
     def body(r):
         held, active, slope, pushed, past = r.held, r.active, r.slope, r.pushed, r.past
         loads = [
-            pltpu.make_async_copy(r.w_down, r.down, r.local.at[0]),
-            pltpu.make_async_copy(r.w_up, r.up, r.local.at[1]),
+            Loading(r.own_down.at[layer], r.w_down, r.down, r.local.at[0]),
+            Loading(r.own_up.at[layer], r.w_up, r.up, r.local.at[1]),
             pltpu.make_async_copy(r.slope_in, slope, r.local.at[2]),
             pltpu.make_async_copy(r.active_in, active, r.local.at[3]),
             pltpu.make_async_copy(r.held_in, past, r.local.at[4]),
         ]
         for copy in loads:
             copy.start()
-        greet(*GROUP)
+        greet(*GROUP, *(FETCH if grads or parts else ()))
+        jobs, shares = scatter_jobs(r, grads), share_jobs(r, parts)
+        every(jobs, "step_spread")
         pulled, gain_three, shift_three = norm_pull(r.second[...], r.gains[layer, 3:4, :], r.grad[...])
         held[pl.ds(0, rows), :] = pulled.astype(bf16)
         for copy in loads:
             copy.wait()
 
+        calls = []
+
         def work(start, size, sink):
+            calls.append(start)
+            if len(calls) == 1:
+                every(shares, "step_along")
+            if len(calls) == 4:
+                every(jobs, "step_fold")
             here = pl.ds(start, size)
 
             def step(columns):
@@ -447,12 +670,16 @@
 
         finish = exchange(rows, held, work, r.first, r.sums, r.send, r.receive)
 
+        every(shares, "step_share")
+
         def step_down(columns):
             r.outcome[0, columns, :] = dot_tn(active[:, columns], held[...]).astype(bf16)
 
         tiles(hidden, step_down)
         out_down = pltpu.make_async_copy(r.outcome.at[0], r.grad_down, r.local.at[0])
         out_down.start()
+        every(jobs, "step_add")
+        every(shares, "step_relay")
 
         def step_up(columns):
             r.outcome[1, columns, :] = dot_tn(past[:, columns], pushed[...]).astype(bf16)
@@ -460,6 +687,7 @@
         tiles(width, step_up)
         out_up = pltpu.make_async_copy(r.outcome.at[1], r.grad_up, r.local.at[1])
         out_up.start()
+        every(shares, "step_mate")
         finish()
         total = r.first[pl.ds(0, rows), :] + r.sums[1].astype(f32) + r.sums[5].astype(f32)
         pulled, gain_two, shift_two = norm_pull(r.middle[...], r.gains[layer, 2:3, :], total)
@@ -468,6 +696,7 @@
             r.norms[index : index + 1, :] = value
         out_down.wait()
         out_up.wait()
+        every(jobs + shares, "step_end")
 
     return run(
         body,
@@ -475,9 +704,11 @@
         {
             "grad": (grad, VMEM), "second": (saved.second, VMEM), "middle": (middle, VMEM), "gains": (gains, VMEM),
             "shifts": (shifts, VMEM), "held_in": (saved.held_out, ANY), "active_in": (saved.active_out, ANY),
-            "slope_in": (saved.slope_out, ANY), "w_up": (w_up, ANY), "w_down": (w_down, ANY),
-        },
-        {
+            "slope_in": (saved.slope_out, ANY), "w_up": (w_up, ANY), "w_down": (w_down, ANY), "own_up": (own_up, ANY), "own_down": (own_down, ANY),
+            **scatter_inputs(grads), **share_inputs(parts),
+        },
+        {
+            **scatter_outputs(grads), **share_outputs(parts),
             "grad_middle": ((rows, width), f32, VMEM), "norms": ((4, width), f32, VMEM),
             "grad_up": (w_up.shape, bf16, ANY), "grad_down": (w_down.shape, bf16, ANY),
         },
@@ -486,6 +717,7 @@
             "active": VMEM((4 * rows, hidden), bf16), "slope": VMEM((4 * rows, hidden), bf16),
             "pushed": VMEM((4 * rows, hidden), bf16), "up": VMEM(w_up.shape, bf16), "down": VMEM(w_down.shape, bf16),
             "outcome": VMEM((2, width, hidden), bf16), **group_scratch(rows, width), "local": semaphores(5),
+            **scatter_scratch(grads), **share_scratch(parts),
         },
         32 * rows * width * hidden,
     )
@@ -629,17 +861,17 @@
     lse[here, :] = tops
 
 
-def attention_forward(layer, stream, gains, shifts, w_qkv, w_out, weights):
+def attention_forward(layer, stream, gains, shifts, w_qkv, w_out, own_qkv, own_out, weights):
     rows, model = stream.shape
     width = w_out.shape[0]
 
     def body(r):
         held, qkv, attended, lse, weight = r.held, r.qkv, r.attended, r.lse, r.weight
         loads = [
-            pltpu.make_async_copy(r.w_qkv.at[index], weight.at[:, pl.ds(index * width, width)], r.local.at[index])
+            Loading(r.own_qkv.at[layer, index], r.w_qkv.at[index], weight.at[:, pl.ds(index * width, width)], r.local.at[index])
             for index in range(3)
         ]
-        loads.append(pltpu.make_async_copy(r.w_out, r.out, r.local.at[3]))
+        loads.append(Loading(r.own_out.at[layer], r.w_out, r.out, r.local.at[3]))
         for copy in loads:
             copy.start()
         greet(*GROUP, *(FETCH if weights else ()))
@@ -706,7 +938,7 @@
         body,
         1 + layer,
         {
-            "stream": (stream, VMEM), "gains": (gains, VMEM), "shifts": (shifts, VMEM), "w_qkv": (w_qkv, ANY), "w_out": (w_out, ANY),
+            "stream": (stream, VMEM), "gains": (gains, VMEM), "shifts": (shifts, VMEM), "w_qkv": (w_qkv, ANY), "w_out": (w_out, ANY), "own_qkv": (own_qkv, ANY), "own_out": (own_out, ANY),
             **fetch_inputs(weights),
         },
         {
@@ -754,7 +986,7 @@
         grad_query[here, columns] = (result * scale).astype(bf16)
 
 
-def attention_backward(layer, grad, stream, saved, gains, shifts, w_qkv, w_out):
+def attention_backward(layer, grad, stream, saved, gains, shifts, w_qkv, w_out, own_qkv, own_out, grads, parts):
     rows, model = stream.shape
     width = w_out.shape[0]
 
@@ -762,19 +994,21 @@
         held, past, qkv, attended, lse, inner, above = r.held, r.past, r.qkv, r.attended, r.lse, r.inner, r.above
         pushed, grad_key, grad_value, weight = r.pushed, r.grad_key, r.grad_value, r.weight
         loads = [
-            pltpu.make_async_copy(r.w_out, r.out, r.local.at[3]),
+            Loading(r.own_out.at[layer], r.w_out, r.out, r.local.at[3]),
             pltpu.make_async_copy(r.attended_in, attended, r.local.at[4]),
             pltpu.make_async_copy(r.qkv_in, qkv, r.local.at[5]),
             pltpu.make_async_copy(r.lse_in, lse, r.local.at[6]),
             *[
-                pltpu.make_async_copy(r.w_qkv.at[index], weight.at[:, pl.ds(index * width, width)], r.local.at[index])
+                Loading(r.own_qkv.at[layer, index], r.w_qkv.at[index], weight.at[:, pl.ds(index * width, width)], r.local.at[index])
                 for index in range(3)
             ],
             pltpu.make_async_copy(r.held_in, past, r.local.at[7]),
         ]
         for copy in loads:
             copy.start()
-        greet(*GROUP)
+        greet(*GROUP, *(FETCH if grads or parts else ()))
+        jobs, shares = scatter_jobs(r, grads), share_jobs(r, parts)
+        every(jobs, "step_spread")
         own = places(rows)[0]
         pulled, gain_one, shift_one = norm_pull(r.branch[...], r.gains[layer, 1:2, :], r.grad[...])
         held[pl.ds(own, rows), :] = pulled.astype(bf16)
@@ -806,12 +1040,18 @@
             inner[here, :] = tile
             blocks.append(size)
             if len(blocks) == 2:
+                every(shares, "step_along")
                 back(2 + zl, True)
                 back(zl, False)
 
         sent = gather(rows, held, arrived, r.send, r.receive)
+        every(jobs[:1], "step_fold")
         back(3 - zl, True)
+        every(shares, "step_share")
+        every(jobs[1:], "step_fold")
         back(1 - zl, False)
+        every(jobs[:1], "step_add")
+        every(shares, "step_relay")
         pushed[:, pl.ds(width, width)] = grad_key[...].astype(bf16)
         pushed[:, pl.ds(2 * width, width)] = grad_value[...].astype(bf16)
 
@@ -824,6 +1064,8 @@
             tiles(model, step)
 
         finish = scatter(rows, term, r.first, r.sums, r.send, r.receive)
+
+        every(jobs[1:], "step_add")
 
         def step_out(columns):
             r.outcome_out[:, columns] = dot_tn(attended[...], held[:, columns]).astype(bf16)
@@ -840,6 +1082,7 @@
             copy = pltpu.make_async_copy(r.outcome.at[:, pl.ds(index * width, width)], r.grad_qkv.at[index], r.local.at[1 + index])
             copy.start()
             outs.append(copy)
+        every(shares, "step_mate")
         finish()
         total = r.first[pl.ds(0, rows), :] + r.sums[1].astype(f32) + r.sums[5].astype(f32)
         pulled, gain_zero, shift_zero = norm_pull(r.stream[...], r.gains[layer, 0:1, :], total)
@@ -849,6 +1092,7 @@
         sent()
         for copy in outs:
             copy.wait()
+        every(jobs + shares, "step_end")
 
     return run(
         body,
@@ -856,9 +1100,11 @@
         {
             "grad": (grad, VMEM), "branch": (saved.branch, VMEM), "stream": (stream, VMEM), "gains": (gains, VMEM),
             "shifts": (shifts, VMEM), "held_in": (saved.held_out, ANY), "qkv_in": (saved.qkv_out, ANY),
-            "attended_in": (saved.attended_out, ANY), "lse_in": (saved.lse_out, ANY), "w_qkv": (w_qkv, ANY), "w_out": (w_out, ANY),
-        },
-        {
+            "attended_in": (saved.attended_out, ANY), "lse_in": (saved.lse_out, ANY), "w_qkv": (w_qkv, ANY), "w_out": (w_out, ANY), "own_qkv": (own_qkv, ANY), "own_out": (own_out, ANY),
+            **scatter_inputs(grads), **share_inputs(parts),
+        },
+        {
+            **scatter_outputs(grads), **share_outputs(parts),
             "grad_stream": ((rows, model), f32, VMEM), "norms": ((4, model), f32, VMEM),
             "grad_qkv": (w_qkv.shape, bf16, ANY), "grad_out": (w_out.shape, bf16, ANY),
         },
@@ -869,182 +1115,79 @@
             "grad_key": VMEM((4 * rows, width), f32), "grad_value": VMEM((4 * rows, width), f32),
             "weight": VMEM((model, 3 * width), bf16), "out": VMEM(w_out.shape, bf16), "outcome": VMEM((model, 3 * width), bf16),
             "outcome_out": VMEM(w_out.shape, bf16), **group_scratch(rows, model), "local": semaphores(8),
+            **scatter_scratch(grads), **share_scratch(parts),
         },
         60 * rows * model * width,
         64 * rows * rows,
     )
 
 
-SUM_COPIES = 11
-
-
-class Summing:
-    def __init__(self, source, target, land, mine, part, cross, send, receive, local):
-        self.source, self.target = source, target
-        self.land, self.mine, self.part, self.cross = land, mine, part, cross
-        self.send, self.receive, self.local = send, receive, local
-        self.size = source.shape[-2] // 4
-
-    def rows_of(self, names=()):
-        gl, p = [(1 - lax.axis_index(name)) if name in names else lax.axis_index(name) for name in ("gl", "p")]
-        return pl.ds(pl.multiple_of((2 * gl + p) * self.size, 16), self.size)
-
-    def copy(self, slot, source, target, device):
-        return remote(source, target, self.send.at[slot], self.receive.at[slot], device)
-
-    def spread(self):
-        return [
-            self.copy(slot, pick(self.source, self.rows_of(names)), self.land.at[slot], flipped(*names))
-            for slot, names in enumerate(ACROSS)
-        ]
-
-    def keep(self):
-        return pltpu.make_async_copy(pick(self.source, self.rows_of()), self.mine, self.local.at[0])
-
-    def along(self):
-        return self.copy(3, self.part, self.cross, flipped("zh"))
-
-    def place(self):
-        return pltpu.make_async_copy(self.part, pick(self.target, self.rows_of()), self.local.at[1])
-
-    def share(self):
-        own = pick(self.target, self.rows_of())
-        return [self.copy(4 + slot, self.part, own, flipped(*names)) for slot, names in enumerate((*ACROSS, ("c",)))]
-
-    def relays(self):
-        rows = [pick(self.target, self.rows_of(names)) for names in ACROSS]
-        return [self.copy(8 + slot, part, part, flipped("c")) for slot, part in enumerate(rows)]
-
-    def step_spread(self):
-        every(self.spread(), "start")
-        self.keep().start()
-
-    def step_add(self):
-        self.keep().wait()
-        every(self.spread(), "wait_recv")
-        total = self.mine[...].astype(f32)
-        for slot in range(3):
-            total = total + self.land[slot].astype(f32)
-        self.part[...] = total.astype(bf16)
-
-        @pl.when(jnp.logical_not(holds()))
-        def _():
-            self.along().start()
-
-    def step_share(self):
-        @pl.when(holds())
-        def _():
-            self.along().wait_recv()
-            self.part[...] = (self.part[...].astype(f32) + self.cross[...].astype(f32)).astype(bf16)
-            every(self.share(), "start")
-            self.place().start()
-
-    def step_relay(self):
-        @pl.when(holds())
-        def _():
-            for copy, relay in zip(self.share()[:3], self.relays()):
-                copy.wait_recv()
-                relay.start()
-
-    def step_end(self):
-        every(self.spread(), "wait_send")
-
-        @pl.when(holds())
-        def _():
-            every(self.share() + self.relays(), "wait_send")
-            self.place().wait()
-
-        @pl.when(jnp.logical_not(holds()))
-        def _():
-            self.along().wait_send()
-            every([self.share()[3]] + self.relays(), "wait_recv")
-
-
-def summing_scratch(name, shape):
-    part = part_shape(shape, 4)
-    return {
-        name + "_land": VMEM((3, *part), bf16),
-        name + "_mine": VMEM(part, bf16),
-        name + "_part": VMEM(part, bf16),
-        name + "_cross": VMEM(part, bf16),
-        name + "_send": semaphores(SUM_COPIES),
-        name + "_receive": semaphores(SUM_COPIES),
-        name + "_local": semaphores(2),
-    }
-
-
 CUBE = ("c", "zl", "p", "gl", "zh")
 
 
-def tail(grads, norms, mixed, grad_in):
+def tail(grads, parts, norms, grad_in):
     def body(r):
-        jobs = [
-            Summing(*[getattr(r, name + end) for end in ("_from", "_to", "_land", "_mine", "_part", "_cross", "_send", "_receive", "_local")])
-            for name in grads
-        ]
         greet(*GROUP, *FETCH, ("c", "zh"))
-        swaps = []
-        for index, (source, low, landed) in enumerate(((r.mixed, r.low_mixed, r.land_mixed), (r.grad_in, r.low_grad, r.land_grad))):
-            low[...] = source[...].astype(bf16)
-            swaps.append(remote(low, landed, r.send.at[index], r.receive.at[index], flipped("c", "zh")))
-
-        @pl.when(jnp.logical_not(holds()))
-        def _():
-            every(swaps, "start")
-
+        jobs = scatter_jobs(r, grads)
+        every(jobs, "step_spread")
+        shares = share_jobs(r, parts)
+        every(shares, "step_along")
+        swap = remote(r.low, r.landed, r.send.at[0], r.receive.at[0], flipped("c", "zh"))
+        r.low[...] = r.grad_in[...].astype(bf16)
+        pl.when(jnp.logical_not(holds()))(swap.start)
         total = r.norms[...]
         for index, name in enumerate(CUBE):
             r.norms_out[...] = total
-            copy = remote(r.norms_out, r.land.at[index], r.send.at[2 + index], r.receive.at[2 + index], flipped(name))
+            copy = remote(r.norms_out, r.land.at[index], r.send.at[1 + index], r.receive.at[1 + index], flipped(name))
             copy.start()
-            if index == 0:
-                every(jobs[:2], "step_spread")
             copy.wait()
             total = total + r.land[index]
         r.norms_out[...] = total
-        count = len(jobs)
-        for index in range(count + 3):
-            if index < count:
-                jobs[index].step_add()
-                every(jobs[index + 2 : index + 3], "step_spread")
-            if 0 <= index - 1 < count:
-                jobs[index - 1].step_share()
-            if 0 <= index - 2 < count:
-                jobs[index - 2].step_relay()
-            if 0 <= index - 3 < count:
-                jobs[index - 3].step_end()
+        every(jobs, "step_fold")
+        every(shares, "step_share")
+        every(jobs, "step_add")
+        every(shares, "step_relay")
+        last = [
+            Sharing(
+                getattr(r, name + "_sum"), getattr(r, name + "_to"),
+                *[getattr(r, f"{name}_{end}") for end in SHARE[2:]],
+            )
+            for name in grads
+        ]
+        every(last, "step_along")
+        every(shares, "step_mate")
+        every(last, "step_share")
+        every(last, "step_relay")
+        every(last, "step_mate")
 
         @pl.when(holds())
         def _():
-            r.mixed_out[...] = r.mixed[...]
             r.grad_out[...] = r.grad_in[...]
 
         @pl.when(jnp.logical_not(holds()))
         def _():
-            every(swaps, "wait")
-            r.mixed_out[...] = r.land_mixed[...].astype(f32)
-            r.grad_out[...] = r.land_grad[...].astype(f32)
-
-    scratch = {
-        "land": VMEM((len(CUBE), *norms.shape), f32),
-        "send": semaphores(2 + len(CUBE)),
-        "receive": semaphores(2 + len(CUBE)),
-        **{name: VMEM(mixed.shape, bf16) for name in ("low_mixed", "land_mixed", "low_grad", "land_grad")},
-    }
-    for name, value in grads.items():
-        scratch.update(summing_scratch(name, value.shape))
+            swap.wait()
+            r.grad_out[...] = r.landed[...].astype(f32)
+
+        every(jobs + shares + last, "step_end")
+
+    extra = {name: jax.ShapeDtypeStruct(part_shape(value.shape, 4), bf16) for name, value in grads.items()}
     return run(
         body,
         9,
-        {
-            **{name + "_from": (value, ANY) for name, value in grads.items()},
-            "norms": (norms, VMEM), "mixed": (mixed, VMEM), "grad_in": (grad_in, VMEM),
-        },
-        {
-            **{name + "_to": (value.shape, bf16, ANY) for name, value in grads.items()},
-            "norms_out": (norms.shape, f32, VMEM), "mixed_out": (mixed.shape, f32, VMEM), "grad_out": (mixed.shape, f32, VMEM),
-        },
-        scratch,
+        {**scatter_inputs(grads), **share_inputs(parts), "norms": (norms, VMEM), "grad_in": (grad_in, VMEM)},
+        {
+            **scatter_outputs(grads), **share_outputs(parts), **share_outputs(extra),
+            "norms_out": (norms.shape, f32, VMEM), "grad_out": (grad_in.shape, f32, VMEM),
+        },
+        {
+            "land": VMEM((len(CUBE), *norms.shape), f32),
+            "send": semaphores(1 + len(CUBE)),
+            "receive": semaphores(1 + len(CUBE)),
+            "low": VMEM(grad_in.shape, bf16),
+            "landed": VMEM(grad_in.shape, bf16),
+            **scatter_scratch(grads), **share_scratch(parts), **share_scratch(extra),
+        },
         1 << 20,
     )
 
@@ -1058,36 +1201,46 @@
     attentions, ffns = [], []
     for layer in range(layers):
         last = layer + 1 == layers
-        att = attention_forward(layer, stream, gains, shifts, qkv, out, {"up": w_up, "down": w_down})
-        ffn = ffn_forward(layer, att.middle, gains, shifts, att.up_to, att.down_to, {} if last else {"qkv": w_qkv, "out": w_out})
+        att = attention_forward(layer, stream, gains, shifts, qkv, out, w_qkv, w_out, {"up": w_up, "down": w_down})
+        ffn = ffn_forward(layer, att.middle, gains, shifts, att.up_to, att.down_to, w_up, w_down, {} if last else {"qkv": w_qkv, "out": w_out})
         ffn.middle = att.middle
         attentions.append((stream, att, qkv, out))
         ffns.append((ffn, att.up_to, att.down_to))
         stream = ffn.stream
         if not last:
             qkv, out = ffn.qkv_to, ffn.out_to
-    cotangent = lax.ppermute(cotangent, ("c", "zh"), ((0, 0), (1, 2), (2, 1), (3, 3)))
-    grad = cotangent.astype(f32) * start.scale[0, 0]
-    grads, norms = {}, [None] * layers
+    swap = functools.partial(lax.ppermute, axis_name=("c", "zh"), perm=((0, 0), (1, 2), (2, 1), (3, 3)))
+    grad = swap(cotangent).astype(f32) * start.scale[0, 0]
+    mixed = swap(stream.astype(bf16))
+    norms, done, grads, parts = [None] * layers, {}, {}, {}
+
+    def carry(result, names):
+        done.update({name: getattr(result, name + "_to") for name in parts})
+        following = {name: getattr(result, name + "_part") for name in grads}
+        return dict(names), following
+
     for layer in reversed(range(layers)):
-        back = ffn_backward(layer, grad, ffns[layer][0], gains, shifts, *ffns[layer][1:])
+        back = ffn_backward(layer, grad, ffns[layer][0], gains, shifts, *ffns[layer][1:], w_up, w_down, grads, parts)
+        grads, parts = carry(back, {f"up{layer}": back.grad_up, f"down{layer}": back.grad_down})
         before, att, qkv, out = attentions[layer]
-        deep = attention_backward(layer, back.grad_middle, before, att, gains, shifts, qkv, out)
+        deep = attention_backward(
+            layer, back.grad_middle, before, att, gains, shifts, qkv, out, w_qkv, w_out, grads, parts
+        )
+        grads, parts = carry(deep, {f"qkv{layer}": deep.grad_qkv, f"out{layer}": deep.grad_out})
         grad = deep.grad_stream
-        for name, value in (("up", back.grad_up), ("down", back.grad_down), ("qkv", deep.grad_qkv), ("out", deep.grad_out)):
-            grads[f"{name}{layer}"] = value
         norms[layer] = jnp.concatenate([deep.norms, back.norms])
-    total = tail(grads, jnp.concatenate(norms), stream, grad)
+    total = tail(grads, parts, jnp.concatenate(norms), grad)
+    done.update({name: getattr(total, name + "_to") for name in (*grads, *parts)})
 
     def stacked(name):
-        whole = jnp.stack([getattr(total, f"{name}{layer}_to") for layer in range(layers)]).astype(f32)
+        whole = jnp.stack([done[f"{name}{layer}"] for layer in range(layers)]).astype(f32)
         return lax.psum(whole, "gh") if lax.axis_size("gh") > 1 else whole
 
     sums = total.norms_out.reshape(layers, 4, 2, -1)
     if lax.axis_size("gh") > 1:
         sums = lax.psum(sums, "gh")
     return (
-        total.mixed_out, total.grad_out, stacked("qkv"), stacked("out"), stacked("up"), stacked("down"), sums[:, :, 0], sums[:, :, 1]
+        mixed.astype(f32), total.grad_out, stacked("qkv"), stacked("out"), stacked("up"), stacked("down"), sums[:, :, 0], sums[:, :, 1]
     )
 
 

time: 882 us -> 607 us (0.69)
  Pallas kernels: 842 us -> 567 us
    pallas_call x10, Pallas kernels: 842 us -> 567 us  [run(): pl.pallas_call(kernel, out_shape=tuple((jax.ShapeDtypeStruct(shape, kind)...]
  transfers between devices with their start and end apart: 1 -> 2, of which waited for: 0 -> 0; matrix products, arithmetic and copies ran while one was open for 0% -> 4% of each run, Pallas kernels for 52% -> 95%
where the time goes in v4:
time: 607 us; the launch traced here: 597 us
  Pallas kernels  567 us (93%)
  other arithmetic  19.6 us (3%)
    pallas_call x10, Pallas kernels, run(): pl.pallas_call(kernel, out_shape=tuple((jax.ShapeDtypeStruct(shape, kind)...  567 us
    convert_element_type x3, other arithmetic, stacked(): jnp.stack([done[f'{name}{layer}'] for layer in range(layers)]).astype(f32)  12.7 us
  transfers between devices with their start and end apart: 2, of which 0 were waited for; matrix products, arithmetic and copies ran while one was open for 4% of the time, Pallas kernels for 95%

profile of v4, /device:TPU:0, one launch (start us, length us, event | category | flops | bytes accessed | tf_op | source)
XLA Modules:
  0.0 597.1 jit_solution(18206261361193345196)
XLA Ops:
  0.6 1.7 collective-permute-start.1
  3.0 1.3 fusion
  5.6 19.3 %shard_map.161 = (f32[272,1024]{1,0:T(8,128)}, f32[8,128]{1,0:T(8,128)}, bf16[3,1024,256]{2,1,0:T(8,128)(2,1)}, bf16[256,1024]{1,0:T(8,128)(2,1)}) custom-call(bf16[272,1024]{1,0:T(8,128)(2,1)} %refs_0_.1, f32[8,128]{1,0:T(8,128)} %broadcast_in_dim.8.refs_1_, bf16[2,3,1024,256]{3,2,1,0:T(8,128)(2,1)} %refs_11_.7, bf16[2,256,1024]{2,1,0:T(8,128)(2,1)} %refs_12_.3), custom_call_target="tpu_custom_call" | custom-call | flops 1048576 | bytes 4755456 | tf_op jit(solution)/shard_map/pallas_call | solution.py:165
  24.9 77.7 %shard_map.162 = (f32[272,1024]{1,0:T(8,128)}, f32[272,1024]{1,0:T(8,128)}, bf16[1088,1024]{1,0:T(8,128)(2,1)}, bf16[1088,768]{1,0:T(8,128)(2,1)}, bf16[1088,256...) custom-call(f32[272,1024]{1,0:T(8,128)} %get-tuple-element.72.refs_0_.refs_2_, ...), custom_call_target="tpu_custom_call" | custom-call | flops 1711276032 | bytes 15859712 | tf_op jit(solution)/shard_map/pallas_call | solution.py:165
  102.6 47.7 %shard_map.163 = (f32[272,1024]{1,0:T(8,128)}, f32[272,1024]{1,0:T(8,128)}, bf16[1088,1024]{1,0:T(8,128)(2,1)}, bf16[1088,1024]{1,0:T(8,128)(2,1)}, bf16[1088,10...) custom-call(f32[272,1024]{1,0:T(8,128)} %get-tuple-element.75.refs_0_.refs_2_, ...), custom_call_target="tpu_custom_call" | custom-call | flops 4563402752 | bytes 17956864 | tf_op jit(solution)/shard_map/pallas_call | solution.py:165
  150.3 59.9 %shard_map.164 = (f32[272,1024]{1,0:T(8,128)}, f32[272,1024]{1,0:T(8,128)}, bf16[1088,1024]{1,0:T(8,128)(2,1)}, bf16[1088,768]{1,0:T(8,128)(2,1)}, bf16[1088,256...) custom-call(f32[272,1024]{1,0:T(8,128)} %get-tuple-element.78.refs_0_.refs_2_, ...), custom_call_target="tpu_custom_call" | custom-call | flops 1711276032 | bytes 15859712 | tf_op jit(solution)/shard_map/pallas_call | solution.py:165
  210.2 55.8 %shard_map.165 = (f32[272,1024]{1,0:T(8,128)}, f32[272,1024]{1,0:T(8,128)}, bf16[1088,1024]{1,0:T(8,128)(2,1)}, bf16[1088,1024]{1,0:T(8,128)(2,1)}, bf16[1088,1024]{1,0:T(8,128)(2,1)}) custom-call(f32[272,1024]{1,0:T(8,128)} %get-tuple-element.81.refs_0_.refs_2_, f32[2,4,1024]{2,1,0:T(4,128)} %refs_3_.9, f32[2,4,1024]{2,1,0:T(4,128)} %refs_4_.7, ...), custom_call_target="tpu_custom_call" | custom-call | flops 4563402752 | bytes 13762560 | tf_op jit(solution)/shard_map/pallas_call | solution.py:165
  266.0 1.3 convert_element_type.25
  267.3 0.7 collective-permute-start
  268.0 1.2 slice.9
  269.2 1.8 convert_multiply_fusion.refs_0_
  271.0 40.7 %shard_map.166 = (f32[272,1024]{1,0:T(8,128)}, f32[4,1024]{1,0:T(4,128)}, bf16[1024,1024]{1,0:T(8,128)(2,1)}, bf16[1024,1024]{1,0:T(8,128)(2,1)}) custom-call(f32[272,1024]{1,0:T(8,128)} %convert_multiply_fusion.refs_0_, f32[272,1024]{1,0:T(8,128)} %get-tuple-element.86.refs_1_, f32[272,1024]{1,0:T(8,128)} %get-tuple-element.81.refs_0_.refs_2_, ...), custom_call_target="tpu_custom_call" | custom-call | flops 9126805504 | bytes 22675456 | tf_op jit(solution)/shard_map/pallas_call | solution.py:165
  311.7 55.5 %shard_map.167 = (bf16[256,1024]{1,0:T(8,128)(2,1)}, bf16[256,1024]{1,0:T(8,128)(2,1)}, f32[272,1024]{1,0:T(8,128)}, f32[4,1024]{1,0:T(4,128)}, bf16[3,1024,256]...) custom-call(f32[272,1024]{1,0:T(8,128)} %get-tuple-element.90.refs_0_, f32[272,1024]{1,0:T(8,128)} %get-tuple-element.91.refs_1_, ...), custom_call_target="tpu_custom_call" | custom-call | flops 4278190080 | bytes 18907136 | tf_op jit(solution)/shard_map/pallas_call | solution.py:165
  367.2 59.9 %shard_map.168 = (bf16[3,256,256]{2,1,0:T(8,128)(2,1)}, bf16[64,1024]{1,0:T(8,128)(2,1)}, bf16[1024,1024]{1,0:T(8,128)(2,1)}, bf16[1024,1024]{1,0:T(8,128)(2,1)}...) custom-call(f32[272,1024]{1,0:T(8,128)} %get-tuple-element.98.refs_0_, ...), custom_call_target="tpu_custom_call" | custom-call | flops 9126805504 | bytes 25821184 | tf_op jit(solution)/shard_map/pallas_call | solution.py:165
  427.1 62.0 %shard_map.169 = (bf16[256,1024]{1,0:T(8,128)(2,1)}, bf16[256,1024]{1,0:T(8,128)(2,1)}, bf16[3,1024,256]{2,1,0:T(8,128)(2,1)}, bf16[256,1024]{1,0:T(8,128)(2,1)}...) custom-call(f32[272,1024]{1,0:T(8,128)} %get-tuple-element.107.refs_0_, ...), custom_call_target="tpu_custom_call" | custom-call | flops 4278190080 | bytes 19431424 | tf_op jit(solution)/shard_map/pallas_call | solution.py:165
  489.2 1.4 pad_maximum_fusion.refs_4_
  490.6 88.1 %shard_map.170 = (bf16[3,256,256]{2,1,0:T(8,128)(2,1)}, bf16[64,1024]{1,0:T(8,128)(2,1)}, bf16[1024,1024]{1,0:T(8,128)(2,1)}, bf16[1024,1024]{1,0:T(8,128)(2,1)}...) custom-call(bf16[3,1024,256]{2,1,0:T(8,128)(2,1)} %get-tuple-element.117., ...), custom_call_target="tpu_custom_call" | custom-call | flops 1048576 | bytes 4325376 | tf_op jit(solution)/shard_map/pallas_call | solution.py:165
  578.7 0.9 reshape.19
  580.3 4.8 maximum_convert_fusion.2
  585.1 1.5 maximum_convert_fusion.3
  586.6 1.0 copy-done
  587.6 6.5 %maximum_convert_fusion = (f32[2,1024,1024]{2,1,0:T(8,128)}, f32[2,1024,1024]{2,1,0:T(8,128)}) fusion(bf16[1,1024,1024]{2,1,0:T(8,128)(2,1)S(1)} %bitcast.15, bf16[1,1024,1024]{2,1,0:T(8,128)(2,1)S(1)} %bitcast.17, bf16[1,1024,1024]{2,1,0:T(8,128)(2,1)S(1)} %bitcast.16, bf16[1,1024,1024]{2,1,0:T(8,128)(2,1)S(1)} %bitcast.18), kind=kLoop, calls=%fused_computation | loop fusion | flops 8388608 | bytes 25165824 | tf_op jit(solution)/shard_map/convert_element_type | solution.py:1236
  594.0 1.1 convert_element_type.26
  595.7 1.0 copy.26
  (26 shorter events, 1.9 us)
Async XLA Ops:
  0.6 268.6 %collective-permute-start.1 = (bf16[272,1024]{1,0:T(8,128)(2,1)}, bf16[272,1024]{1,0:T(8,128)(2,1)S(1)}, u32[]{:S(2)}, u32[]{:S(2)}) collective-permute-start(bf16[272,1024]{1,0:T(8,128)(2,1)} %param.11), channel_id=1, source_target_pairs={{0,0},{2,4},{4,2},{6,6},{1,1},{3,5},{5,3},{7,7},{8,8},{10,12},{12,... | collective-permute-start | bytes 1671176 | tf_op jit(solution)/shard_map/ppermute | solution.py:1213
  267.3 326.7 %collective-permute-start = (bf16[272,1024]{1,0:T(8,128)(2,1)S(1)}, bf16[272,1024]{1,0:T(8,128)(2,1)S(1)}, u32[]{:S(2)}, u32[]{:S(2)}) collective-permute-start(bf16[272,1024]{1,0:T(8,128)(2,1)S(1)} %convert_element_type.25), channel_id=1, source_target_pairs={{0,0},{2,4},{4,2},{6,6},{1,1},{3,5},{5,3},{7,7},{8,8},{10,12},{12,... | collective-permute-start | bytes 1671176 | tf_op jit(solution)/shard_map/ppermute | solution.py:1214
  427.1 62.1 %copy-start.8 = (f32[4,1024]{1,0:T(4,128)S(1)}, f32[4,1024]{1,0:T(4,128)}, u32[]{:S(2)}) copy-start(f32[4,1024]{1,0:T(4,128)} %get-tuple-element.124) | copy-start | bytes 49156
  427.1 62.1 %copy-start.9 = (f32[4,1024]{1,0:T(4,128)S(1)}, f32[4,1024]{1,0:T(4,128)}, u32[]{:S(2)}) copy-start(f32[4,1024]{1,0:T(4,128)} %get-tuple-element.123) | copy-start | bytes 49156
  427.1 62.1 %copy-start.10 = (f32[4,1024]{1,0:T(4,128)S(1)}, f32[4,1024]{1,0:T(4,128)}, u32[]{:S(2)}) copy-start(f32[4,1024]{1,0:T(4,128)} %get-tuple-element.122) | copy-start | bytes 49156
  490.6 89.7 %copy-start.4 = (bf16[3,1024,256]{2,1,0:T(8,128)(2,1)S(1)}, bf16[3,1024,256]{2,1,0:T(8,128)(2,1)}, u32[]{:S(2)}) copy-start(bf16[3,1024,256]{2,1,0:T(8,128)(2,1)} %get-tuple-element.128) | copy-start | bytes 4718596
  580.3 4.9 copy-start.6
  580.3 4.9 copy-start.7
  580.3 6.3 %copy-start.1 = (bf16[1024,1024]{1,0:T(8,128)(2,1)S(1)}, bf16[1024,1024]{1,0:T(8,128)(2,1)}, u32[]{:S(2)}) copy-start(bf16[1024,1024]{1,0:T(8,128)(2,1)} %get-tuple-element.134) | copy-start | bytes 6291460
  580.3 6.3 %copy-start.2 = (bf16[1024,1024]{1,0:T(8,128)(2,1)S(1)}, bf16[1024,1024]{1,0:T(8,128)(2,1)}, u32[]{:S(2)}) copy-start(bf16[1024,1024]{1,0:T(8,128)(2,1)} %get-tuple-element.131) | copy-start | bytes 6291460
  580.3 6.3 %copy-start.3 = (bf16[1024,1024]{1,0:T(8,128)(2,1)S(1)}, bf16[1024,1024]{1,0:T(8,128)(2,1)}, u32[]{:S(2)}) copy-start(bf16[1024,1024]{1,0:T(8,128)(2,1)} %get-tuple-element.133) | copy-start | bytes 6291460
  585.1 2.4 copy-start
  594.0 1.6 copy-start.5

commit v5 on v4

--- a/solution.py
+++ b/solution.py
@@ -71,8 +71,7 @@
 
 
 GROUP = (("c",), ("zl",))
-ACROSS = (("p",), ("gl",), ("gl", "p"))
-FETCH = (("zh",), *ACROSS)
+FETCH = (("zh",), ("p",), ("gl",))
 
 
 def remote(source, target, send, receive, device):
@@ -195,55 +194,12 @@
     return (*shape[:-2], int(shape[-2] / parts), shape[-1])
 
 
+def inner():
+    return lax.axis_index("zl") != lax.axis_index("zh")
+
+
 def holds():
     return lax.axis_index("c") == lax.axis_index("zh")
-
-
-class Fetching:
-    copies = 4
-
-    def __init__(self, source, target, send, receive):
-        self.source, self.target, self.send, self.receive = source, target, send, receive
-        self.size = source.shape[-2] // 4
-
-    def rows_of(self, names=()):
-        gl, p = [(1 - lax.axis_index(name)) if name in names else lax.axis_index(name) for name in ("gl", "p")]
-        return pl.ds(pl.multiple_of((2 * gl + p) * self.size, 16), self.size)
-
-    def along(self):
-        rows = self.rows_of()
-        return remote(
-            pick(self.source, rows), pick(self.target, rows), self.send.at[0], self.receive.at[0], flipped("zh")
-        )
-
-    def share(self):
-        rows = pick(self.target, self.rows_of())
-        return [
-            remote(rows, rows, self.send.at[1 + slot], self.receive.at[1 + slot], flipped(*names))
-            for slot, names in enumerate(ACROSS)
-        ]
-
-    def step_along(self):
-        @pl.when(holds())
-        def _():
-            self.along().start()
-
-    def step_share(self):
-        @pl.when(jnp.logical_not(holds()))
-        def _():
-            self.along().wait_recv()
-            for copy in self.share():
-                copy.start()
-
-    def step_end(self):
-        @pl.when(holds())
-        def _():
-            self.along().wait_send()
-
-        @pl.when(jnp.logical_not(holds()))
-        def _():
-            for copy in self.share():
-                copy.wait()
 
 
 def fetch_jobs(refs, names, layer):
@@ -267,8 +223,8 @@
 def fetch_scratch(weights):
     result = {}
     for name in weights:
-        result[name + "_send"] = semaphores(4)
-        result[name + "_receive"] = semaphores(4)
+        result[name + "_send"] = semaphores(8)
+        result[name + "_receive"] = semaphores(8)
     return result
 
 
@@ -290,6 +246,7 @@
         getattr(job, step)()
 
 
+CUBE = ("c", "zl", "p", "gl", "zh")
 ORDERS = (("p", "gl"), ("gl", "p"))
 
 
@@ -304,12 +261,77 @@
         return pl.ds(pl.multiple_of(start + second * self.size, 16), self.size)
 
 
-class Scattering(Halves):
-    def __init__(self, source, out, land, mine, more, part, send, receive, local):
-        self.source, self.out = source, out
-        self.land, self.mine, self.more, self.part = land, mine, more, part
-        self.send, self.receive, self.local = send, receive, local
+class Fetching(Halves):
+    def __init__(self, source, target, send, receive):
+        self.source, self.target, self.send, self.receive = source, target, send, receive
         self.size = source.shape[-2] // 8
+
+    def own(self, half):
+        return self.at(half, *[lax.axis_index(name) for name in ORDERS[half]])
+
+    def along(self, half):
+        return self.copy(half, pick(self.source, self.own(half)), pick(self.target, self.own(half)), "zh")
+
+    def direct(self, half, axis):
+        rows = pick(self.target, self.own(half))
+        return self.copy(2 + 2 * half + axis, rows, rows, ORDERS[half][axis])
+
+    def relay(self, half):
+        first, second = ORDERS[half]
+        rows = pick(self.target, self.at(half, lax.axis_index(first), 1 - lax.axis_index(second)))
+        return self.copy(6 + half, rows, rows, first)
+
+    def start_along(self, here):
+        @pl.when(jnp.logical_and(holds(), here))
+        def _():
+            for half in range(2):
+                self.along(half).start()
+
+    def step_inner(self):
+        self.start_along(inner())
+
+    def step_outer(self):
+        self.start_along(jnp.logical_not(inner()))
+
+    def step_share(self):
+        @pl.when(jnp.logical_not(holds()))
+        def _():
+            for half in range(2):
+                self.along(half).wait_recv()
+                self.direct(half, 1).start()
+                self.direct(half, 0).start()
+
+    def step_relay(self):
+        @pl.when(jnp.logical_not(holds()))
+        def _():
+            for half in range(2):
+                self.direct(half, 1).wait_recv()
+                self.relay(half).start()
+
+    def step_end(self):
+        @pl.when(holds())
+        def _():
+            for half in range(2):
+                self.along(half).wait_send()
+
+        @pl.when(jnp.logical_not(holds()))
+        def _():
+            for half in range(2):
+                self.direct(half, 0).wait()
+                self.direct(half, 1).wait_send()
+                self.relay(half).wait()
+
+
+class Passing(Halves):
+    def __init__(self, refs, name, first, last, source=None):
+        self.first, self.last = first, last
+        for field in ("in", "out", "land", "mine", "more", "sum", "cross", "send", "receive", "local"):
+            setattr(self, field, getattr(refs, f"{name}_{field}", None))
+        self.source = source if source is not None else getattr(refs, f"{name}_in", None)
+        self.size = self.sum.shape[-2] // 2
+
+    def place_of(self, half):
+        return [lax.axis_index(name) for name in ORDERS[half]]
 
     def spread(self, half):
         name = ORDERS[half][0]
@@ -326,8 +348,34 @@
         name = ORDERS[half][1]
         return self.copy(2 + half, pick(self.mine.at[half], self.second(1 - lax.axis_index(name))), self.more.at[half], name)
 
+    def load(self):
+        return pltpu.make_async_copy(self.source, self.sum, self.local.at[2])
+
     def store(self):
-        return pltpu.make_async_copy(self.part, self.out, self.local.at[2])
+        return pltpu.make_async_copy(self.sum, self.out, self.local.at[2])
+
+    def along(self):
+        return self.copy(4, self.sum, self.cross, "zh")
+
+    def own(self, half):
+        return pick(self.sum, pl.ds(half * self.size, self.size))
+
+    def place(self, half):
+        return pltpu.make_async_copy(self.own(half), pick(self.out, self.at(half, *self.place_of(half))), self.local.at[half])
+
+    def direct(self, half, axis):
+        own = pick(self.out, self.at(half, *self.place_of(half)))
+        return self.copy(5 + 2 * half + axis, self.own(half), own, ORDERS[half][axis])
+
+    def relay(self, half):
+        first, second = self.place_of(half)
+        rows = pick(self.out, self.at(half, first, 1 - second))
+        return self.copy(9 + half, rows, rows, ORDERS[half][0])
+
+    def mate(self, half, index):
+        first = self.place_of(half)[0]
+        rows = pick(self.out, self.at(half, first if index == 0 else 1 - first))
+        return self.copy(11 + 2 * half + index, rows, rows, "c")
 
     def step_spread(self):
         for half in range(2):
@@ -345,63 +393,29 @@
         for half in range(2):
             self.fold(half).wait_recv()
             own = pick(self.mine.at[half], self.second(lax.axis_index(ORDERS[half][1])))
-            total = own[...].astype(f32) + self.more[half].astype(f32)
-            pick(self.part, pl.ds(half * self.size, self.size))[...] = total.astype(bf16)
-        self.store().start()
-
-    def step_end(self):
-        for half in range(2):
-            self.spread(half).wait_send()
-            self.fold(half).wait_send()
-        self.store().wait()
-
-
-class Sharing(Halves):
-    def __init__(self, part, target, mine, cross, send, receive, local):
-        self.part, self.target, self.mine, self.cross = part, target, mine, cross
-        self.send, self.receive, self.local = send, receive, local
-        self.size = target.shape[-2] // 8
-
-    def place_of(self, half):
-        return [lax.axis_index(name) for name in ORDERS[half]]
-
-    def along(self):
-        return self.copy(0, self.part, self.cross, "zh")
-
-    def load(self):
-        return pltpu.make_async_copy(self.part, self.mine, self.local.at[0])
-
-    def place(self, half):
-        own = pick(self.target, self.at(half, *self.place_of(half)))
-        return pltpu.make_async_copy(self.own(half), own, self.local.at[1 + half])
-
-    def own(self, half):
-        return pick(self.mine, pl.ds(half * self.size, self.size))
-
-    def direct(self, half, axis):
-        own = pick(self.target, self.at(half, *self.place_of(half)))
-        return self.copy(1 + 2 * half + axis, self.own(half), own, ORDERS[half][axis])
-
-    def relay(self, half):
-        first, second = self.place_of(half)
-        rows = pick(self.target, self.at(half, first, 1 - second))
-        return self.copy(5 + half, rows, rows, ORDERS[half][0])
-
-    def mate(self, half, index):
-        first = self.place_of(half)[0]
-        rows = pick(self.target, self.at(half, first if index == 0 else 1 - first))
-        return self.copy(7 + 2 * half + index, rows, rows, "c")
-
-    def step_along(self):
-        pl.when(holds())(self.load().start)
-        pl.when(jnp.logical_not(holds()))(self.along().start)
+            self.own(half)[...] = (own[...].astype(f32) + self.more[half].astype(f32)).astype(bf16)
+
+    def step_load(self):
+        self.load().start()
+
+    def step_loaded(self):
+        self.load().wait()
+
+    def step_inner(self):
+        pl.when(jnp.logical_and(jnp.logical_not(holds()), inner()))(self.along().start)
+
+    def step_outer(self):
+        pl.when(jnp.logical_not(jnp.logical_or(holds(), inner())))(self.along().start)
+
+    def step_join(self):
+        @pl.when(holds())
+        def _():
+            self.along().wait_recv()
+            self.sum[...] = (self.sum[...].astype(f32) + self.cross[...].astype(f32)).astype(bf16)
 
     def step_share(self):
         @pl.when(holds())
         def _():
-            self.load().wait()
-            self.along().wait_recv()
-            self.mine[...] = (self.mine[...].astype(f32) + self.cross[...].astype(f32)).astype(bf16)
             for half in range(2):
                 self.direct(half, 1).start()
                 self.direct(half, 0).start()
@@ -424,120 +438,104 @@
                 self.relay(half).wait_recv()
                 self.mate(half, 1).start()
 
+    def step_store(self):
+        self.store().start()
+
     def step_end(self):
+        if self.first == 0:
+            for half in range(2):
+                self.spread(half).wait_send()
+                self.fold(half).wait_send()
+        if self.last < 2:
+            self.store().wait()
+
         @pl.when(holds())
         def _():
-            for half in range(2):
-                self.direct(half, 0).wait_send()
-                self.direct(half, 1).wait_send()
-                self.relay(half).wait_send()
-                self.mate(half, 0).wait_send()
-                self.mate(half, 1).wait_send()
+            if self.last == 2:
+                for half in range(2):
+                    self.direct(half, 0).wait_send()
+                    self.direct(half, 1).wait_send()
+                    self.relay(half).wait_send()
+                    self.mate(half, 0).wait_send()
+                    self.mate(half, 1).wait_send()
 
         @pl.when(jnp.logical_not(holds()))
         def _():
-            self.along().wait_send()
-            for half in range(2):
-                self.mate(half, 0).wait_recv()
-                self.mate(half, 1).wait_recv()
-
-
-SPREAD = ("from", "part", "land", "mine", "more", "sum", "send", "receive", "local")
-SHARE = ("part", "to", "own", "cross", "along_send", "along_receive", "along_local")
-
-
-def scatter_jobs(refs, names):
-    return [Scattering(*[getattr(refs, f"{name}_{end}") for end in SPREAD]) for name in names]
-
-
-def scatter_inputs(grads):
-    return {name + "_from": (value, ANY) for name, value in grads.items()}
-
-
-def scatter_outputs(grads):
-    return {name + "_part": (part_shape(value.shape, 4), bf16, ANY) for name, value in grads.items()}
-
-
-def scatter_scratch(grads):
+            if self.first <= 1 <= self.last:
+                self.along().wait_send()
+            if self.last == 2:
+                for half in range(2):
+                    self.mate(half, 0).wait_recv()
+                    self.mate(half, 1).wait_recv()
+
+
+def pass_shapes(grads):
+    for name, (value, first, last) in grads.items():
+        whole = value.shape if first == 0 else part_shape(value.shape, 1 / 4)
+        yield name, whole, part_shape(whole, 4), first, last
+
+
+def pass_jobs(refs, grads, sources=None):
+    return {name: Passing(refs, name, first, last, (sources or {}).get(name)) for name, (_, first, last) in grads.items()}
+
+
+def pass_inputs(grads):
+    return {name + "_in": (value, ANY) for name, (value, *_) in grads.items() if isinstance(value, jax.Array)}
+
+
+def pass_outputs(grads):
+    return {name + "_out": (whole if last == 2 else part, bf16, ANY) for name, whole, part, first, last in pass_shapes(grads)}
+
+
+def pass_scratch(grads):
     result = {}
-    for name, value in grads.items():
-        result[name + "_land"] = VMEM((2, *part_shape(value.shape, 4)), bf16)
-        result[name + "_mine"] = VMEM((2, *part_shape(value.shape, 4)), bf16)
-        result[name + "_more"] = VMEM((2, *part_shape(value.shape, 8)), bf16)
-        result[name + "_sum"] = VMEM(part_shape(value.shape, 4), bf16)
-        result[name + "_send"] = semaphores(4)
-        result[name + "_receive"] = semaphores(4)
+    for name, whole, part, first, last in pass_shapes(grads):
+        if first == 0:
+            result[name + "_land"] = VMEM((2, *part), bf16)
+            result[name + "_mine"] = VMEM((2, *part), bf16)
+            result[name + "_more"] = VMEM((2, *part_shape(whole, 8)), bf16)
+        result[name + "_sum"] = VMEM(part, bf16)
+        if first <= 1 <= last:
+            result[name + "_cross"] = VMEM(part, bf16)
+        result[name + "_send"] = semaphores(15)
+        result[name + "_receive"] = semaphores(15)
         result[name + "_local"] = semaphores(3)
     return result
 
 
-def share_jobs(refs, names):
-    return [Sharing(*[getattr(refs, f"{name}_{end}") for end in SHARE]) for name in names]
-
-
-def share_inputs(parts):
-    return {name + "_part": (value, ANY) for name, value in parts.items()}
-
-
-def share_outputs(parts):
-    return {name + "_to": (part_shape(value.shape, 1 / 4), bf16, ANY) for name, value in parts.items()}
-
-
-def share_scratch(parts):
-    result = {}
-    for name, value in parts.items():
-        result[name + "_own"] = VMEM(value.shape, bf16)
-        result[name + "_cross"] = VMEM(value.shape, bf16)
-        result[name + "_along_send"] = semaphores(11)
-        result[name + "_along_receive"] = semaphores(11)
-        result[name + "_along_local"] = semaphores(3)
-    return result
-
-
-def head(hidden_in, weight, weights):
-    def body(r):
-        greet(("c",), ("c", "zh"), *FETCH)
-        jobs = fetch_jobs(r, weights, 0)
-        jobs[0].step_along()
-        swap = remote(r.hidden, r.landed, r.send.at[0], r.receive.at[0], flipped("c", "zh"))
-        scale = remote(r.weight, r.other, r.send.at[1], r.receive.at[1], flipped("c"))
-        scale.start()
+def every_of(jobs, names, *steps):
+    for step in steps:
+        for name in names:
+            getattr(jobs[name], step)()
+
+
+class Swapping:
+    def __init__(self, source, landed, send, receive):
+        self.landed = landed
+        self.copy = remote(source, landed, send, receive, flipped("c", "zh"))
+
+    def start(self):
+        pl.when(jnp.logical_not(holds()))(self.copy.start)
+
+    def step_inner(self):
+        pl.when(jnp.logical_and(jnp.logical_not(holds()), inner()))(self.copy.start)
+
+    def step_outer(self):
+        pl.when(jnp.logical_not(jnp.logical_or(holds(), inner())))(self.copy.start)
+
+    def wait(self):
+        pl.when(jnp.logical_not(holds()))(self.copy.wait)
+
+    def give(self, target, own, scale=None):
+        factor = 1.0 if scale is None else scale
+
+        @pl.when(holds())
+        def _():
+            target[...] = own[...].astype(f32) * factor
 
         @pl.when(jnp.logical_not(holds()))
         def _():
-            swap.start()
-
-        every(jobs[1:], "step_along")
-        every(jobs, "step_share")
-
-        @pl.when(holds())
-        def _():
-            r.stream[...] = r.hidden[...].astype(f32)
-
-        scale.wait()
-        r.scale[...] = jnp.where(holds(), r.weight[...], r.other[...])
-
-        @pl.when(jnp.logical_not(holds()))
-        def _():
-            swap.wait()
-            r.stream[...] = r.landed[...].astype(f32)
-
-        every(jobs, "step_end")
-
-    return run(
-        body,
-        0,
-        {"hidden": (hidden_in, VMEM), "weight": (weight, VMEM), **fetch_inputs(weights)},
-        {"stream": (hidden_in.shape, f32, VMEM), "scale": (weight.shape, f32, VMEM), **fetch_outputs(weights)},
-        {
-            "landed": VMEM(hidden_in.shape, bf16),
-            "other": VMEM(weight.shape, f32),
-            "send": semaphores(2),
-            "receive": semaphores(2),
-            **fetch_scratch(weights),
-        },
-        1 << 20,
-    )
+            target[...] = self.landed[...].astype(f32) * factor
 
 
 def gelu_and_slope(values):
@@ -549,7 +547,7 @@
     return values * half, slope
 
 
-def ffn_forward(layer, middle, gains, shifts, w_up, w_down, own_up, own_down, weights):
+def ffn_forward(layer, middle, gains, shifts, w_up, w_down, own_up, own_down, weights, cotangent=None, scale=None):
     rows, width = middle.shape
     hidden = w_up.shape[1]
 
@@ -557,8 +555,10 @@
         loads = [Loading(r.own_up.at[layer], r.w_up, r.up, r.local.at[0]), Loading(r.own_down.at[layer], r.w_down, r.down, r.local.at[1])]
         for copy in loads:
             copy.start()
-        greet(*GROUP, *(FETCH if weights else ()))
+        greet(*GROUP, *(FETCH if weights else ()), *(() if cotangent is None else (("c", "zh"),)))
         jobs = fetch_jobs(r, weights, layer + 1)
+        swaps = [] if cotangent is None else [Swapping(r.cotangent, r.landed, r.swap.at[0], r.swap.at[1])]
+        every(jobs + swaps, "step_inner")
         held, active, slope = r.held, r.active, r.slope
         held[pl.ds(0, rows), :] = norm_rows(r.middle[...], r.gains[layer, 2:3, :], r.shifts[layer, 2:3, :]).astype(bf16)
         for copy in loads:
@@ -568,7 +568,9 @@
         def work(start, size, sink):
             calls.append(start)
             if len(calls) == 1:
-                every(jobs, "step_along")
+                every(jobs + swaps, "step_outer")
+            if len(calls) == 4:
+                every(jobs, "step_share")
             here = pl.ds(start, size)
 
             def step(columns):
@@ -592,12 +594,15 @@
         ]
         for copy in stores:
             copy.start()
-        every(jobs, "step_share")
+        every(jobs, "step_relay")
         finish()
         total = r.first[pl.ds(0, rows), :] + r.sums[1].astype(f32) + r.sums[5].astype(f32)
         r.second[...] = total
         r.stream[...] = r.middle[...] + norm_rows(total, r.gains[layer, 3:4, :], r.shifts[layer, 3:4, :])
         every(jobs, "step_end")
+        for swap in swaps:
+            swap.wait()
+            swap.give(r.grad, r.cotangent, r.scale[0:1, 0:1])
         for copy in stores:
             copy.wait()
 
@@ -606,24 +611,26 @@
         3 + layer,
         {
             "middle": (middle, VMEM), "gains": (gains, VMEM), "shifts": (shifts, VMEM), "w_up": (w_up, ANY), "w_down": (w_down, ANY), "own_up": (own_up, ANY), "own_down": (own_down, ANY),
-            **fetch_inputs(weights),
+            **fetch_inputs(weights), **({} if cotangent is None else {"cotangent": (cotangent, VMEM), "scale": (scale, VMEM)}),
         },
         {
             "second": ((rows, width), f32, VMEM), "stream": ((rows, width), f32, VMEM),
             "held_out": ((4 * rows, width), bf16, ANY), "active_out": ((4 * rows, hidden), bf16, ANY),
             "slope_out": ((4 * rows, hidden), bf16, ANY), **fetch_outputs(weights),
+            **({} if cotangent is None else {"grad": ((rows, width), f32, VMEM)}),
         },
         {
             "held": VMEM((4 * rows, width), bf16), "active": VMEM((4 * rows, hidden), bf16), "slope": VMEM((4 * rows, hidden), bf16),
             "up": VMEM(w_up.shape, bf16), "down": VMEM(w_down.shape, bf16), **group_scratch(rows, width), "local": semaphores(5),
             **fetch_scratch(weights),
+            **({} if cotangent is None else {"landed": VMEM(cotangent.shape, bf16), "swap": semaphores(2)}),
         },
         16 * rows * width * hidden,
         4 * rows * hidden,
     )
 
 
-def ffn_backward(layer, grad, saved, gains, shifts, w_up, w_down, own_up, own_down, grads, parts):
+def ffn_backward(layer, grad, saved, gains, shifts, w_up, w_down, own_up, own_down, grads, mixed=None):
     middle = saved.middle
     rows, width = middle.shape
     hidden = w_up.shape[1]
@@ -639,9 +646,18 @@
         ]
         for copy in loads:
             copy.start()
-        greet(*GROUP, *(FETCH if grads or parts else ()))
-        jobs, shares = scatter_jobs(r, grads), share_jobs(r, parts)
-        every(jobs, "step_spread")
+        greet(*GROUP, *(FETCH if grads else ()), *(() if mixed is None else (("c", "zh"),)))
+        jobs = pass_jobs(r, grads)
+        new = [name for name in grads if grads[name][1] == 0]
+        late = [name for name in grads if grads[name][1] == 2]
+        swaps = [] if mixed is None else [Swapping(r.low, r.landed, r.swap.at[0], r.swap.at[1])]
+        if mixed is not None:
+            r.low[...] = r.mixed[...].astype(bf16)
+        crossing = [name for name in grads if grads[name][1] == 1]
+        every(swaps, "step_inner")
+        every_of(jobs, crossing, "step_load", "step_loaded", "step_inner")
+        every_of(jobs, late, "step_load")
+        every_of(jobs, new, "step_spread")
         pulled, gain_three, shift_three = norm_pull(r.second[...], r.gains[layer, 3:4, :], r.grad[...])
         held[pl.ds(0, rows), :] = pulled.astype(bf16)
         for copy in loads:
@@ -652,9 +668,13 @@
         def work(start, size, sink):
             calls.append(start)
             if len(calls) == 1:
-                every(shares, "step_along")
+                every(swaps, "step_outer")
+                every_of(jobs, crossing, "step_outer")
+                every_of(jobs, late, "step_loaded", "step_share")
+            if len(calls) == 3:
+                every_of(jobs, late, "step_relay")
             if len(calls) == 4:
-                every(jobs, "step_fold")
+                every_of(jobs, new, "step_fold")
             here = pl.ds(start, size)
 
             def step(columns):
@@ -670,7 +690,8 @@
 
         finish = exchange(rows, held, work, r.first, r.sums, r.send, r.receive)
 
-        every(shares, "step_share")
+        every_of(jobs, late, "step_mate")
+        every_of(jobs, crossing, "step_join", "step_share")
 
         def step_down(columns):
             r.outcome[0, columns, :] = dot_tn(active[:, columns], held[...]).astype(bf16)
@@ -678,8 +699,8 @@
         tiles(hidden, step_down)
         out_down = pltpu.make_async_copy(r.outcome.at[0], r.grad_down, r.local.at[0])
         out_down.start()
-        every(jobs, "step_add")
-        every(shares, "step_relay")
+        every_of(jobs, new, "step_add", "step_store")
+        every_of(jobs, crossing, "step_relay")
 
         def step_up(columns):
             r.outcome[1, columns, :] = dot_tn(past[:, columns], pushed[...]).astype(bf16)
@@ -687,7 +708,6 @@
         tiles(width, step_up)
         out_up = pltpu.make_async_copy(r.outcome.at[1], r.grad_up, r.local.at[1])
         out_up.start()
-        every(shares, "step_mate")
         finish()
         total = r.first[pl.ds(0, rows), :] + r.sums[1].astype(f32) + r.sums[5].astype(f32)
         pulled, gain_two, shift_two = norm_pull(r.middle[...], r.gains[layer, 2:3, :], total)
@@ -696,7 +716,11 @@
             r.norms[index : index + 1, :] = value
         out_down.wait()
         out_up.wait()
-        every(jobs + shares, "step_end")
+        every_of(jobs, crossing, "step_mate")
+        every_of(jobs, grads, "step_end")
+        for swap in swaps:
+            swap.wait()
+            swap.give(r.mixed_out, r.mixed)
 
     return run(
         body,
@@ -705,10 +729,10 @@
             "grad": (grad, VMEM), "second": (saved.second, VMEM), "middle": (middle, VMEM), "gains": (gains, VMEM),
             "shifts": (shifts, VMEM), "held_in": (saved.held_out, ANY), "active_in": (saved.active_out, ANY),
             "slope_in": (saved.slope_out, ANY), "w_up": (w_up, ANY), "w_down": (w_down, ANY), "own_up": (own_up, ANY), "own_down": (own_down, ANY),
-            **scatter_inputs(grads), **share_inputs(parts),
+            **pass_inputs(grads), **({} if mixed is None else {"mixed": (mixed, VMEM)}),
         },
         {
-            **scatter_outputs(grads), **share_outputs(parts),
+            **pass_outputs(grads), **({} if mixed is None else {"mixed_out": (mixed.shape, f32, VMEM)}),
             "grad_middle": ((rows, width), f32, VMEM), "norms": ((4, width), f32, VMEM),
             "grad_up": (w_up.shape, bf16, ANY), "grad_down": (w_down.shape, bf16, ANY),
         },
@@ -717,7 +741,12 @@
             "active": VMEM((4 * rows, hidden), bf16), "slope": VMEM((4 * rows, hidden), bf16),
             "pushed": VMEM((4 * rows, hidden), bf16), "up": VMEM(w_up.shape, bf16), "down": VMEM(w_down.shape, bf16),
             "outcome": VMEM((2, width, hidden), bf16), **group_scratch(rows, width), "local": semaphores(5),
-            **scatter_scratch(grads), **share_scratch(parts),
+            **pass_scratch(grads),
+            **(
+                {}
+                if mixed is None
+                else {"low": VMEM(mixed.shape, bf16), "landed": VMEM(mixed.shape, bf16), "swap": semaphores(2)}
+            ),
         },
         32 * rows * width * hidden,
     )
@@ -861,31 +890,64 @@
     lse[here, :] = tops
 
 
-def attention_forward(layer, stream, gains, shifts, w_qkv, w_out, own_qkv, own_out, weights):
+def attention_forward(layer, stream, gains, shifts, w_qkv, w_out, own_qkv, own_out, weights, scale=None):
     rows, model = stream.shape
-    width = w_out.shape[0]
+    width = own_out.shape[1]
+    first = scale is not None
+    early = {"qkv": own_qkv, "out": own_out} if first else {}
 
     def body(r):
         held, qkv, attended, lse, weight = r.held, r.qkv, r.attended, r.lse, r.weight
+        w_qkv, w_out = (r.qkv_to, r.out_to) if first else (r.w_qkv, r.w_out)
         loads = [
-            Loading(r.own_qkv.at[layer, index], r.w_qkv.at[index], weight.at[:, pl.ds(index * width, width)], r.local.at[index])
+            Loading(r.own_qkv.at[layer, index], w_qkv.at[index], weight.at[:, pl.ds(index * width, width)], r.local.at[index])
             for index in range(3)
         ]
-        loads.append(Loading(r.own_out.at[layer], r.w_out, r.out, r.local.at[3]))
-        for copy in loads:
-            copy.start()
-        greet(*GROUP, *(FETCH if weights else ()))
+        loads.append(Loading(r.own_out.at[layer], w_out, r.out, r.local.at[3]))
+        if not first:
+            every(loads, "start")
+        greet(*GROUP, *(FETCH if weights else ()), *((("c", "zh"),) if first else ()))
         jobs = fetch_jobs(r, weights, layer)
+        stream = r.stream
+        if first:
+            swap = Swapping(r.stream, r.landed, r.swap.at[0], r.swap.at[1])
+            exchanged = remote(r.weight_in, r.other, r.swap.at[2], r.swap.at[3], flipped("c"))
+            exchanged.start()
+            before = [
+                Fetching(source.at[layer], target, send, receive)
+                for source, target, send, receive in (
+                    (r.own_qkv, r.qkv_to, r.qkv_send, r.qkv_receive), (r.own_out, r.out_to, r.out_send, r.out_receive)
+                )
+            ]
+            every(before, "step_inner")
+            every(before, "step_outer")
+            before[0].step_share()
+            swap.start()
+            before[0].step_relay()
+            before[1].step_share()
+            exchanged.wait()
+            r.scale[...] = jnp.where(holds(), r.weight_in[...], r.other[...])
+            swap.wait()
+            swap.give(r.stream_out, r.stream)
+            stream = r.stream_out
         own = places(rows)[0]
-        held[pl.ds(own, rows), :] = norm_rows(r.stream[...], r.gains[layer, 0:1, :], r.shifts[layer, 0:1, :]).astype(bf16)
-        for copy in loads:
-            copy.wait()
+        held[pl.ds(own, rows), :] = norm_rows(stream[...], r.gains[layer, 0:1, :], r.shifts[layer, 0:1, :]).astype(bf16)
+        if not first:
+            every(loads, "wait")
         calls = []
 
         def arrived(start, size):
             calls.append(start)
             if len(calls) == 1:
-                every(jobs, "step_along")
+                if first:
+                    before[1].step_relay()
+                    before[0].step_end()
+                    every(loads[:3], "start")
+                    every(loads[:3], "wait")
+                else:
+                    every(jobs[:1], "step_outer")
+            if len(calls) == 2 and first:
+                every(jobs, "step_outer")
             here = pl.ds(start, size)
 
             def step(columns):
@@ -902,18 +964,27 @@
         def attend(quarter, high):
             attend_block(rows, pl.multiple_of(quarter * rows, 16), high, qkv, attended, lse)
 
+        every(jobs if first else jobs[:1], "step_inner")
+        if not first:
+            every(jobs[1:], "step_outer")
         attend(3 - zl, True)
+        if not first:
+            every(jobs[1:], "step_inner")
+        if first:
+            before[1].step_end()
+            loads[3].start()
         attend(1 - zl, False)
+        if first:
+            loads[3].wait()
         done = []
 
         def term(start, size, sink):
             if size == rows and not done:
                 done.append(True)
-                if jobs:
-                    jobs[0].step_share()
                 attend(2 + zl, True)
-                every(jobs[1:], "step_share")
+                every(jobs[:1], "step_share")
                 attend(zl, False)
+                every(jobs[:1], "step_relay")
             here = pl.ds(start, size)
 
             def step(columns):
@@ -925,10 +996,12 @@
         late = [pltpu.make_async_copy(attended, r.attended_out, r.local.at[2]), pltpu.make_async_copy(lse, r.lse_out, r.local.at[3])]
         for copy in late:
             copy.start()
+        every(jobs[1:], "step_share")
         finish()
+        every(jobs[1:], "step_relay")
         total = r.first[pl.ds(0, rows), :] + r.sums[1].astype(f32) + r.sums[5].astype(f32)
         r.branch[...] = total
-        r.middle[...] = r.stream[...] + norm_rows(total, r.gains[layer, 1:2, :], r.shifts[layer, 1:2, :])
+        r.middle[...] = stream[...] + norm_rows(total, r.gains[layer, 1:2, :], r.shifts[layer, 1:2, :])
         sent()
         every(jobs, "step_end")
         for copy in stores + late:
@@ -938,18 +1011,22 @@
         body,
         1 + layer,
         {
-            "stream": (stream, VMEM), "gains": (gains, VMEM), "shifts": (shifts, VMEM), "w_qkv": (w_qkv, ANY), "w_out": (w_out, ANY), "own_qkv": (own_qkv, ANY), "own_out": (own_out, ANY),
-            **fetch_inputs(weights),
+            "stream": (stream, VMEM), "gains": (gains, VMEM), "shifts": (shifts, VMEM), "own_qkv": (own_qkv, ANY), "own_out": (own_out, ANY),
+            **fetch_inputs(weights), **({"weight_in": (scale, VMEM)} if first else {"w_qkv": (w_qkv, ANY), "w_out": (w_out, ANY)}),
         },
         {
             "branch": ((rows, model), f32, VMEM), "middle": ((rows, model), f32, VMEM),
             "held_out": ((4 * rows, model), bf16, ANY), "qkv_out": ((4 * rows, 3 * width), bf16, ANY),
             "attended_out": ((4 * rows, width), bf16, ANY), "lse_out": ((4 * rows, 128), f32, ANY), **fetch_outputs(weights),
+            **fetch_outputs(early),
+            **({"stream_out": (stream.shape, f32, VMEM), "scale": (scale.shape, f32, VMEM)} if first else {}),
         },
         {
             "held": VMEM((4 * rows, model), bf16), "qkv": VMEM((4 * rows, 3 * width), bf16), "attended": VMEM((4 * rows, width), bf16),
-            "lse": VMEM((4 * rows, 128), f32), "weight": VMEM((model, 3 * width), bf16), "out": VMEM(w_out.shape, bf16),
+            "lse": VMEM((4 * rows, 128), f32), "weight": VMEM((model, 3 * width), bf16), "out": VMEM((width, model), bf16),
             **group_scratch(rows, model), "local": semaphores(4), **fetch_scratch(weights),
+            **fetch_scratch(early),
+            **({"landed": VMEM(stream.shape, bf16), "other": VMEM(scale.shape, f32), "swap": semaphores(4)} if first else {}),
         },
         24 * rows * model * width,
         64 * rows * rows,
@@ -986,9 +1063,12 @@
         grad_query[here, columns] = (result * scale).astype(bf16)
 
 
-def attention_backward(layer, grad, stream, saved, gains, shifts, w_qkv, w_out, own_qkv, own_out, grads, parts):
+def attention_backward(layer, grad, stream, saved, gains, shifts, w_qkv, w_out, own_qkv, own_out, grads, norms=None):
     rows, model = stream.shape
     width = w_out.shape[0]
+    final = norms is not None
+    shape = jax.ShapeDtypeStruct
+    mine = {"qkv_last": (shape(w_qkv.shape, bf16), 0, 2), "out_last": (shape(w_out.shape, bf16), 0, 2)} if final else {}
 
     def body(r):
         held, past, qkv, attended, lse, inner, above = r.held, r.past, r.qkv, r.attended, r.lse, r.inner, r.above
@@ -1006,9 +1086,12 @@
         ]
         for copy in loads:
             copy.start()
-        greet(*GROUP, *(FETCH if grads or parts else ()))
-        jobs, shares = scatter_jobs(r, grads), share_jobs(r, parts)
-        every(jobs, "step_spread")
+        greet(*GROUP, *(FETCH if grads else ()), *((("c", "zh"),) if final else ()))
+        jobs = pass_jobs(r, {**grads, **mine}, {"qkv_last": r.outcome, "out_last": r.outcome_out})
+        new = [name for name in grads if grads[name][1] == 0]
+        crossing = [name for name in grads if grads[name][1] == 1]
+        every_of(jobs, crossing, "step_load")
+        every_of(jobs, new[:1], "step_spread")
         own = places(rows)[0]
         pulled, gain_one, shift_one = norm_pull(r.branch[...], r.gains[layer, 1:2, :], r.grad[...])
         held[pl.ds(own, rows), :] = pulled.astype(bf16)
@@ -1040,18 +1123,21 @@
             inner[here, :] = tile
             blocks.append(size)
             if len(blocks) == 2:
-                every(shares, "step_along")
                 back(2 + zl, True)
                 back(zl, False)
 
         sent = gather(rows, held, arrived, r.send, r.receive)
-        every(jobs[:1], "step_fold")
+        every_of(jobs, crossing, "step_loaded", "step_outer")
+        every_of(jobs, new[:1], "step_fold")
+        every_of(jobs, new[1:], "step_spread")
         back(3 - zl, True)
-        every(shares, "step_share")
-        every(jobs[1:], "step_fold")
+        every_of(jobs, new[:1], "step_add")
+        if not final:
+            every_of(jobs, new[:1], "step_outer")
+        every_of(jobs, crossing, "step_inner")
         back(1 - zl, False)
-        every(jobs[:1], "step_add")
-        every(shares, "step_relay")
+        if not final:
+            every_of(jobs, new[:1], "step_inner")
         pushed[:, pl.ds(width, width)] = grad_key[...].astype(bf16)
         pushed[:, pl.ds(2 * width, width)] = grad_value[...].astype(bf16)
 
@@ -1065,34 +1151,91 @@
 
         finish = scatter(rows, term, r.first, r.sums, r.send, r.receive)
 
-        every(jobs[1:], "step_add")
+        every_of(jobs, new[1:], "step_fold")
+        if final:
+            every_of(jobs, new[:1], "step_outer", "step_inner")
 
         def step_out(columns):
             r.outcome_out[:, columns] = dot_tn(attended[...], held[:, columns]).astype(bf16)
 
         tiles(model, step_out)
-        outs = [pltpu.make_async_copy(r.outcome_out, r.grad_out, r.local.at[0])]
-        outs[0].start()
+        outs = [] if final else [pltpu.make_async_copy(r.outcome_out, r.grad_out, r.local.at[0])]
+        every(outs, "start")
+        every_of(jobs, [name for name in mine if name == "out_last"], "step_spread")
 
         def step_qkv(columns):
-            r.outcome[columns, :] = dot_tn(past[:, columns], pushed[...]).astype(bf16)
+            value = dot_tn(past[:, columns], pushed[...]).astype(bf16)
+            for index in range(3):
+                r.outcome[index, columns, :] = value[:, index * width : (index + 1) * width]
 
         tiles(model, step_qkv)
-        for index in range(3):
-            copy = pltpu.make_async_copy(r.outcome.at[:, pl.ds(index * width, width)], r.grad_qkv.at[index], r.local.at[1 + index])
-            copy.start()
-            outs.append(copy)
-        every(shares, "step_mate")
+        if final:
+            jobs["qkv_last"].step_spread()
+            every_of(jobs, new[1:], "step_add", "step_outer", "step_inner")
+            for name in crossing:
+                every_of(jobs, [name], "step_join", "step_share")
+        else:
+            out = pltpu.make_async_copy(r.outcome, r.grad_qkv, r.local.at[1])
+            out.start()
+            outs.append(out)
+            every_of(jobs, new[:1], "step_join")
+            every_of(jobs, new[1:], "step_add")
+            every_of(jobs, new, "step_store")
         finish()
         total = r.first[pl.ds(0, rows), :] + r.sums[1].astype(f32) + r.sums[5].astype(f32)
         pulled, gain_zero, shift_zero = norm_pull(r.stream[...], r.gains[layer, 0:1, :], total)
-        r.grad_stream[...] = r.grad[...] + pulled
-        for index, value in enumerate((gain_zero, shift_zero, gain_one, shift_one)):
-            r.norms[index : index + 1, :] = value
+        rows_norms = (gain_zero, shift_zero, gain_one, shift_one)
+        if final:
+            r.home[...] = r.grad[...] + pulled
+            r.low[...] = r.home[...].astype(bf16)
+            swap = Swapping(r.low, r.landed, r.swap.at[0], r.swap.at[1])
+            for index, value in enumerate(rows_norms):
+                r.norms[index : index + 1, :] = value
+            for index in range(len(norms)):
+                r.norms[pl.ds(4 + 4 * index, 4), :] = getattr(r, f"norms{index}")[...]
+
+            def cube(index, wait):
+                copy = remote(
+                    r.norms, r.norms_land.at[index], r.swap.at[2 + index], r.swap.at[7 + index], flipped(CUBE[index])
+                )
+                if not wait:
+                    copy.start()
+                    return
+                copy.wait()
+                r.norms[...] = r.norms[...] + r.norms_land[index]
+
+            cube(0, False)
+            every_of(jobs, mine, "step_fold")
+            cube(0, True)
+            cube(1, False)
+            every_of(jobs, crossing, "step_relay")
+            cube(1, True)
+            cube(2, False)
+            every_of(jobs, mine, "step_add", "step_outer", "step_inner")
+            swap.start()
+            every_of(jobs, crossing, "step_mate")
+            cube(2, True)
+            cube(3, False)
+            every_of(jobs, new[:1], "step_join", "step_share")
+            cube(3, True)
+            cube(4, False)
+            every_of(jobs, new[1:], "step_join", "step_share")
+            every_of(jobs, new, "step_relay")
+            every_of(jobs, new[:1], "step_mate")
+            every_of(jobs, mine, "step_join", "step_share")
+            every_of(jobs, new[1:], "step_mate")
+            every_of(jobs, mine, "step_relay")
+            every_of(jobs, mine, "step_mate")
+            cube(4, True)
+            swap.wait()
+            swap.give(r.grad_stream, r.home)
+        else:
+            r.grad_stream[...] = r.grad[...] + pulled
+            for index, value in enumerate(rows_norms):
+                r.norms[index : index + 1, :] = value
         sent()
-        for copy in outs:
-            copy.wait()
-        every(jobs + shares, "step_end")
+        every(outs, "wait")
+        every_of(jobs, jobs, "step_end")
 
     return run(
         body,
@@ -1101,147 +1244,84 @@
             "grad": (grad, VMEM), "branch": (saved.branch, VMEM), "stream": (stream, VMEM), "gains": (gains, VMEM),
             "shifts": (shifts, VMEM), "held_in": (saved.held_out, ANY), "qkv_in": (saved.qkv_out, ANY),
             "attended_in": (saved.attended_out, ANY), "lse_in": (saved.lse_out, ANY), "w_qkv": (w_qkv, ANY), "w_out": (w_out, ANY), "own_qkv": (own_qkv, ANY), "own_out": (own_out, ANY),
-            **scatter_inputs(grads), **share_inputs(parts),
+            **pass_inputs(grads), **({f"norms{index}": (value, VMEM) for index, value in enumerate(norms)} if final else {}),
         },
         {
-            **scatter_outputs(grads), **share_outputs(parts),
-            "grad_stream": ((rows, model), f32, VMEM), "norms": ((4, model), f32, VMEM),
-            "grad_qkv": (w_qkv.shape, bf16, ANY), "grad_out": (w_out.shape, bf16, ANY),
+            **pass_outputs({**grads, **mine}),
+            "grad_stream": ((rows, model), f32, VMEM), "norms": ((16 if final else 4, model), f32, VMEM),
+            **({} if final else {"grad_qkv": (w_qkv.shape, bf16, ANY), "grad_out": (w_out.shape, bf16, ANY)}),
         },
         {
             "held": VMEM((4 * rows, model), bf16), "past": VMEM((4 * rows, model), bf16), "qkv": VMEM((4 * rows, 3 * width), bf16),
             "attended": VMEM((4 * rows, width), bf16), "lse": VMEM((4 * rows, 128), f32), "inner": VMEM((4 * rows, 128), f32),
             "above": VMEM((4 * rows, width), bf16), "pushed": VMEM((4 * rows, 3 * width), bf16),
             "grad_key": VMEM((4 * rows, width), f32), "grad_value": VMEM((4 * rows, width), f32),
-            "weight": VMEM((model, 3 * width), bf16), "out": VMEM(w_out.shape, bf16), "outcome": VMEM((model, 3 * width), bf16),
+            "weight": VMEM((model, 3 * width), bf16), "out": VMEM(w_out.shape, bf16), "outcome": VMEM((3, model, width), bf16),
             "outcome_out": VMEM(w_out.shape, bf16), **group_scratch(rows, model), "local": semaphores(8),
-            **scatter_scratch(grads), **share_scratch(parts),
+            **pass_scratch({**grads, **mine}),
+            **(
+                {
+                    "home": VMEM((rows, model), f32), "low": VMEM((rows, model), bf16), "landed": VMEM((rows, model), bf16),
+                    "norms_land": VMEM((len(CUBE), 16, model), f32), "swap": semaphores(12),
+                }
+                if final
+                else {}
+            ),
         },
         60 * rows * model * width,
         64 * rows * rows,
     )
 
 
-CUBE = ("c", "zl", "p", "gl", "zh")
-
-
-def tail(grads, parts, norms, grad_in):
-    def body(r):
-        greet(*GROUP, *FETCH, ("c", "zh"))
-        jobs = scatter_jobs(r, grads)
-        every(jobs, "step_spread")
-        shares = share_jobs(r, parts)
-        every(shares, "step_along")
-        swap = remote(r.low, r.landed, r.send.at[0], r.receive.at[0], flipped("c", "zh"))
-        r.low[...] = r.grad_in[...].astype(bf16)
-        pl.when(jnp.logical_not(holds()))(swap.start)
-        total = r.norms[...]
-        for index, name in enumerate(CUBE):
-            r.norms_out[...] = total
-            copy = remote(r.norms_out, r.land.at[index], r.send.at[1 + index], r.receive.at[1 + index], flipped(name))
-            copy.start()
-            copy.wait()
-            total = total + r.land[index]
-        r.norms_out[...] = total
-        every(jobs, "step_fold")
-        every(shares, "step_share")
-        every(jobs, "step_add")
-        every(shares, "step_relay")
-        last = [
-            Sharing(
-                getattr(r, name + "_sum"), getattr(r, name + "_to"),
-                *[getattr(r, f"{name}_{end}") for end in SHARE[2:]],
-            )
-            for name in grads
-        ]
-        every(last, "step_along")
-        every(shares, "step_mate")
-        every(last, "step_share")
-        every(last, "step_relay")
-        every(last, "step_mate")
-
-        @pl.when(holds())
-        def _():
-            r.grad_out[...] = r.grad_in[...]
-
-        @pl.when(jnp.logical_not(holds()))
-        def _():
-            swap.wait()
-            r.grad_out[...] = r.landed[...].astype(f32)
-
-        every(jobs + shares + last, "step_end")
-
-    extra = {name: jax.ShapeDtypeStruct(part_shape(value.shape, 4), bf16) for name, value in grads.items()}
-    return run(
-        body,
-        9,
-        {**scatter_inputs(grads), **share_inputs(parts), "norms": (norms, VMEM), "grad_in": (grad_in, VMEM)},
-        {
-            **scatter_outputs(grads), **share_outputs(parts), **share_outputs(extra),
-            "norms_out": (norms.shape, f32, VMEM), "grad_out": (grad_in.shape, f32, VMEM),
-        },
-        {
-            "land": VMEM((len(CUBE), *norms.shape), f32),
-            "send": semaphores(1 + len(CUBE)),
-            "receive": semaphores(1 + len(CUBE)),
-            "low": VMEM(grad_in.shape, bf16),
-            "landed": VMEM(grad_in.shape, bf16),
-            **scatter_scratch(grads), **share_scratch(parts), **share_scratch(extra),
-        },
-        1 << 20,
-    )
-
-
 def per_device(hidden_in, cotangent, group_ids, group_sizes, w_qkv, w_out, w_up, w_down, gains, shifts):
-    layers = w_qkv.shape[0]
     size = jnp.sum(jnp.where(jnp.arange(group_sizes.shape[0]) == group_ids[0], group_sizes, 0))
     weight = jnp.full((8, 128), 1.0 / size.astype(f32), f32)
-    start = head(hidden_in, weight, {"qkv": w_qkv, "out": w_out})
-    stream, qkv, out = start.stream, start.qkv_to, start.out_to
-    attentions, ffns = [], []
-    for layer in range(layers):
-        last = layer + 1 == layers
-        att = attention_forward(layer, stream, gains, shifts, qkv, out, w_qkv, w_out, {"up": w_up, "down": w_down})
-        ffn = ffn_forward(layer, att.middle, gains, shifts, att.up_to, att.down_to, w_up, w_down, {} if last else {"qkv": w_qkv, "out": w_out})
-        ffn.middle = att.middle
-        attentions.append((stream, att, qkv, out))
-        ffns.append((ffn, att.up_to, att.down_to))
-        stream = ffn.stream
-        if not last:
-            qkv, out = ffn.qkv_to, ffn.out_to
-    swap = functools.partial(lax.ppermute, axis_name=("c", "zh"), perm=((0, 0), (1, 2), (2, 1), (3, 3)))
-    grad = swap(cotangent).astype(f32) * start.scale[0, 0]
-    mixed = swap(stream.astype(bf16))
-    norms, done, grads, parts = [None] * layers, {}, {}, {}
-
-    def carry(result, names):
-        done.update({name: getattr(result, name + "_to") for name in parts})
-        following = {name: getattr(result, name + "_part") for name in grads}
-        return dict(names), following
-
-    for layer in reversed(range(layers)):
-        back = ffn_backward(layer, grad, ffns[layer][0], gains, shifts, *ffns[layer][1:], w_up, w_down, grads, parts)
-        grads, parts = carry(back, {f"up{layer}": back.grad_up, f"down{layer}": back.grad_down})
-        before, att, qkv, out = attentions[layer]
-        deep = attention_backward(
-            layer, back.grad_middle, before, att, gains, shifts, qkv, out, w_qkv, w_out, grads, parts
+    own_att, own_ffn = (w_qkv, w_out), (w_up, w_down)
+    att_zero = attention_forward(
+        0, hidden_in, gains, shifts, None, None, *own_att, {"up": w_up, "down": w_down}, weight
+    )
+    att_weights = [(att_zero.qkv_to, att_zero.out_to)]
+    ffn_weights = [(att_zero.up_to, att_zero.down_to)]
+    ffn_zero = ffn_forward(
+        0, att_zero.middle, gains, shifts, *ffn_weights[0], *own_ffn, {"qkv": w_qkv, "out": w_out}
+    )
+    att_weights.append((ffn_zero.qkv_to, ffn_zero.out_to))
+    att_one = attention_forward(1, ffn_zero.stream, gains, shifts, *att_weights[1], *own_att, {"up": w_up, "down": w_down})
+    ffn_weights.append((att_one.up_to, att_one.down_to))
+    ffn_one = ffn_forward(
+        1, att_one.middle, gains, shifts, *ffn_weights[1], *own_ffn, {}, cotangent, att_zero.scale
+    )
+    ffn_zero.middle, ffn_one.middle = att_zero.middle, att_one.middle
+    back_one = ffn_backward(1, ffn_one.grad, ffn_one, gains, shifts, *ffn_weights[1], *own_ffn, {}, ffn_one.stream)
+    deep_one = attention_backward(
+        1, back_one.grad_middle, ffn_zero.stream, att_one, gains, shifts, *att_weights[1], *own_att,
+        {"up1": (back_one.grad_up, 0, 1), "down1": (back_one.grad_down, 0, 0)},
+    )
+    back_zero = ffn_backward(
+        0, deep_one.grad_stream, ffn_zero, gains, shifts, *ffn_weights[0], *own_ffn,
+        {"up1": (deep_one.up1_out, 2, 2), "down1": (deep_one.down1_out, 1, 2), "qkv1": (deep_one.grad_qkv, 0, 0), "out1": (deep_one.grad_out, 0, 0)},
+    )
+    last = attention_backward(
+        0, back_zero.grad_middle, att_zero.stream_out, att_zero, gains, shifts, *att_weights[0], *own_att,
+        {
+            "qkv1": (back_zero.qkv1_out, 1, 2), "out1": (back_zero.out1_out, 1, 2),
+            "up0": (back_zero.grad_up, 0, 2), "down0": (back_zero.grad_down, 0, 2),
+        },
+        (back_zero.norms, deep_one.norms, back_one.norms),
+    )
+    grads = [
+        jnp.stack(pair).astype(f32)
+        for pair in (
+            (last.qkv_last_out, last.qkv1_out),
+            (last.out_last_out, last.out1_out),
+            (last.up0_out, back_zero.up1_out),
+            (last.down0_out, back_zero.down1_out),
         )
-        grads, parts = carry(deep, {f"qkv{layer}": deep.grad_qkv, f"out{layer}": deep.grad_out})
-        grad = deep.grad_stream
-        norms[layer] = jnp.concatenate([deep.norms, back.norms])
-    total = tail(grads, parts, jnp.concatenate(norms), grad)
-    done.update({name: getattr(total, name + "_to") for name in (*grads, *parts)})
-
-    def stacked(name):
-        whole = jnp.stack([done[f"{name}{layer}"] for layer in range(layers)]).astype(f32)
-        return lax.psum(whole, "gh") if lax.axis_size("gh") > 1 else whole
-
-    sums = total.norms_out.reshape(layers, 4, 2, -1)
+    ]
+    sums = last.norms.reshape(2, 4, 2, -1)
     if lax.axis_size("gh") > 1:
-        sums = lax.psum(sums, "gh")
-    return (
-        mixed.astype(f32), total.grad_out, stacked("qkv"), stacked("out"), stacked("up"), stacked("down"), sums[:, :, 0], sums[:, :, 1]
-    )
+        grads, sums = lax.psum((grads, sums), "gh")
+    return (back_one.mixed_out, last.grad_stream, *grads, sums[:, :, 0], sums[:, :, 1])
 
 
 def solution(mesh):

time: 607 us -> 512 us (0.84)
  Pallas kernels: 567 us -> 479 us
    pallas_call x10 -> x8, Pallas kernels: 567 us -> 479 us  [run(): pl.pallas_call(kernel, out_shape=tuple((jax.ShapeDtypeStruct(shape, kind)...]
    convert_element_type x5 -> x3, other arithmetic: 15.2 us -> 12.7 us  [per_device(): jnp.stack(pair).astype(f32)]
  transfers between devices with their start and end apart: 2 -> 0, of which waited for: 0 -> 0; matrix products, arithmetic and copies ran while one was open for 4% -> 0% of each run, Pallas kernels for 95% -> 0%
where the time goes in v5:
time: 512 us; the launch traced here: 503 us
  Pallas kernels  479 us (94%)
  other arithmetic  14 us (3%)
  local copies, waits for them, and re-layouts  7.07 us (1%)
    pallas_call x8, Pallas kernels, run(): pl.pallas_call(kernel, out_shape=tuple((jax.ShapeDtypeStruct(shape, kind)...  479 us
    convert_element_type x3, other arithmetic, per_device(): jnp.stack(pair).astype(f32)  12.7 us

profile of v5, /device:TPU:0, one launch (start us, length us, event | category | flops | bytes accessed | tf_op | source)
XLA Modules:
  0.0 503.0 jit_solution(16382911809804935967)
XLA Ops:
  1.3 1.3 fusion
  3.3 0.6 broadcast_in_dim.8.refs_7_
  3.9 79.9 %shard_map.161 = (f32[272,1024]{1,0:T(8,128)}, f32[272,1024]{1,0:T(8,128)}, bf16[1088,1024]{1,0:T(8,128)(2,1)}, bf16[1088,768]{1,0:T(8,128)(2,1)}, bf16[1088,256...) custom-call(bf16[272,1024]{1,0:T(8,128)(2,1)} %refs_0_.1, ...), custom_call_target="tpu_custom_call" | custom-call | flops 1711276032 | bytes 13209600 | tf_op jit(solution)/shard_map/pallas_call | solution.py:164
  83.8 41.8 %shard_map.162 = (f32[272,1024]{1,0:T(8,128)}, f32[272,1024]{1,0:T(8,128)}, bf16[1088,1024]{1,0:T(8,128)(2,1)}, bf16[1088,1024]{1,0:T(8,128)(2,1)}, bf16[1088,10...) custom-call(f32[272,1024]{1,0:T(8,128)} %get-tuple-element.68.refs_0_.refs_2_, ...), custom_call_target="tpu_custom_call" | custom-call | flops 4563402752 | bytes 17956864 | tf_op jit(solution)/shard_map/pallas_call | solution.py:164
  125.6 54.1 %shard_map.163 = (f32[272,1024]{1,0:T(8,128)}, f32[272,1024]{1,0:T(8,128)}, bf16[1088,1024]{1,0:T(8,128)(2,1)}, bf16[1088,768]{1,0:T(8,128)(2,1)}, bf16[1088,256...) custom-call(f32[272,1024]{1,0:T(8,128)} %get-tuple-element.71.refs_0_.refs_2_, ...), custom_call_target="tpu_custom_call" | custom-call | flops 1711276032 | bytes 15859712 | tf_op jit(solution)/shard_map/pallas_call | solution.py:164
  179.7 42.0 %shard_map.164 = (f32[272,1024]{1,0:T(8,128)}, f32[272,1024]{1,0:T(8,128)}, bf16[1088,1024]{1,0:T(8,128)(2,1)}, bf16[1088,1024]{1,0:T(8,128)(2,1)}, bf16[1088,1024]{1,0:T(8,128)(2,1)}, /*index=5*/f32[272,1024]{1,0:T(8,128)}) custom-call(f32[272,1024]{1,0:T(8,128)} %get-tuple-element.74.refs_0_.refs_2_, f32[2,4,1024]{2,1,0:T(4,128)} %refs_3_.11, ...), custom_call_target="tpu_custom_call" | custom-call | flops 4563402752 | bytes 14323712 | tf_op jit(solution)/shard_map/pallas_call | solution.py:164
  221.7 42.1 %shard_map.165 = (f32[272,1024]{1,0:T(8,128)}, f32[272,1024]{1,0:T(8,128)}, f32[4,1024]{1,0:T(4,128)}, bf16[1024,1024]{1,0:T(8,128)(2,1)}, bf16[1024,1024]{1,0:T(8,128)(2,1)}) custom-call(f32[272,1024]{1,0:T(8,128)} %get-tuple-element.78.refs_0_, f32[272,1024]{1,0:T(8,128)} %get-tuple-element.79.refs_1_, f32[272,1024]{1,0:T(8,128)} %get-tuple-element.74.refs_0_.refs_2_, ...), custom_call_target="tpu_custom_call" | custom-call | flops 9126805504 | bytes 23789568 | tf_op jit(solution)/shard_map/pallas_call | solution.py:164
  263.8 57.2 %shard_map.166 = (bf16[256,1024]{1,0:T(8,128)(2,1)}, bf16[256,1024]{1,0:T(8,128)(2,1)}, f32[272,1024]{1,0:T(8,128)}, f32[4,1024]{1,0:T(4,128)}, bf16[3,1024,256]...) custom-call(f32[272,1024]{1,0:T(8,128)} %get-tuple-element.85.refs_0_, f32[272,1024]{1,0:T(8,128)} %get-tuple-element.86.refs_1_, ...), custom_call_target="tpu_custom_call" | custom-call | flops 4278190080 | bytes 18907136 | tf_op jit(solution)/shard_map/pallas_call | solution.py:164
  321.0 53.9 %shard_map.167 = (bf16[1024,1024]{1,0:T(8,128)(2,1)}, bf16[1024,1024]{1,0:T(8,128)(2,1)}, bf16[3,256,256]{2,1,0:T(8,128)(2,1)}, bf16[64,1024]{1,0:T(8,128)(2,1)}...) custom-call(f32[272,1024]{1,0:T(8,128)} %get-tuple-element.93.refs_0_, ...), custom_call_target="tpu_custom_call" | custom-call | flops 9126805504 | bytes 25821184 | tf_op jit(solution)/shard_map/pallas_call | solution.py:164
  374.9 108.4 %shard_map.168 = (bf16[3,1024,256]{2,1,0:T(8,128)(2,1)}, bf16[256,1024]{1,0:T(8,128)(2,1)}, bf16[1024,1024]{1,0:T(8,128)(2,1)}, bf16[1024,1024]{1,0:T(8,128)(2,1...) custom-call(f32[272,1024]{1,0:T(8,128)} %get-tuple-element.102.refs_0_,, ...), custom_call_target="tpu_custom_call" | custom-call | flops 4278190080 | bytes 19480576 | tf_op jit(solution)/shard_map/pallas_call | solution.py:164
  483.3 0.0 copy-start.4
  483.3 1.0 reshape.19
  484.4 0.1 fusion.1
  484.4 0.6 copy_bitcast_fusion
  485.1 2.7 maximum_convert_fusion.3
  487.7 0.0 copy-done.5
  487.8 3.6 maximum_convert_fusion.2
  491.4 0.6 copy-done.1
  492.0 0.9 copy-done.2
  492.9 0.6 copy-done.3
  493.5 6.5 %maximum_convert_fusion = (f32[2,1024,1024]{2,1,0:T(8,128)}, f32[2,1024,1024]{2,1,0:T(8,128)}) fusion(bf16[1,1024,1024]{2,1,0:T(8,128)(2,1)S(1)} %bitcast.14, bf16[1,1024,1024]{2,1,0:T(8,128)(2,1)S(1)} %bitcast.16, bf16[1,1024,1024]{2,1,0:T(8,128)(2,1)S(1)} %bitcast.15, bf16[1,1024,1024]{2,1,0:T(8,128)(2,1)S(1)} %bitcast.17), kind=kLoop, calls=%fused_computation | loop fusion | flops 8388608 | bytes 25165824 | tf_op jit(solution)/shard_map/convert_element_type | solution.py:1313
  499.9 1.0 copy.27
  500.9 0.7 copy-done.7
  501.6 1.0 copy.28
  (10 shorter events, 0.0 us)
Async XLA Ops:
  483.3 4.4 copy-start.4
  483.3 4.4 copy-start.5
  487.7 3.6 copy-start
  487.7 4.2 copy-start.1
  487.7 5.1 %copy-start.2 = (bf16[1024,1024]{1,0:T(8,128)(2,1)S(1)}, bf16[1024,1024]{1,0:T(8,128)(2,1)}, u32[]{:S(2)}) copy-start(bf16[1024,1024]{1,0:T(8,128)(2,1)} %get-tuple-element.123) | copy-start | bytes 6291460
  487.7 5.7 %copy-start.3 = (bf16[1024,1024]{1,0:T(8,128)(2,1)S(1)}, bf16[1024,1024]{1,0:T(8,128)(2,1)}, u32[]{:S(2)}) copy-start(bf16[1024,1024]{1,0:T(8,128)(2,1)} %get-tuple-element.125) | copy-start | bytes 6291460
  493.5 6.5 %copy-start.6 = (f32[272,1024]{1,0:T(8,128)S(1)}, f32[272,1024]{1,0:T(8,128)}, u32[]{:S(2)}) copy-start(f32[272,1024]{1,0:T(8,128)} %get-tuple-element.142) | copy-start | bytes 3342340
  499.9 1.6 copy-start.7

commit v6 on v5

--- a/solution.py
+++ b/solution.py
@@ -93,18 +93,19 @@
     lax.fori_loop(0, width // TILE, step, 0)
 
 
-def exchange(rows, held, work, first, sums, send, receive):
+def exchange(rows, held, prepare, work, first, sums, send, receive):
     mate, near = flipped("c"), flipped("zl")
     own = pl.ds(0, rows)
     parts = cut_rows(rows)
-    copies = [remote(held.at[own], held.at[pl.ds(rows, rows)], send.at[0], receive.at[0], mate)]
-    copies[0].start()
     along = []
     for index, (start, size) in enumerate(parts):
+        prepare(start, size)
         place = pl.ds(2 * rows + 2 * start, size)
         copy = remote(held.at[pl.ds(start, size)], held.at[place], send.at[1 + index], receive.at[1 + index], near)
         copy.start()
         along.append(copy)
+    copies = [remote(held.at[own], held.at[pl.ds(rows, rows)], send.at[0], receive.at[0], mate)]
+    copies[0].start()
 
     def keep(row, columns, value):
         first[pl.ds(row, value.shape[0]), columns] = value
@@ -144,29 +145,43 @@
         final.append(last)
         copies += [relay, cross]
 
-    def finish():
+    def finish(done):
         back.wait_recv()
-        for copy in final:
+        for copy, (start, size) in zip(final, parts):
             copy.wait_recv()
-        for copy in copies + along + final:
-            copy.wait_send()
+            done(start, size, summed(first, sums, start, size))
+        every(copies + along + final, "wait_send")
 
     return finish
 
 
+def summed(first, sums, start, size):
+    part = pl.ds(start, size)
+    return first[part, :] + sums[1, part, :].astype(f32) + sums[5, part, :].astype(f32)
+
+
 def run(body, number, inputs, outputs, scratch, flops, transcendentals=0):
-    names = [*inputs, *outputs, *scratch]
+    copied = [name for name, (_, memory) in inputs.items() if memory is VMEM]
+    own = {name: VMEM(inputs[name][0].shape, inputs[name][0].dtype) for name in copied}
+    names = [*inputs, *outputs, *scratch, *(name + "_copy" for name in copied), "arrivals"]
 
     def kernel(*refs):
-        body(types.SimpleNamespace(**dict(zip(names, refs))))
+        found = dict(zip(names, refs))
+        copies = [
+            pltpu.make_async_copy(found[name], found[name + "_copy"], found["arrivals"].at[index])
+            for index, name in enumerate(copied)
+        ]
+        every(copies, "start")
+        found.update({name: found[name + "_copy"] for name in copied})
+        body(types.SimpleNamespace(**found, ready=lambda: every(copies, "wait")))
 
     moved = sum(value.size * value.dtype.itemsize for value, _ in inputs.values())
     results = pl.pallas_call(
         kernel,
         out_shape=tuple(jax.ShapeDtypeStruct(shape, kind) for shape, kind, _ in outputs.values()),
-        in_specs=[pl.BlockSpec(memory_space=memory) for _, memory in inputs.values()],
+        in_specs=[pl.BlockSpec(memory_space=ANY) for _ in inputs],
         out_specs=tuple(pl.BlockSpec(memory_space=memory) for _, _, memory in outputs.values()),
-        scratch_shapes=list(scratch.values()),
+        scratch_shapes=[*scratch.values(), *own.values(), semaphores(len(copied))],
         compiler_params=pltpu.CompilerParams(collective_id=number, has_side_effects=True, vmem_limit_bytes=58 << 20),
         cost_estimate=pl.CostEstimate(flops=flops, bytes_accessed=moved, transcendentals=transcendentals),
     )(*[value for value, _ in inputs.values()])
@@ -269,11 +284,14 @@
     def own(self, half):
         return self.at(half, *[lax.axis_index(name) for name in ORDERS[half]])
 
+    def quarter(self, half):
+        return pick(self.target, self.own(half))
+
     def along(self, half):
-        return self.copy(half, pick(self.source, self.own(half)), pick(self.target, self.own(half)), "zh")
+        return self.copy(half, pick(self.source, self.own(half)), self.quarter(half), "zh")
 
     def direct(self, half, axis):
-        rows = pick(self.target, self.own(half))
+        rows = self.quarter(half)
         return self.copy(2 + 2 * half + axis, rows, rows, ORDERS[half][axis])
 
     def relay(self, half):
@@ -293,13 +311,28 @@
     def step_outer(self):
         self.start_along(jnp.logical_not(inner()))
 
-    def step_share(self):
-        @pl.when(jnp.logical_not(holds()))
+    def step_sent(self):
+        @pl.when(holds())
+        def _():
+            for half in range(2):
+                self.along(half).wait_send()
+
+    def share_if(self, here):
+        @pl.when(jnp.logical_and(jnp.logical_not(holds()), here))
         def _():
             for half in range(2):
                 self.along(half).wait_recv()
                 self.direct(half, 1).start()
                 self.direct(half, 0).start()
+
+    def step_share(self):
+        self.share_if(True)
+
+    def step_share_outer(self):
+        self.share_if(jnp.logical_not(inner()))
+
+    def step_share_inner(self):
+        self.share_if(inner())
 
     def step_relay(self):
         @pl.when(jnp.logical_not(holds()))
@@ -308,12 +341,7 @@
                 self.direct(half, 1).wait_recv()
                 self.relay(half).start()
 
-    def step_end(self):
-        @pl.when(holds())
-        def _():
-            for half in range(2):
-                self.along(half).wait_send()
-
+    def step_got(self):
         @pl.when(jnp.logical_not(holds()))
         def _():
             for half in range(2):
@@ -321,13 +349,19 @@
                 self.direct(half, 1).wait_send()
                 self.relay(half).wait()
 
+    def step_end(self):
+        self.step_sent()
+        self.step_got()
+
 
 class Passing(Halves):
-    def __init__(self, refs, name, first, last, source=None):
+    def __init__(self, refs, name, first, last, source=None, out=None):
         self.first, self.last = first, last
         for field in ("in", "out", "land", "mine", "more", "sum", "cross", "send", "receive", "local"):
             setattr(self, field, getattr(refs, f"{name}_{field}", None))
         self.source = source if source is not None else getattr(refs, f"{name}_in", None)
+        if out is not None:
+            self.out = out
         self.size = self.sum.shape[-2] // 2
 
     def place_of(self, half):
@@ -407,11 +441,25 @@
     def step_outer(self):
         pl.when(jnp.logical_not(jnp.logical_or(holds(), inner())))(self.along().start)
 
-    def step_join(self):
-        @pl.when(holds())
+    def join_if(self, here):
+        @pl.when(jnp.logical_and(holds(), here))
         def _():
             self.along().wait_recv()
             self.sum[...] = (self.sum[...].astype(f32) + self.cross[...].astype(f32)).astype(bf16)
+            if self.last == 2:
+                for half in range(2):
+                    self.direct(half, 1).start()
+                    self.direct(half, 0).start()
+                    self.place(half).start()
+
+    def step_join_outer(self):
+        self.join_if(jnp.logical_not(inner()))
+
+    def step_join_inner(self):
+        self.join_if(inner())
+
+    def step_join(self):
+        self.join_if(True)
 
     def step_share(self):
         @pl.when(holds())
@@ -475,8 +523,8 @@
         yield name, whole, part_shape(whole, 4), first, last
 
 
-def pass_jobs(refs, grads, sources=None):
-    return {name: Passing(refs, name, first, last, (sources or {}).get(name)) for name, (_, first, last) in grads.items()}
+def pass_jobs(refs, grads, ends=None):
+    return {name: Passing(refs, name, first, last, *(ends or {}).get(name, ())) for name, (_, first, last) in grads.items()}
 
 
 def pass_inputs(grads):
@@ -510,32 +558,49 @@
 
 
 class Swapping:
-    def __init__(self, source, landed, send, receive):
-        self.landed = landed
-        self.copy = remote(source, landed, send, receive, flipped("c", "zh"))
+    def __init__(self, source, landed, semaphores):
+        self.source, self.landed = source, landed
+        self.parts = cut_rows(source.shape[0])
+        self.copies = [
+            remote(
+                source.at[pl.ds(start, size)], landed.at[pl.ds(start, size)], semaphores.at[index], semaphores.at[2 + index],
+                flipped("c", "zh"),
+            )
+            for index, (start, size) in enumerate(self.parts)
+        ]
+
+    def start_if(self, here):
+        @pl.when(here)
+        def _():
+            every(self.copies, "start")
 
     def start(self):
-        pl.when(jnp.logical_not(holds()))(self.copy.start)
+        self.start_if(jnp.logical_not(holds()))
 
     def step_inner(self):
-        pl.when(jnp.logical_and(jnp.logical_not(holds()), inner()))(self.copy.start)
+        self.start_if(jnp.logical_and(jnp.logical_not(holds()), inner()))
 
     def step_outer(self):
-        pl.when(jnp.logical_not(jnp.logical_or(holds(), inner())))(self.copy.start)
-
-    def wait(self):
-        pl.when(jnp.logical_not(holds()))(self.copy.wait)
-
-    def give(self, target, own, scale=None):
+        self.start_if(jnp.logical_not(jnp.logical_or(holds(), inner())))
+
+    def give(self, target, own, scale=None, only=(0, 1)):
         factor = 1.0 if scale is None else scale
-
-        @pl.when(holds())
-        def _():
-            target[...] = own[...].astype(f32) * factor
-
+        for index in only:
+            rows = pl.ds(*self.parts[index])
+
+            @pl.when(holds())
+            def _(rows=rows):
+                target[rows, :] = own[rows, :].astype(f32) * factor
+
+            @pl.when(jnp.logical_not(holds()))
+            def _(index=index, rows=rows):
+                self.copies[index].wait_recv()
+                target[rows, :] = self.landed[rows, :].astype(f32) * factor
+
+    def end(self):
         @pl.when(jnp.logical_not(holds()))
         def _():
-            target[...] = self.landed[...].astype(f32) * factor
+            every(self.copies, "wait_send")
 
 
 def gelu_and_slope(values):
@@ -556,21 +621,27 @@
         for copy in loads:
             copy.start()
         greet(*GROUP, *(FETCH if weights else ()), *(() if cotangent is None else (("c", "zh"),)))
+        r.ready()
         jobs = fetch_jobs(r, weights, layer + 1)
-        swaps = [] if cotangent is None else [Swapping(r.cotangent, r.landed, r.swap.at[0], r.swap.at[1])]
+        swaps = [] if cotangent is None else [Swapping(r.cotangent, r.landed, r.swap)]
         every(jobs + swaps, "step_inner")
         held, active, slope = r.held, r.active, r.slope
-        held[pl.ds(0, rows), :] = norm_rows(r.middle[...], r.gains[layer, 2:3, :], r.shifts[layer, 2:3, :]).astype(bf16)
-        for copy in loads:
-            copy.wait()
+
+        def prepare(start, size):
+            part = pl.ds(start, size)
+            held[part, :] = norm_rows(r.middle[part, :], r.gains[layer, 2:3, :], r.shifts[layer, 2:3, :]).astype(bf16)
+
         calls = []
 
         def work(start, size, sink):
             calls.append(start)
             if len(calls) == 1:
                 every(jobs + swaps, "step_outer")
+                every(loads, "wait")
+            if len(calls) == 3:
+                every(jobs, "step_share_outer")
             if len(calls) == 4:
-                every(jobs, "step_share")
+                every(jobs, "step_share_inner")
             here = pl.ds(start, size)
 
             def step(columns):
@@ -586,7 +657,7 @@
 
             tiles(width, step_down)
 
-        finish = exchange(rows, held, work, r.first, r.sums, r.send, r.receive)
+        finish = exchange(rows, held, prepare, work, r.first, r.sums, r.send, r.receive)
         stores = [
             pltpu.make_async_copy(held, r.held_out, r.local.at[2]),
             pltpu.make_async_copy(active, r.active_out, r.local.at[3]),
@@ -595,14 +666,17 @@
         for copy in stores:
             copy.start()
         every(jobs, "step_relay")
-        finish()
-        total = r.first[pl.ds(0, rows), :] + r.sums[1].astype(f32) + r.sums[5].astype(f32)
-        r.second[...] = total
-        r.stream[...] = r.middle[...] + norm_rows(total, r.gains[layer, 3:4, :], r.shifts[layer, 3:4, :])
+
+        def done(start, size, total):
+            part = pl.ds(start, size)
+            r.second[part, :] = total
+            r.stream[part, :] = r.middle[part, :] + norm_rows(total, r.gains[layer, 3:4, :], r.shifts[layer, 3:4, :])
+
+        finish(done)
         every(jobs, "step_end")
         for swap in swaps:
-            swap.wait()
             swap.give(r.grad, r.cotangent, r.scale[0:1, 0:1])
+            swap.end()
         for copy in stores:
             copy.wait()
 
@@ -623,14 +697,14 @@
             "held": VMEM((4 * rows, width), bf16), "active": VMEM((4 * rows, hidden), bf16), "slope": VMEM((4 * rows, hidden), bf16),
             "up": VMEM(w_up.shape, bf16), "down": VMEM(w_down.shape, bf16), **group_scratch(rows, width), "local": semaphores(5),
             **fetch_scratch(weights),
-            **({} if cotangent is None else {"landed": VMEM(cotangent.shape, bf16), "swap": semaphores(2)}),
+            **({} if cotangent is None else {"landed": VMEM(cotangent.shape, bf16), "swap": semaphores(4)}),
         },
         16 * rows * width * hidden,
         4 * rows * hidden,
     )
 
 
-def ffn_backward(layer, grad, saved, gains, shifts, w_up, w_down, own_up, own_down, grads, mixed=None):
+def ffn_backward(layer, grad, saved, gains, shifts, w_up, w_down, own_up, own_down, grads):
     middle = saved.middle
     rows, width = middle.shape
     hidden = w_up.shape[1]
@@ -646,35 +720,37 @@
         ]
         for copy in loads:
             copy.start()
-        greet(*GROUP, *(FETCH if grads else ()), *(() if mixed is None else (("c", "zh"),)))
+        greet(*GROUP, *(FETCH if grads else ()))
         jobs = pass_jobs(r, grads)
         new = [name for name in grads if grads[name][1] == 0]
         late = [name for name in grads if grads[name][1] == 2]
-        swaps = [] if mixed is None else [Swapping(r.low, r.landed, r.swap.at[0], r.swap.at[1])]
-        if mixed is not None:
-            r.low[...] = r.mixed[...].astype(bf16)
+        r.ready()
         crossing = [name for name in grads if grads[name][1] == 1]
-        every(swaps, "step_inner")
         every_of(jobs, crossing, "step_load", "step_loaded", "step_inner")
         every_of(jobs, late, "step_load")
         every_of(jobs, new, "step_spread")
-        pulled, gain_three, shift_three = norm_pull(r.second[...], r.gains[layer, 3:4, :], r.grad[...])
-        held[pl.ds(0, rows), :] = pulled.astype(bf16)
-        for copy in loads:
-            copy.wait()
+        norms = {}
+
+        def pull(row, values, part, grad):
+            pulled, *sums = norm_pull(values[part, :], r.gains[layer, row : row + 1, :], grad)
+            norms[row] = [old + new for old, new in zip(norms.get(row, (0.0, 0.0)), sums)]
+            return pulled
+
+        def prepare(start, size):
+            part = pl.ds(start, size)
+            held[part, :] = pull(3, r.second, part, r.grad[part, :]).astype(bf16)
 
         calls = []
 
         def work(start, size, sink):
             calls.append(start)
             if len(calls) == 1:
-                every(swaps, "step_outer")
                 every_of(jobs, crossing, "step_outer")
                 every_of(jobs, late, "step_loaded", "step_share")
-            if len(calls) == 3:
-                every_of(jobs, late, "step_relay")
+                every(loads, "wait")
             if len(calls) == 4:
                 every_of(jobs, new, "step_fold")
+                every_of(jobs, crossing, "step_join_outer")
             here = pl.ds(start, size)
 
             def step(columns):
@@ -688,10 +764,10 @@
 
             tiles(width, step_up)
 
-        finish = exchange(rows, held, work, r.first, r.sums, r.send, r.receive)
-
-        every_of(jobs, late, "step_mate")
-        every_of(jobs, crossing, "step_join", "step_share")
+        finish = exchange(rows, held, prepare, work, r.first, r.sums, r.send, r.receive)
+
+        every_of(jobs, late, "step_relay")
+        every_of(jobs, crossing, "step_join_inner")
 
         def step_down(columns):
             r.outcome[0, columns, :] = dot_tn(active[:, columns], held[...]).astype(bf16)
@@ -699,28 +775,27 @@
         tiles(hidden, step_down)
         out_down = pltpu.make_async_copy(r.outcome.at[0], r.grad_down, r.local.at[0])
         out_down.start()
-        every_of(jobs, new, "step_add", "step_store")
-        every_of(jobs, crossing, "step_relay")
-
         def step_up(columns):
             r.outcome[1, columns, :] = dot_tn(past[:, columns], pushed[...]).astype(bf16)
 
         tiles(width, step_up)
         out_up = pltpu.make_async_copy(r.outcome.at[1], r.grad_up, r.local.at[1])
         out_up.start()
-        finish()
-        total = r.first[pl.ds(0, rows), :] + r.sums[1].astype(f32) + r.sums[5].astype(f32)
-        pulled, gain_two, shift_two = norm_pull(r.middle[...], r.gains[layer, 2:3, :], total)
-        r.grad_middle[...] = r.grad[...] + pulled
-        for index, value in enumerate((gain_two, shift_two, gain_three, shift_three)):
+        every_of(jobs, new, "step_add", "step_store")
+        every_of(jobs, crossing, "step_relay")
+        every_of(jobs, late, "step_mate")
+
+        def done(start, size, total):
+            part = pl.ds(start, size)
+            r.grad_middle[part, :] = r.grad[part, :] + pull(2, r.middle, part, total)
+
+        finish(done)
+        every_of(jobs, crossing, "step_mate")
+        for index, value in enumerate((*norms[2], *norms[3])):
             r.norms[index : index + 1, :] = value
         out_down.wait()
         out_up.wait()
-        every_of(jobs, crossing, "step_mate")
         every_of(jobs, grads, "step_end")
-        for swap in swaps:
-            swap.wait()
-            swap.give(r.mixed_out, r.mixed)
 
     return run(
         body,
@@ -729,10 +804,10 @@
             "grad": (grad, VMEM), "second": (saved.second, VMEM), "middle": (middle, VMEM), "gains": (gains, VMEM),
             "shifts": (shifts, VMEM), "held_in": (saved.held_out, ANY), "active_in": (saved.active_out, ANY),
             "slope_in": (saved.slope_out, ANY), "w_up": (w_up, ANY), "w_down": (w_down, ANY), "own_up": (own_up, ANY), "own_down": (own_down, ANY),
-            **pass_inputs(grads), **({} if mixed is None else {"mixed": (mixed, VMEM)}),
+            **pass_inputs(grads),
         },
         {
-            **pass_outputs(grads), **({} if mixed is None else {"mixed_out": (mixed.shape, f32, VMEM)}),
+            **pass_outputs(grads),
             "grad_middle": ((rows, width), f32, VMEM), "norms": ((4, width), f32, VMEM),
             "grad_up": (w_up.shape, bf16, ANY), "grad_down": (w_down.shape, bf16, ANY),
         },
@@ -742,11 +817,6 @@
             "pushed": VMEM((4 * rows, hidden), bf16), "up": VMEM(w_up.shape, bf16), "down": VMEM(w_down.shape, bf16),
             "outcome": VMEM((2, width, hidden), bf16), **group_scratch(rows, width), "local": semaphores(5),
             **pass_scratch(grads),
-            **(
-                {}
-                if mixed is None
-                else {"low": VMEM(mixed.shape, bf16), "landed": VMEM(mixed.shape, bf16), "swap": semaphores(2)}
-            ),
         },
         32 * rows * width * hidden,
     )
@@ -761,23 +831,25 @@
     return at(c, zl), at(1 - c, zl), at(c, 1 - zl), at(1 - c, 1 - zl)
 
 
-def gather(rows, held, arrived, send, receive):
+def gather(rows, held, prepare, arrived, send, receive):
     mate, near = flipped("c"), flipped("zl")
     own, others, along, across = places(rows)
     parts = cut_rows(rows)
-    here = pl.ds(own, rows)
-    copies = [remote(held.at[here], held.at[here], send.at[0], receive.at[0], mate)]
-    copies[0].start()
+    copies = []
     for index, (start, size) in enumerate(parts):
+        prepare(start, size)
         part = pl.ds(pl.multiple_of(own + start, 16), size)
         copy = remote(held.at[part], held.at[part], send.at[1 + index], receive.at[1 + index], near)
         copy.start()
         copies.append(copy)
+    here = pl.ds(own, rows)
+    copies.append(remote(held.at[here], held.at[here], send.at[0], receive.at[0], mate))
+    copies[-1].start()
     arrived(own, rows)
-    copies[0].wait_recv()
+    copies[-1].wait_recv()
     arrived(others, rows)
     for index, (start, size) in enumerate(parts):
-        copies[1 + index].wait_recv()
+        copies[index].wait_recv()
         first = pl.multiple_of(along + start, 16)
         part = pl.ds(first, size)
         relay = remote(held.at[part], held.at[part], send.at[4 + index], receive.at[4 + index], mate)
@@ -788,39 +860,48 @@
         arrived(pl.multiple_of(across + start, 16), size)
 
     def finish():
-        for copy in copies:
-            copy.wait_send()
+        every(copies, "wait_send")
 
     return finish
 
 
-def scatter(rows, project, first, sums, send, receive):
+def scatter(rows, before, project, first, sums, send, receive):
     mate, near = flipped("c"), flipped("zl")
-    own, others, along, across = places(rows)
+    own, others, _, _ = places(rows)
     parts = cut_rows(rows)
-    copies, crossing, final = [], [], []
-    for index, (start, size) in enumerate(parts):
-        part = pl.ds(start, size)
-
-        def keep_far(columns, value, part=part):
-            sums[2, part, columns] = value.astype(bf16)
-
-        project(pl.multiple_of(across + start, 16), size, keep_far)
-        cross = remote(sums.at[2, part], sums.at[3, part], send.at[6 + index], receive.at[6 + index], mate)
-        cross.start()
-        crossing.append(cross)
-    for index, (start, size) in enumerate(parts):
-        part = pl.ds(start, size)
-
-        def keep_near(columns, value, start=start, size=size):
-            first[pl.ds(rows + start, size), columns] = value
-
-        project(pl.multiple_of(along + start, 16), size, keep_near)
-        crossing[index].wait_recv()
-        sums[4, part, :] = (first[pl.ds(rows + start, size), :] + sums[3, part, :].astype(f32)).astype(bf16)
-        last = remote(sums.at[4, part], sums.at[5, part], send.at[8 + index], receive.at[8 + index], near)
-        last.start()
-        final.append(last)
+    crossing = [
+        remote(sums.at[2, pl.ds(start, size)], sums.at[3, pl.ds(start, size)], send.at[6 + index], receive.at[6 + index], mate)
+        for index, (start, size) in enumerate(parts)
+    ]
+    final = [
+        remote(sums.at[4, pl.ds(start, size)], sums.at[5, pl.ds(start, size)], send.at[8 + index], receive.at[8 + index], near)
+        for index, (start, size) in enumerate(parts)
+    ]
+    for half, name in ((1, "high"), (0, "low")):
+        before(name)
+        base = pl.multiple_of((2 * half + 1 - lax.axis_index("zl")) * rows, 16)
+        far = lax.axis_index("c") != half
+        for index, (start, size) in enumerate(parts):
+
+            def keep(columns, value, start=start, size=size):
+                first[pl.ds(rows + start, size), columns] = value
+
+            project(pl.multiple_of(base + start, 16), size, keep)
+
+            @pl.when(far)
+            def _(index=index, start=start, size=size):
+                sums[2, pl.ds(start, size), :] = first[pl.ds(rows + start, size), :].astype(bf16)
+                crossing[index].start()
+
+        @pl.when(jnp.logical_not(far))
+        def _():
+            for index, (start, size) in enumerate(parts):
+                crossing[index].wait_recv()
+                part = pl.ds(start, size)
+                sums[4, part, :] = (first[pl.ds(rows + start, size), :] + sums[3, part, :].astype(f32)).astype(bf16)
+                final[index].start()
+
+    before("rest")
 
     def keep_mate(columns, value):
         sums[0, :, columns] = value.astype(bf16)
@@ -829,17 +910,17 @@
     back = remote(sums.at[0], sums.at[1], send.at[3], receive.at[3], mate)
     back.start()
 
-    def keep(columns, value):
+    def keep_own(columns, value):
         first[pl.ds(0, rows), columns] = value
 
-    project(own, rows, keep)
-
-    def finish():
+    project(own, rows, keep_own)
+
+    def finish(done):
         back.wait_recv()
-        for copy in final:
+        for copy, (start, size) in zip(final, parts):
             copy.wait_recv()
-        for copy in [back] + crossing + final:
-            copy.wait_send()
+            done(start, size, summed(first, sums, start, size))
+        every([back] + crossing + final, "wait_send")
 
     return finish
 
@@ -909,45 +990,53 @@
         greet(*GROUP, *(FETCH if weights else ()), *((("c", "zh"),) if first else ()))
         jobs = fetch_jobs(r, weights, layer)
         stream = r.stream
+        r.ready()
         if first:
-            swap = Swapping(r.stream, r.landed, r.swap.at[0], r.swap.at[1])
-            exchanged = remote(r.weight_in, r.other, r.swap.at[2], r.swap.at[3], flipped("c"))
-            exchanged.start()
+            swap = Swapping(r.stream, r.landed, r.swap)
+            exchanged = remote(r.weight_in, r.other, r.swap.at[4], r.swap.at[5], flipped("c"))
             before = [
                 Fetching(source.at[layer], target, send, receive)
                 for source, target, send, receive in (
                     (r.own_qkv, r.qkv_to, r.qkv_send, r.qkv_receive), (r.own_out, r.out_to, r.out_send, r.out_receive)
                 )
             ]
-            every(before, "step_inner")
-            every(before, "step_outer")
+            before[0].step_inner()
+            before[0].step_outer()
+            before[0].step_sent()
+            exchanged.start()
             before[0].step_share()
-            swap.start()
-            before[0].step_relay()
-            before[1].step_share()
             exchanged.wait()
             r.scale[...] = jnp.where(holds(), r.weight_in[...], r.other[...])
-            swap.wait()
-            swap.give(r.stream_out, r.stream)
+            swap.start()
+            before[1].step_inner()
+            before[1].step_outer()
+            before[0].step_relay()
             stream = r.stream_out
         own = places(rows)[0]
-        held[pl.ds(own, rows), :] = norm_rows(stream[...], r.gains[layer, 0:1, :], r.shifts[layer, 0:1, :]).astype(bf16)
-        if not first:
-            every(loads, "wait")
+
+        def prepare(start, size):
+            part = pl.ds(start, size)
+            if first:
+                swap.give(r.stream_out, r.stream, None, (0 if start == 0 else 1,))
+            value = norm_rows(stream[part, :], r.gains[layer, 0:1, :], r.shifts[layer, 0:1, :])
+            held[pl.ds(pl.multiple_of(own + start, 16), size), :] = value.astype(bf16)
+
         calls = []
 
         def arrived(start, size):
             calls.append(start)
             if len(calls) == 1:
                 if first:
-                    before[1].step_relay()
-                    before[0].step_end()
+                    before[1].step_share()
+                    before[0].step_got()
                     every(loads[:3], "start")
                     every(loads[:3], "wait")
                 else:
-                    every(jobs[:1], "step_outer")
+                    every(jobs, "step_outer")
+                    every(loads, "wait")
             if len(calls) == 2 and first:
                 every(jobs, "step_outer")
+                before[1].step_relay()
             here = pl.ds(start, size)
 
             def step(columns):
@@ -955,7 +1044,7 @@
 
             tiles(3 * width, step)
 
-        sent = gather(rows, held, arrived, r.send, r.receive)
+        sent = gather(rows, held, prepare, arrived, r.send, r.receive)
         stores = [pltpu.make_async_copy(held, r.held_out, r.local.at[0]), pltpu.make_async_copy(qkv, r.qkv_out, r.local.at[1])]
         for copy in stores:
             copy.start()
@@ -964,27 +1053,25 @@
         def attend(quarter, high):
             attend_block(rows, pl.multiple_of(quarter * rows, 16), high, qkv, attended, lse)
 
-        every(jobs if first else jobs[:1], "step_inner")
-        if not first:
-            every(jobs[1:], "step_outer")
-        attend(3 - zl, True)
-        if not first:
-            every(jobs[1:], "step_inner")
-        if first:
-            before[1].step_end()
-            loads[3].start()
-        attend(1 - zl, False)
-        if first:
-            loads[3].wait()
-        done = []
+        every(jobs, "step_inner")
+
+        def before_part(name):
+            if name == "high":
+                attend(3 - zl, True)
+                if first:
+                    before[1].step_end()
+                    loads[3].start()
+                    loads[3].wait()
+            elif name == "low":
+                attend(1 - zl, False)
+                if first:
+                    every(jobs[:1], "step_share")
+            else:
+                attend(2 + zl, True)
+                every(jobs[1:] if first else jobs, "step_share")
+                attend(zl, False)
 
         def term(start, size, sink):
-            if size == rows and not done:
-                done.append(True)
-                attend(2 + zl, True)
-                every(jobs[:1], "step_share")
-                attend(zl, False)
-                every(jobs[:1], "step_relay")
             here = pl.ds(start, size)
 
             def step(columns):
@@ -992,18 +1079,22 @@
 
             tiles(model, step)
 
-        finish = scatter(rows, term, r.first, r.sums, r.send, r.receive)
+        finish = scatter(rows, before_part, term, r.first, r.sums, r.send, r.receive)
         late = [pltpu.make_async_copy(attended, r.attended_out, r.local.at[2]), pltpu.make_async_copy(lse, r.lse_out, r.local.at[3])]
         for copy in late:
             copy.start()
-        every(jobs[1:], "step_share")
-        finish()
-        every(jobs[1:], "step_relay")
-        total = r.first[pl.ds(0, rows), :] + r.sums[1].astype(f32) + r.sums[5].astype(f32)
-        r.branch[...] = total
-        r.middle[...] = stream[...] + norm_rows(total, r.gains[layer, 1:2, :], r.shifts[layer, 1:2, :])
+        every(jobs, "step_relay")
+
+        def done(start, size, total):
+            part = pl.ds(start, size)
+            r.branch[part, :] = total
+            r.middle[part, :] = stream[part, :] + norm_rows(total, r.gains[layer, 1:2, :], r.shifts[layer, 1:2, :])
+
+        finish(done)
         sent()
         every(jobs, "step_end")
+        if first:
+            swap.end()
         for copy in stores + late:
             copy.wait()
 
@@ -1026,7 +1117,7 @@
             "lse": VMEM((4 * rows, 128), f32), "weight": VMEM((model, 3 * width), bf16), "out": VMEM((width, model), bf16),
             **group_scratch(rows, model), "local": semaphores(4), **fetch_scratch(weights),
             **fetch_scratch(early),
-            **({"landed": VMEM(stream.shape, bf16), "other": VMEM(scale.shape, f32), "swap": semaphores(4)} if first else {}),
+            **({"landed": VMEM(stream.shape, bf16), "other": VMEM(scale.shape, f32), "swap": semaphores(6)} if first else {}),
         },
         24 * rows * model * width,
         64 * rows * rows,
@@ -1063,12 +1154,14 @@
         grad_query[here, columns] = (result * scale).astype(bf16)
 
 
-def attention_backward(layer, grad, stream, saved, gains, shifts, w_qkv, w_out, own_qkv, own_out, grads, norms=None):
+def attention_backward(layer, grad, stream, saved, gains, shifts, w_qkv, w_out, own_qkv, own_out, grads, norms=None, mixed=None):
     rows, model = stream.shape
     width = w_out.shape[0]
     final = norms is not None
     shape = jax.ShapeDtypeStruct
-    mine = {"qkv_last": (shape(w_qkv.shape, bf16), 0, 2), "out_last": (shape(w_out.shape, bf16), 0, 2)} if final else {}
+    thirds = ("query_last", "key_last", "value_last")
+    mine = {name: (shape(w_qkv.shape[1:], bf16), 0, 2) for name in thirds} if final else {}
+    mine_out = {"out_last": (shape(w_out.shape, bf16), 0, 2)} if final else {}
 
     def body(r):
         held, past, qkv, attended, lse, inner, above = r.held, r.past, r.qkv, r.attended, r.lse, r.inner, r.above
@@ -1086,19 +1179,34 @@
         ]
         for copy in loads:
             copy.start()
-        greet(*GROUP, *(FETCH if grads else ()), *((("c", "zh"),) if final else ()))
-        jobs = pass_jobs(r, {**grads, **mine}, {"qkv_last": r.outcome, "out_last": r.outcome_out})
+        greet(*GROUP, *(FETCH if grads else ()), *((("c", "zh"),) if final or mixed is not None else ()))
+        ends = {"out_last": (r.outcome_out,)}
+        if final:
+            ends.update({name: (r.outcome.at[index], r.qkv_last_out.at[index]) for index, name in enumerate(thirds)})
+        jobs = pass_jobs(r, {**grads, **mine, **mine_out}, ends)
         new = [name for name in grads if grads[name][1] == 0]
         crossing = [name for name in grads if grads[name][1] == 1]
+        r.ready()
+        swaps = []
+        if mixed is not None:
+            r.low[...] = r.mixed[...].astype(bf16)
+            swaps.append(Swapping(r.low, r.landed, r.swap))
         every_of(jobs, crossing, "step_load")
         every_of(jobs, new[:1], "step_spread")
+        older = crossing
         own = places(rows)[0]
-        pulled, gain_one, shift_one = norm_pull(r.branch[...], r.gains[layer, 1:2, :], r.grad[...])
-        held[pl.ds(own, rows), :] = pulled.astype(bf16)
-        grad_key[...] = jnp.zeros_like(grad_key)
-        grad_value[...] = jnp.zeros_like(grad_value)
-        for copy in loads:
-            copy.wait()
+        norms_of = {}
+
+        def pull(row, values, part, grad):
+            pulled, *sums = norm_pull(values[part, :], r.gains[layer, row : row + 1, :], grad)
+            norms_of[row] = [old + new for old, new in zip(norms_of.get(row, (0.0, 0.0)), sums)]
+            return pulled
+
+        def prepare(start, size):
+            part = pl.ds(start, size)
+            value = pull(1, r.branch, part, r.grad[part, :])
+            held[pl.ds(pl.multiple_of(own + start, 16), size), :] = value.astype(bf16)
+
         zl = lax.axis_index("zl")
 
         def back(quarter, high):
@@ -1109,6 +1217,10 @@
         blocks = []
 
         def arrived(start, size):
+            if not blocks:
+                grad_key[...] = jnp.zeros_like(grad_key)
+                grad_value[...] = jnp.zeros_like(grad_value)
+                every(loads, "wait")
             here = pl.ds(start, size)
             value = dot_nt(held[here, :], r.out[...]).astype(bf16)
             above[here, :] = value
@@ -1126,69 +1238,85 @@
                 back(2 + zl, True)
                 back(zl, False)
 
-        sent = gather(rows, held, arrived, r.send, r.receive)
-        every_of(jobs, crossing, "step_loaded", "step_outer")
+        sent = gather(rows, held, prepare, arrived, r.send, r.receive)
+        every(swaps, "start")
+        every_of(jobs, crossing, "step_loaded", "step_outer", "step_inner")
+
+        def step_out(columns):
+            r.outcome_out[:, columns] = dot_tn(attended[...], held[:, columns]).astype(bf16)
+
+        outs = []
+        if final:
+            tiles(model, step_out)
+            every_of(jobs, mine_out, "step_spread")
         every_of(jobs, new[:1], "step_fold")
         every_of(jobs, new[1:], "step_spread")
-        back(3 - zl, True)
-        every_of(jobs, new[:1], "step_add")
-        if not final:
-            every_of(jobs, new[:1], "step_outer")
-        every_of(jobs, crossing, "step_inner")
-        back(1 - zl, False)
-        if not final:
-            every_of(jobs, new[:1], "step_inner")
-        pushed[:, pl.ds(width, width)] = grad_key[...].astype(bf16)
-        pushed[:, pl.ds(2 * width, width)] = grad_value[...].astype(bf16)
-
-        def term(start, size, sink):
-            here = pl.ds(start, size)
-
-            def step(columns):
-                sink(columns, dot_nt(pushed[here, :], weight[columns, :]))
-
-            tiles(model, step)
-
-        finish = scatter(rows, term, r.first, r.sums, r.send, r.receive)
-
-        every_of(jobs, new[1:], "step_fold")
-        if final:
-            every_of(jobs, new[:1], "step_outer", "step_inner")
-
-        def step_out(columns):
-            r.outcome_out[:, columns] = dot_tn(attended[...], held[:, columns]).astype(bf16)
-
-        tiles(model, step_out)
-        outs = [] if final else [pltpu.make_async_copy(r.outcome_out, r.grad_out, r.local.at[0])]
-        every(outs, "start")
-        every_of(jobs, [name for name in mine if name == "out_last"], "step_spread")
 
         def step_qkv(columns):
             value = dot_tn(past[:, columns], pushed[...]).astype(bf16)
             for index in range(3):
                 r.outcome[index, columns, :] = value[:, index * width : (index + 1) * width]
 
-        tiles(model, step_qkv)
+        def cast(quarter):
+            part = pl.ds(pl.multiple_of(quarter * rows, 16), rows)
+            pushed[part, pl.ds(width, width)] = grad_key[part, :].astype(bf16)
+            pushed[part, pl.ds(2 * width, width)] = grad_value[part, :].astype(bf16)
+
+        def before_part(name):
+            if name == "high":
+                back(3 - zl, True)
+                cast(3 - zl)
+            elif name == "low":
+                every_of(jobs, new[:1], "step_add", "step_outer", "step_inner")
+                every_of(jobs, mine_out, "step_fold")
+                back(1 - zl, False)
+                cast(1 - zl)
+            else:
+                cast(2 + zl)
+                cast(zl)
+                every_of(jobs, new[1:], "step_fold")
+                if final:
+                    tiles(model, step_qkv)
+                    every_of(jobs, mine, "step_spread")
+                    every_of(jobs, mine_out, "step_add")
+
+        def term(start, size, sink):
+            here = pl.ds(start, size)
+
+            def step(columns):
+                sink(columns, dot_nt(pushed[here, :], weight[columns, :]))
+
+            tiles(model, step)
+
+        finish = scatter(rows, before_part, term, r.first, r.sums, r.send, r.receive)
         if final:
-            jobs["qkv_last"].step_spread()
             every_of(jobs, new[1:], "step_add", "step_outer", "step_inner")
-            for name in crossing:
-                every_of(jobs, [name], "step_join", "step_share")
+            every_of(jobs, mine_out, "step_outer", "step_inner")
         else:
-            out = pltpu.make_async_copy(r.outcome, r.grad_qkv, r.local.at[1])
-            out.start()
-            outs.append(out)
+            tiles(model, step_out)
+            outs.append(pltpu.make_async_copy(r.outcome_out, r.grad_out, r.local.at[0]))
+            outs[0].start()
+            tiles(model, step_qkv)
+            outs.append(pltpu.make_async_copy(r.outcome, r.grad_qkv, r.local.at[1]))
+            outs[1].start()
+
+        def done(start, size, total):
+            part = pl.ds(start, size)
+            target = r.home if final else r.grad_stream
+            target[part, :] = r.grad[part, :] + pull(0, r.stream, part, total)
+
+        finish(done)
+        if not final:
+            every_of(jobs, new[1:], "step_add")
             every_of(jobs, new[:1], "step_join")
-            every_of(jobs, new[1:], "step_add")
             every_of(jobs, new, "step_store")
-        finish()
-        total = r.first[pl.ds(0, rows), :] + r.sums[1].astype(f32) + r.sums[5].astype(f32)
-        pulled, gain_zero, shift_zero = norm_pull(r.stream[...], r.gains[layer, 0:1, :], total)
-        rows_norms = (gain_zero, shift_zero, gain_one, shift_one)
+        for swap in swaps:
+            swap.give(r.mixed_out, r.mixed)
+            swap.end()
+        rows_norms = (*norms_of[0], *norms_of[1])
         if final:
-            r.home[...] = r.grad[...] + pulled
             r.low[...] = r.home[...].astype(bf16)
-            swap = Swapping(r.low, r.landed, r.swap.at[0], r.swap.at[1])
+            swap = Swapping(r.low, r.landed, r.swap)
             for index, value in enumerate(rows_norms):
                 r.norms[index : index + 1, :] = value
             for index in range(len(norms)):
@@ -1196,7 +1324,7 @@
 
             def cube(index, wait):
                 copy = remote(
-                    r.norms, r.norms_land.at[index], r.swap.at[2 + index], r.swap.at[7 + index], flipped(CUBE[index])
+                    r.norms, r.norms_land.at[index], r.swap.at[4 + index], r.swap.at[9 + index], flipped(CUBE[index])
                 )
                 if not wait:
                     copy.start()
@@ -1204,33 +1332,44 @@
                 copy.wait()
                 r.norms[...] = r.norms[...] + r.norms_land[index]
 
+            query, key, value = [[name] for name in thirds]
             cube(0, False)
-            every_of(jobs, mine, "step_fold")
+            every_of(jobs, query, "step_fold")
             cube(0, True)
             cube(1, False)
-            every_of(jobs, crossing, "step_relay")
+            every_of(jobs, key, "step_fold")
             cube(1, True)
+            every_of(jobs, value, "step_fold")
             cube(2, False)
-            every_of(jobs, mine, "step_add", "step_outer", "step_inner")
-            swap.start()
-            every_of(jobs, crossing, "step_mate")
+            every_of(jobs, older, "step_join")
+            every_of(jobs, query, "step_add", "step_outer", "step_inner")
             cube(2, True)
             cube(3, False)
-            every_of(jobs, new[:1], "step_join", "step_share")
+            every_of(jobs, key, "step_add", "step_outer", "step_inner")
+            every_of(jobs, value, "step_add", "step_outer", "step_inner")
             cube(3, True)
             cube(4, False)
-            every_of(jobs, new[1:], "step_join", "step_share")
-            every_of(jobs, new, "step_relay")
+            swap.start()
+            every_of(jobs, new[:1], "step_join")
+            every_of(jobs, older, "step_relay")
+            every_of(jobs, new[1:], "step_join")
+            every_of(jobs, mine_out, "step_join")
+            every_of(jobs, older, "step_mate")
+            every_of(jobs, new[:1], "step_relay")
+            every_of(jobs, query, "step_join")
+            every_of(jobs, key, "step_join")
+            every_of(jobs, value, "step_join")
+            every_of(jobs, new[1:], "step_relay")
+            every_of(jobs, mine_out, "step_relay")
             every_of(jobs, new[:1], "step_mate")
-            every_of(jobs, mine, "step_join", "step_share")
+            every_of(jobs, mine, "step_relay")
             every_of(jobs, new[1:], "step_mate")
-            every_of(jobs, mine, "step_relay")
+            every_of(jobs, mine_out, "step_mate")
             every_of(jobs, mine, "step_mate")
             cube(4, True)
-            swap.wait()
             swap.give(r.grad_stream, r.home)
+            swap.end()
         else:
-            r.grad_stream[...] = r.grad[...] + pulled
             for index, value in enumerate(rows_norms):
                 r.norms[index : index + 1, :] = value
         sent()
@@ -1244,10 +1383,12 @@
             "grad": (grad, VMEM), "branch": (saved.branch, VMEM), "stream": (stream, VMEM), "gains": (gains, VMEM),
             "shifts": (shifts, VMEM), "held_in": (saved.held_out, ANY), "qkv_in": (saved.qkv_out, ANY),
             "attended_in": (saved.attended_out, ANY), "lse_in": (saved.lse_out, ANY), "w_qkv": (w_qkv, ANY), "w_out": (w_out, ANY), "own_qkv": (own_qkv, ANY), "own_out": (own_out, ANY),
-            **pass_inputs(grads), **({f"norms{index}": (value, VMEM) for index, value in enumerate(norms)} if final else {}),
+            **pass_inputs(grads), **({} if mixed is None else {"mixed": (mixed, VMEM)}), **({f"norms{index}": (value, VMEM) for index, value in enumerate(norms)} if final else {}),
         },
         {
-            **pass_outputs({**grads, **mine}),
+            **pass_outputs({**grads, **mine_out}),
+            **({"qkv_last_out": (w_qkv.shape, bf16, ANY)} if final else {}),
+            **({} if mixed is None else {"mixed_out": (mixed.shape, f32, VMEM)}),
             "grad_stream": ((rows, model), f32, VMEM), "norms": ((16 if final else 4, model), f32, VMEM),
             **({} if final else {"grad_qkv": (w_qkv.shape, bf16, ANY), "grad_out": (w_out.shape, bf16, ANY)}),
         },
@@ -1258,11 +1399,16 @@
             "grad_key": VMEM((4 * rows, width), f32), "grad_value": VMEM((4 * rows, width), f32),
             "weight": VMEM((model, 3 * width), bf16), "out": VMEM(w_out.shape, bf16), "outcome": VMEM((3, model, width), bf16),
             "outcome_out": VMEM(w_out.shape, bf16), **group_scratch(rows, model), "local": semaphores(8),
-            **pass_scratch({**grads, **mine}),
+            **pass_scratch({**grads, **mine, **mine_out}),
+            **(
+                {}
+                if mixed is None
+                else {"low": VMEM(mixed.shape, bf16), "landed": VMEM(mixed.shape, bf16), "swap": semaphores(4)}
+            ),
             **(
                 {
                     "home": VMEM((rows, model), f32), "low": VMEM((rows, model), bf16), "landed": VMEM((rows, model), bf16),
-                    "norms_land": VMEM((len(CUBE), 16, model), f32), "swap": semaphores(12),
+                    "norms_land": VMEM((len(CUBE), 16, model), f32), "swap": semaphores(14),
                 }
                 if final
                 else {}
@@ -1283,19 +1429,20 @@
     att_weights = [(att_zero.qkv_to, att_zero.out_to)]
     ffn_weights = [(att_zero.up_to, att_zero.down_to)]
     ffn_zero = ffn_forward(
-        0, att_zero.middle, gains, shifts, *ffn_weights[0], *own_ffn, {"qkv": w_qkv, "out": w_out}
+        0, att_zero.middle, gains, shifts, *ffn_weights[0], *own_ffn, {"qkv": w_qkv, "out": w_out, "down": w_down}
     )
     att_weights.append((ffn_zero.qkv_to, ffn_zero.out_to))
-    att_one = attention_forward(1, ffn_zero.stream, gains, shifts, *att_weights[1], *own_att, {"up": w_up, "down": w_down})
-    ffn_weights.append((att_one.up_to, att_one.down_to))
+    att_one = attention_forward(1, ffn_zero.stream, gains, shifts, *att_weights[1], *own_att, {"up": w_up})
+    ffn_weights.append((att_one.up_to, ffn_zero.down_to))
     ffn_one = ffn_forward(
         1, att_one.middle, gains, shifts, *ffn_weights[1], *own_ffn, {}, cotangent, att_zero.scale
     )
     ffn_zero.middle, ffn_one.middle = att_zero.middle, att_one.middle
-    back_one = ffn_backward(1, ffn_one.grad, ffn_one, gains, shifts, *ffn_weights[1], *own_ffn, {}, ffn_one.stream)
+    back_one = ffn_backward(1, ffn_one.grad, ffn_one, gains, shifts, *ffn_weights[1], *own_ffn, {})
     deep_one = attention_backward(
         1, back_one.grad_middle, ffn_zero.stream, att_one, gains, shifts, *att_weights[1], *own_att,
         {"up1": (back_one.grad_up, 0, 1), "down1": (back_one.grad_down, 0, 0)},
+        mixed=ffn_one.stream,
     )
     back_zero = ffn_backward(
         0, deep_one.grad_stream, ffn_zero, gains, shifts, *ffn_weights[0], *own_ffn,
@@ -1321,7 +1468,7 @@
     sums = last.norms.reshape(2, 4, 2, -1)
     if lax.axis_size("gh") > 1:
         grads, sums = lax.psum((grads, sums), "gh")
-    return (back_one.mixed_out, last.grad_stream, *grads, sums[:, :, 0], sums[:, :, 1])
+    return (deep_one.mixed_out, last.grad_stream, *grads, sums[:, :, 0], sums[:, :, 1])
 
 
 def solution(mesh):

time: 512 us -> 480 us (0.938)
  Pallas kernels: 479 us -> 448 us
    pallas_call x8, Pallas kernels: 479 us -> 448 us  [run(): pl.pallas_call(kernel, out_shape=tuple((jax.ShapeDtypeStruct(shape, kind)...]
where the time goes in v6:
time: 480 us; the launch traced here: 471 us
  Pallas kernels  448 us (93%)
  other arithmetic  14 us (3%)
  local copies, waits for them, and re-layouts  7.07 us (1%)
    pallas_call x8, Pallas kernels, run(): pl.pallas_call(kernel, out_shape=tuple((jax.ShapeDtypeStruct(shape, kind)...  448 us
    convert_element_type x3, other arithmetic, per_device(): jnp.stack(pair).astype(f32)  12.7 us

profile of v6, /device:TPU:0, one launch (start us, length us, event | category | flops | bytes accessed | tf_op | source)
XLA Modules:
  0.0 471.5 jit_solution(10248158227267503362)
XLA Ops:
  1.3 1.3 fusion
  3.3 0.6 broadcast_in_dim.8.refs_7_
  3.9 72.3 %shard_map.161 = (f32[272,1024]{1,0:T(8,128)}, f32[272,1024]{1,0:T(8,128)}, bf16[1088,1024]{1,0:T(8,128)(2,1)}, bf16[1088,768]{1,0:T(8,128)(2,1)}, bf16[1088,256...) custom-call(bf16[272,1024]{1,0:T(8,128)(2,1)} %refs_0_.1, ...), custom_call_target="tpu_custom_call" | custom-call | flops 1711276032 | bytes 13209600 | tf_op jit(solution)/shard_map/pallas_call | solution.py:179
  76.2 44.7 %shard_map.162 = (f32[272,1024]{1,0:T(8,128)}, f32[272,1024]{1,0:T(8,128)}, bf16[1088,1024]{1,0:T(8,128)(2,1)}, bf16[1088,1024]{1,0:T(8,128)(2,1)}, bf16[1088,10...) custom-call(f32[272,1024]{1,0:T(8,128)} %get-tuple-element.68.refs_0_.re, ...), custom_call_target="tpu_custom_call" | custom-call | flops 4563402752 | bytes 22151168 | tf_op jit(solution)/shard_map/pallas_call | solution.py:179
  120.9 44.8 %shard_map.163 = (f32[272,1024]{1,0:T(8,128)}, f32[272,1024]{1,0:T(8,128)}, bf16[1088,1024]{1,0:T(8,128)(2,1)}, bf16[1088,768]{1,0:T(8,128)(2,1)}, bf16[1088,256...) custom-call(f32[272,1024]{1,0:T(8,128)} %get-tuple-element.71.refs_0_.refs_2_, ...), custom_call_target="tpu_custom_call" | custom-call | flops 1711276032 | bytes 11665408 | tf_op jit(solution)/shard_map/pallas_call | solution.py:179
  165.8 38.2 %shard_map.164 = (f32[272,1024]{1,0:T(8,128)}, f32[272,1024]{1,0:T(8,128)}, bf16[1088,1024]{1,0:T(8,128)(2,1)}, bf16[1088,1024]{1,0:T(8,128)(2,1)}, bf16[1088,1024]{1,0:T(8,128)(2,1)}, /*index=5*/f32[272,1024]{1,0:T(8,128)}) custom-call(f32[272,1024]{1,0:T(8,128)} %get-tuple-element.74.refs_0_.refs_2_, f32[2,4,1024]{2,1,0:T(4,128)} %refs_3_.11, ...), custom_call_target="tpu_custom_call" | custom-call | flops 4563402752 | bytes 14323712 | tf_op jit(solution)/shard_map/pallas_call | solution.py:179
  203.9 36.2 %shard_map.165 = (f32[272,1024]{1,0:T(8,128)}, f32[4,1024]{1,0:T(4,128)}, bf16[1024,1024]{1,0:T(8,128)(2,1)}, bf16[1024,1024]{1,0:T(8,128)(2,1)}) custom-call(f32[272,1024]{1,0:T(8,128)} %get-tuple-element.78.refs_0_, f32[272,1024]{1,0:T(8,128)} %get-tuple-element.79.refs_1_, f32[272,1024]{1,0:T(8,128)} %get-tuple-element.74.refs_0_.refs_2_, ...), custom_call_target="tpu_custom_call" | custom-call | flops 9126805504 | bytes 22675456 | tf_op jit(solution)/shard_map/pallas_call | solution.py:179
  240.1 57.0 %shard_map.166 = (bf16[256,1024]{1,0:T(8,128)(2,1)}, bf16[256,1024]{1,0:T(8,128)(2,1)}, f32[272,1024]{1,0:T(8,128)}, f32[272,1024]{1,0:T(8,128)}, f32[4,1024]{1,...) custom-call(f32[272,1024]{1,0:T(8,128)} %get-tuple-element.83.refs_0_, ...), custom_call_target="tpu_custom_call" | custom-call | flops 4278190080 | bytes 20021248 | tf_op jit(solution)/shard_map/pallas_call | solution.py:179
  297.2 48.3 %shard_map.167 = (bf16[1024,1024]{1,0:T(8,128)(2,1)}, bf16[1024,1024]{1,0:T(8,128)(2,1)}, bf16[3,256,256]{2,1,0:T(8,128)(2,1)}, bf16[64,1024]{1,0:T(8,128)(2,1)}...) custom-call(f32[272,1024]{1,0:T(8,128)} %get-tuple-element.93.refs_0_, ...), custom_call_target="tpu_custom_call" | custom-call | flops 9126805504 | bytes 25821184 | tf_op jit(solution)/shard_map/pallas_call | solution.py:179
  345.5 106.3 %shard_map.168 = (bf16[3,1024,256]{2,1,0:T(8,128)(2,1)}, bf16[256,1024]{1,0:T(8,128)(2,1)}, bf16[1024,1024]{1,0:T(8,128)(2,1)}, bf16[1024,1024]{1,0:T(8,128)(2,1...) custom-call(f32[272,1024]{1,0:T(8,128)} %get-tuple-element.102.refs_0_,, ...), custom_call_target="tpu_custom_call" | custom-call | flops 4278190080 | bytes 19480576 | tf_op jit(solution)/shard_map/pallas_call | solution.py:179
  451.8 0.0 copy-start.4
  451.8 0.0 copy-start.5
  451.8 1.0 reshape.19
  452.8 0.1 fusion.1
  452.9 0.6 copy_bitcast_fusion
  453.5 2.7 maximum_convert_fusion.3
  456.2 3.6 maximum_convert_fusion.2
  459.8 0.6 copy-done.1
  460.4 0.9 copy-done.2
  461.3 0.6 copy-done.3
  461.9 6.5 %maximum_convert_fusion = (f32[2,1024,1024]{2,1,0:T(8,128)}, f32[2,1024,1024]{2,1,0:T(8,128)}) fusion(bf16[1,1024,1024]{2,1,0:T(8,128)(2,1)S(1)} %bitcast.14, bf16[1,1024,1024]{2,1,0:T(8,128)(2,1)S(1)} %bitcast.16, bf16[1,1024,1024]{2,1,0:T(8,128)(2,1)S(1)} %bitcast.15, bf16[1,1024,1024]{2,1,0:T(8,128)(2,1)S(1)} %bitcast.17), kind=kLoop, calls=%fused_computation | loop fusion | flops 8388608 | bytes 25165824 | tf_op jit(solution)/shard_map/convert_element_type | solution.py:1460
  468.4 1.0 copy.27
  469.4 0.7 copy-done.7
  470.0 1.0 copy.28
  (10 shorter events, 0.0 us)
Async XLA Ops:
  451.8 4.4 copy-start.4
  451.8 4.4 copy-start.5
  456.2 3.6 copy-start
  456.2 4.2 copy-start.1
  456.2 5.1 %copy-start.2 = (bf16[1024,1024]{1,0:T(8,128)(2,1)S(1)}, bf16[1024,1024]{1,0:T(8,128)(2,1)}, u32[]{:S(2)}) copy-start(bf16[1024,1024]{1,0:T(8,128)(2,1)} %get-tuple-element.123) | copy-start | bytes 6291460
  456.2 5.7 %copy-start.3 = (bf16[1024,1024]{1,0:T(8,128)(2,1)S(1)}, bf16[1024,1024]{1,0:T(8,128)(2,1)}, u32[]{:S(2)}) copy-start(bf16[1024,1024]{1,0:T(8,128)(2,1)} %get-tuple-element.125) | copy-start | bytes 6291460
  461.9 6.5 %copy-start.6 = (f32[272,1024]{1,0:T(8,128)S(1)}, f32[272,1024]{1,0:T(8,128)}, u32[]{:S(2)}) copy-start(f32[272,1024]{1,0:T(8,128)} %get-tuple-element.142) | copy-start | bytes 3342340
  468.4 1.6 copy-start.7

commit v7 on v6

--- a/solution.py
+++ b/solution.py
@@ -971,14 +971,14 @@
     lse[here, :] = tops
 
 
-def attention_forward(layer, stream, gains, shifts, w_qkv, w_out, own_qkv, own_out, weights, scale=None):
+def attention_forward(layer, stream, gains, shifts, w_qkv, w_out, own_qkv, own_out, weights, groups=None):
     rows, model = stream.shape
     width = own_out.shape[1]
-    first = scale is not None
+    first = groups is not None
     early = {"qkv": own_qkv, "out": own_out} if first else {}
 
     def body(r):
-        held, qkv, attended, lse, weight = r.held, r.qkv, r.attended, r.lse, r.weight
+        held, qkv, attended, lse, weight = r.held, r.qkv, r.attended, r.lse, r.matrix
         w_qkv, w_out = (r.qkv_to, r.out_to) if first else (r.w_qkv, r.w_out)
         loads = [
             Loading(r.own_qkv.at[layer, index], w_qkv.at[index], weight.at[:, pl.ds(index * width, width)], r.local.at[index])
@@ -993,7 +993,10 @@
         r.ready()
         if first:
             swap = Swapping(r.stream, r.landed, r.swap)
-            exchanged = remote(r.weight_in, r.other, r.swap.at[4], r.swap.at[5], flipped("c"))
+            index = lax.broadcasted_iota(jnp.int32, r.sizes.shape, 1)
+            size = jnp.sum(jnp.where(index == r.ids[...], r.sizes[...], 0), axis=1, keepdims=True)
+            r.weight[...] = jnp.broadcast_to(1.0 / size.astype(f32), r.weight.shape)
+            exchanged = remote(r.weight, r.other, r.swap.at[4], r.swap.at[5], flipped("c"))
             before = [
                 Fetching(source.at[layer], target, send, receive)
                 for source, target, send, receive in (
@@ -1006,7 +1009,7 @@
             exchanged.start()
             before[0].step_share()
             exchanged.wait()
-            r.scale[...] = jnp.where(holds(), r.weight_in[...], r.other[...])
+            r.scale[...] = jnp.where(holds(), r.weight[...], r.other[...])
             swap.start()
             before[1].step_inner()
             before[1].step_outer()
@@ -1103,21 +1106,21 @@
         1 + layer,
         {
             "stream": (stream, VMEM), "gains": (gains, VMEM), "shifts": (shifts, VMEM), "own_qkv": (own_qkv, ANY), "own_out": (own_out, ANY),
-            **fetch_inputs(weights), **({"weight_in": (scale, VMEM)} if first else {"w_qkv": (w_qkv, ANY), "w_out": (w_out, ANY)}),
+            **fetch_inputs(weights), **({"ids": (groups[0], VMEM), "sizes": (groups[1], VMEM)} if first else {"w_qkv": (w_qkv, ANY), "w_out": (w_out, ANY)}),
         },
         {
             "branch": ((rows, model), f32, VMEM), "middle": ((rows, model), f32, VMEM),
             "held_out": ((4 * rows, model), bf16, ANY), "qkv_out": ((4 * rows, 3 * width), bf16, ANY),
             "attended_out": ((4 * rows, width), bf16, ANY), "lse_out": ((4 * rows, 128), f32, ANY), **fetch_outputs(weights),
             **fetch_outputs(early),
-            **({"stream_out": (stream.shape, f32, VMEM), "scale": (scale.shape, f32, VMEM)} if first else {}),
+            **({"stream_out": (stream.shape, f32, VMEM), "scale": ((8, 128), f32, VMEM)} if first else {}),
         },
         {
             "held": VMEM((4 * rows, model), bf16), "qkv": VMEM((4 * rows, 3 * width), bf16), "attended": VMEM((4 * rows, width), bf16),
-            "lse": VMEM((4 * rows, 128), f32), "weight": VMEM((model, 3 * width), bf16), "out": VMEM((width, model), bf16),
+            "lse": VMEM((4 * rows, 128), f32), "matrix": VMEM((model, 3 * width), bf16), "out": VMEM((width, model), bf16),
             **group_scratch(rows, model), "local": semaphores(4), **fetch_scratch(weights),
             **fetch_scratch(early),
-            **({"landed": VMEM(stream.shape, bf16), "other": VMEM(scale.shape, f32), "swap": semaphores(6)} if first else {}),
+            **({"landed": VMEM(stream.shape, bf16), "weight": VMEM((8, 128), f32), "other": VMEM((8, 128), f32), "swap": semaphores(6)} if first else {}),
         },
         24 * rows * model * width,
         64 * rows * rows,
@@ -1132,25 +1135,28 @@
         columns = slice(pair * 128, pair * 128 + 128)
         query = qkv[here, columns] * bf16(scale)
         above = attended_grad[here, columns]
+        queries = [jnp.where(head_lanes(query.shape, half), query, 0) for half in range(2)]
+        grads = [jnp.where(head_lanes(query.shape, half), above, 0) for half in range(2)]
         result = 0.0
-        for half in range(2):
-            head = 2 * pair + half
-            only = jnp.where(head_lanes(query.shape, half), query, 0)
-            grad = jnp.where(head_lanes(query.shape, half), above, 0)
-            for begin, size, mask in spans(rows, high):
-                keys = pl.ds(begin, size)
-                key = qkv[keys, width + pair * 128 : width + pair * 128 + 128]
-                value = qkv[keys, 2 * width + pair * 128 : 2 * width + pair * 128 + 128]
-                scores = dot_nt(only, key)
+        for begin, size, mask in spans(rows, high):
+            keys = pl.ds(begin, size)
+            key = qkv[keys, width + pair * 128 : width + pair * 128 + 128]
+            value = qkv[keys, 2 * width + pair * 128 : 2 * width + pair * 128 + 128]
+            both_probs, both_scores = [], []
+            for half in range(2):
+                head = 2 * pair + half
+                scores = dot_nt(queries[half], key)
                 if mask:
                     scores = masked(scores, start, begin)
                 probs = jnp.exp(scores - lse[here, head : head + 1])
-                grad_probs = dot_nt(grad, value)
+                grad_probs = dot_nt(grads[half], value)
                 grad_scores = (probs * (grad_probs - inner[here, head : head + 1])).astype(bf16)
                 key_only = jnp.where(head_lanes(key.shape, half), key, 0)
                 result = result + dot_nn(grad_scores, key_only)
-                grad_key[keys, columns] += dot_tn(grad_scores, only)
-                grad_value[keys, columns] += dot_tn(probs.astype(bf16), grad)
+                both_probs.append(probs.astype(bf16))
+                both_scores.append(grad_scores)
+            grad_key[keys, columns] += dot_tn(jnp.concatenate(both_scores), jnp.concatenate(queries))
+            grad_value[keys, columns] += dot_tn(jnp.concatenate(both_probs), jnp.concatenate(grads))
         grad_query[here, columns] = (result * scale).astype(bf16)
 
 
@@ -1236,6 +1242,7 @@
             blocks.append(size)
             if len(blocks) == 2:
                 back(2 + zl, True)
+                every_of(jobs, new[1:], "step_spread")
                 back(zl, False)
 
         sent = gather(rows, held, prepare, arrived, r.send, r.receive)
@@ -1250,7 +1257,6 @@
             tiles(model, step_out)
             every_of(jobs, mine_out, "step_spread")
         every_of(jobs, new[:1], "step_fold")
-        every_of(jobs, new[1:], "step_spread")
 
         def step_qkv(columns):
             value = dot_tn(past[:, columns], pushed[...]).astype(bf16)
@@ -1267,6 +1273,7 @@
                 back(3 - zl, True)
                 cast(3 - zl)
             elif name == "low":
+                every_of(jobs, new[1:], "step_fold")
                 every_of(jobs, new[:1], "step_add", "step_outer", "step_inner")
                 every_of(jobs, mine_out, "step_fold")
                 back(1 - zl, False)
@@ -1274,11 +1281,13 @@
             else:
                 cast(2 + zl)
                 cast(zl)
-                every_of(jobs, new[1:], "step_fold")
                 if final:
+                    every_of(jobs, older, "step_join")
                     tiles(model, step_qkv)
                     every_of(jobs, mine, "step_spread")
                     every_of(jobs, mine_out, "step_add")
+                    every_of(jobs, new[1:], "step_add", "step_outer", "step_inner")
+                    every_of(jobs, mine_out, "step_outer", "step_inner")
 
         def term(start, size, sink):
             here = pl.ds(start, size)
@@ -1290,9 +1299,11 @@
 
         finish = scatter(rows, before_part, term, r.first, r.sums, r.send, r.receive)
         if final:
-            every_of(jobs, new[1:], "step_add", "step_outer", "step_inner")
-            every_of(jobs, mine_out, "step_outer", "step_inner")
+            every_of(jobs, mine, "step_fold")
+            every_of(jobs, older, "step_relay")
+            every_of(jobs, new[:1], "step_join")
         else:
+            every_of(jobs, new[1:], "step_add")
             tiles(model, step_out)
             outs.append(pltpu.make_async_copy(r.outcome_out, r.grad_out, r.local.at[0]))
             outs[0].start()
@@ -1307,7 +1318,6 @@
 
         finish(done)
         if not final:
-            every_of(jobs, new[1:], "step_add")
             every_of(jobs, new[:1], "step_join")
             every_of(jobs, new, "step_store")
         for swap in swaps:
@@ -1332,36 +1342,27 @@
                 copy.wait()
                 r.norms[...] = r.norms[...] + r.norms_land[index]
 
-            query, key, value = [[name] for name in thirds]
             cube(0, False)
-            every_of(jobs, query, "step_fold")
             cube(0, True)
             cube(1, False)
-            every_of(jobs, key, "step_fold")
+            for name in mine:
+                every_of(jobs, [name], "step_add", "step_outer", "step_inner")
             cube(1, True)
-            every_of(jobs, value, "step_fold")
             cube(2, False)
-            every_of(jobs, older, "step_join")
-            every_of(jobs, query, "step_add", "step_outer", "step_inner")
+            every_of(jobs, older, "step_mate")
             cube(2, True)
             cube(3, False)
-            every_of(jobs, key, "step_add", "step_outer", "step_inner")
-            every_of(jobs, value, "step_add", "step_outer", "step_inner")
+            every_of(jobs, new[1:], "step_join")
+            every_of(jobs, mine_out, "step_join")
             cube(3, True)
             cube(4, False)
             swap.start()
-            every_of(jobs, new[:1], "step_join")
-            every_of(jobs, older, "step_relay")
-            every_of(jobs, new[1:], "step_join")
-            every_of(jobs, mine_out, "step_join")
-            every_of(jobs, older, "step_mate")
             every_of(jobs, new[:1], "step_relay")
-            every_of(jobs, query, "step_join")
-            every_of(jobs, key, "step_join")
-            every_of(jobs, value, "step_join")
+            every_of(jobs, new[:1], "step_mate")
+            for name in mine:
+                every_of(jobs, [name], "step_join")
             every_of(jobs, new[1:], "step_relay")
             every_of(jobs, mine_out, "step_relay")
-            every_of(jobs, new[:1], "step_mate")
             every_of(jobs, mine, "step_relay")
             every_of(jobs, new[1:], "step_mate")
             every_of(jobs, mine_out, "step_mate")
@@ -1420,11 +1421,10 @@
 
 
 def per_device(hidden_in, cotangent, group_ids, group_sizes, w_qkv, w_out, w_up, w_down, gains, shifts):
-    size = jnp.sum(jnp.where(jnp.arange(group_sizes.shape[0]) == group_ids[0], group_sizes, 0))
-    weight = jnp.full((8, 128), 1.0 / size.astype(f32), f32)
+    groups = (group_ids.reshape(1, 1), group_sizes.reshape(1, -1))
     own_att, own_ffn = (w_qkv, w_out), (w_up, w_down)
     att_zero = attention_forward(
-        0, hidden_in, gains, shifts, None, None, *own_att, {"up": w_up, "down": w_down}, weight
+        0, hidden_in, gains, shifts, None, None, *own_att, {"up": w_up, "down": w_down}, groups
     )
     att_weights = [(att_zero.qkv_to, att_zero.out_to)]
     ffn_weights = [(att_zero.up_to, att_zero.down_to)]

time: 480 us -> 476 us (level)
  no operation moved by 1% of the time
where the time goes in v7:
time: 476 us; the launch traced here: 467 us
  Pallas kernels  446 us (94%)
  other arithmetic  12.7 us (3%)
  local copies, waits for them, and re-layouts  6.48 us (1%)
    pallas_call x8, Pallas kernels, run(): pl.pallas_call(kernel, out_shape=tuple((jax.ShapeDtypeStruct(shape, kind)...  446 us
    convert_element_type x3, other arithmetic, per_device(): jnp.stack(pair).astype(f32)  12.7 us

profile of v7, /device:TPU:0, one launch (start us, length us, event | category | flops | bytes accessed | tf_op | source)
XLA Modules:
  0.0 466.9 jit_solution(13228979891145497725)
XLA Ops:
  1.3 72.6 %shard_map.161 = (f32[272,1024]{1,0:T(8,128)}, f32[272,1024]{1,0:T(8,128)}, bf16[1088,1024]{1,0:T(8,128)(2,1)}, bf16[1088,768]{1,0:T(8,128)(2,1)}, bf16[1088,256...) custom-call(bf16[272,1024]{1,0:T(8,128)(2,1)} %refs_0_.1, ...), custom_call_target="tpu_custom_call" | custom-call | flops 1711276032 | bytes 13205540 | tf_op jit(solution)/shard_map/pallas_call | solution.py:179
  73.9 44.7 %shard_map.162 = (f32[272,1024]{1,0:T(8,128)}, f32[272,1024]{1,0:T(8,128)}, bf16[1088,1024]{1,0:T(8,128)(2,1)}, bf16[1088,1024]{1,0:T(8,128)(2,1)}, bf16[1088,10...) custom-call(f32[272,1024]{1,0:T(8,128)} %get-tuple-element.68.refs_0_.re, ...), custom_call_target="tpu_custom_call" | custom-call | flops 4563402752 | bytes 22151168 | tf_op jit(solution)/shard_map/pallas_call | solution.py:179
  118.6 44.6 %shard_map.163 = (f32[272,1024]{1,0:T(8,128)}, f32[272,1024]{1,0:T(8,128)}, bf16[1088,1024]{1,0:T(8,128)(2,1)}, bf16[1088,768]{1,0:T(8,128)(2,1)}, bf16[1088,256...) custom-call(f32[272,1024]{1,0:T(8,128)} %get-tuple-element.71.refs_0_.refs_2_, ...), custom_call_target="tpu_custom_call" | custom-call | flops 1711276032 | bytes 11665408 | tf_op jit(solution)/shard_map/pallas_call | solution.py:179
  163.2 38.1 %shard_map.164 = (f32[272,1024]{1,0:T(8,128)}, f32[272,1024]{1,0:T(8,128)}, bf16[1088,1024]{1,0:T(8,128)(2,1)}, bf16[1088,1024]{1,0:T(8,128)(2,1)}, bf16[1088,1024]{1,0:T(8,128)(2,1)}, /*index=5*/f32[272,1024]{1,0:T(8,128)}) custom-call(f32[272,1024]{1,0:T(8,128)} %get-tuple-element.74.refs_0_.refs_2_, f32[2,4,1024]{2,1,0:T(4,128)} %refs_3_.11, ...), custom_call_target="tpu_custom_call" | custom-call | flops 4563402752 | bytes 14323712 | tf_op jit(solution)/shard_map/pallas_call | solution.py:179
  201.3 36.2 %shard_map.165 = (f32[272,1024]{1,0:T(8,128)}, f32[4,1024]{1,0:T(4,128)}, bf16[1024,1024]{1,0:T(8,128)(2,1)}, bf16[1024,1024]{1,0:T(8,128)(2,1)}) custom-call(f32[272,1024]{1,0:T(8,128)} %get-tuple-element.78.refs_0_, f32[272,1024]{1,0:T(8,128)} %get-tuple-element.79.refs_1_, f32[272,1024]{1,0:T(8,128)} %get-tuple-element.74.refs_0_.refs_2_, ...), custom_call_target="tpu_custom_call" | custom-call | flops 9126805504 | bytes 22675456 | tf_op jit(solution)/shard_map/pallas_call | solution.py:179
  237.5 56.4 %shard_map.166 = (bf16[256,1024]{1,0:T(8,128)(2,1)}, bf16[256,1024]{1,0:T(8,128)(2,1)}, f32[272,1024]{1,0:T(8,128)}, f32[272,1024]{1,0:T(8,128)}, f32[4,1024]{1,...) custom-call(f32[272,1024]{1,0:T(8,128)} %get-tuple-element.83.refs_0_, ...), custom_call_target="tpu_custom_call" | custom-call | flops 4278190080 | bytes 20021248 | tf_op jit(solution)/shard_map/pallas_call | solution.py:179
  294.0 47.4 %shard_map.167 = (bf16[1024,1024]{1,0:T(8,128)(2,1)}, bf16[1024,1024]{1,0:T(8,128)(2,1)}, bf16[3,256,256]{2,1,0:T(8,128)(2,1)}, bf16[64,1024]{1,0:T(8,128)(2,1)}...) custom-call(f32[272,1024]{1,0:T(8,128)} %get-tuple-element.93.refs_0_, ...), custom_call_target="tpu_custom_call" | custom-call | flops 9126805504 | bytes 25821184 | tf_op jit(solution)/shard_map/pallas_call | solution.py:179
  341.4 105.7 %shard_map.168 = (bf16[3,1024,256]{2,1,0:T(8,128)(2,1)}, bf16[256,1024]{1,0:T(8,128)(2,1)}, bf16[1024,1024]{1,0:T(8,128)(2,1)}, bf16[1024,1024]{1,0:T(8,128)(2,1...) custom-call(f32[272,1024]{1,0:T(8,128)} %get-tuple-element.102.refs_0_,, ...), custom_call_target="tpu_custom_call" | custom-call | flops 4278190080 | bytes 19480576 | tf_op jit(solution)/shard_map/pallas_call | solution.py:179
  447.2 0.0 copy-start.4
  447.2 0.0 copy-start.5
  447.2 1.0 reshape.27
  448.2 0.1 fusion
  448.3 0.6 copy_bitcast_fusion
  448.9 2.7 maximum_convert_fusion.3
  451.6 0.0 copy-done.4
  451.6 0.0 copy-done.5
  451.6 3.6 maximum_convert_fusion.2
  455.2 0.6 copy-done.1
  455.8 0.9 copy-done.2
  456.7 0.6 copy-done.3
  457.3 6.5 %maximum_convert_fusion = (f32[2,1024,1024]{2,1,0:T(8,128)}, f32[2,1024,1024]{2,1,0:T(8,128)}) fusion(bf16[1,1024,1024]{2,1,0:T(8,128)(2,1)S(1)} %bitcast.15, bf16[1,1024,1024]{2,1,0:T(8,128)(2,1)S(1)} %bitcast.17, bf16[1,1024,1024]{2,1,0:T(8,128)(2,1)S(1)} %bitcast.16, bf16[1,1024,1024]{2,1,0:T(8,128)(2,1)S(1)} %bitcast.18), kind=kLoop, calls=%fused_computation | loop fusion | flops 8388608 | bytes 25165824 | tf_op jit(solution)/shard_map/convert_element_type | solution.py:1460
  463.8 1.0 copy.27
  464.8 0.7 copy-done.7
  465.4 1.0 copy.28
  (8 shorter events, 0.0 us)
Async XLA Ops:
  447.2 4.4 copy-start.4
  447.2 4.4 copy-start.5
  451.6 3.6 copy-start
  451.6 4.2 copy-start.1
  451.6 5.1 %copy-start.2 = (bf16[1024,1024]{1,0:T(8,128)(2,1)S(1)}, bf16[1024,1024]{1,0:T(8,128)(2,1)}, u32[]{:S(2)}) copy-start(bf16[1024,1024]{1,0:T(8,128)(2,1)} %get-tuple-element.123) | copy-start | bytes 6291460
  451.6 5.7 %copy-start.3 = (bf16[1024,1024]{1,0:T(8,128)(2,1)S(1)}, bf16[1024,1024]{1,0:T(8,128)(2,1)}, u32[]{:S(2)}) copy-start(bf16[1024,1024]{1,0:T(8,128)(2,1)} %get-tuple-element.125) | copy-start | bytes 6291460
  457.3 6.5 %copy-start.6 = (f32[272,1024]{1,0:T(8,128)S(1)}, f32[272,1024]{1,0:T(8,128)}, u32[]{:S(2)}) copy-start(f32[272,1024]{1,0:T(8,128)} %get-tuple-element.142) | copy-start | bytes 3342340
  463.8 1.6 copy-start.7

commit v8 on v7

--- a/solution.py
+++ b/solution.py
@@ -173,7 +173,7 @@
         ]
         every(copies, "start")
         found.update({name: found[name + "_copy"] for name in copied})
-        body(types.SimpleNamespace(**found, ready=lambda: every(copies, "wait")))
+        body(types.SimpleNamespace(**found, ready=lambda: every(copies, "wait"), greet=greet))
 
     moved = sum(value.size * value.dtype.itemsize for value, _ in inputs.values())
     results = pl.pallas_call(
@@ -186,6 +186,37 @@
         cost_estimate=pl.CostEstimate(flops=flops, bytes_accessed=moved, transcendentals=transcendentals),
     )(*[value for value, _ in inputs.values()])
     return types.SimpleNamespace(**dict(zip(outputs, results)))
+
+
+def plan(body, inputs, outputs, scratch, flops, transcendentals=0):
+    return types.SimpleNamespace(
+        body=body, inputs=inputs, outputs=outputs, scratch=scratch, flops=flops, transcendentals=transcendentals
+    )
+
+
+def run_both(number, first, second, links, extra=()):
+    def both(one, two):
+        return {**{"a_" + name: value for name, value in one.items()}, **{"b_" + name: value for name, value in two.items()}}
+
+    def parts(found):
+        return [{name[2:]: value for name, value in found.items() if name[:2] == mark} for mark in ("a_", "b_")]
+
+    def body(r):
+        one, two = parts(vars(r))
+        two.update({name: one[source] for name, source in links.items()})
+        first.body(types.SimpleNamespace(**one, ready=r.ready, greet=lambda *others: greet(*others, *extra)))
+        second.body(types.SimpleNamespace(**two, ready=lambda: None, greet=lambda *others: None))
+
+    result = run(
+        body,
+        number,
+        both(first.inputs, {name: value for name, value in second.inputs.items() if name not in links}),
+        both(first.outputs, second.outputs),
+        both(first.scratch, second.scratch),
+        first.flops + second.flops,
+        first.transcendentals + second.transcendentals,
+    )
+    return [types.SimpleNamespace(**part) for part in parts(vars(result))]
 
 
 def semaphores(count):
@@ -620,7 +651,7 @@
         loads = [Loading(r.own_up.at[layer], r.w_up, r.up, r.local.at[0]), Loading(r.own_down.at[layer], r.w_down, r.down, r.local.at[1])]
         for copy in loads:
             copy.start()
-        greet(*GROUP, *(FETCH if weights else ()), *(() if cotangent is None else (("c", "zh"),)))
+        r.greet(*GROUP, *(FETCH if weights else ()), *(() if cotangent is None else (("c", "zh"),)))
         r.ready()
         jobs = fetch_jobs(r, weights, layer + 1)
         swaps = [] if cotangent is None else [Swapping(r.cotangent, r.landed, r.swap)]
@@ -680,9 +711,8 @@
         for copy in stores:
             copy.wait()
 
-    return run(
+    return plan(
         body,
-        3 + layer,
         {
             "middle": (middle, VMEM), "gains": (gains, VMEM), "shifts": (shifts, VMEM), "w_up": (w_up, ANY), "w_down": (w_down, ANY), "own_up": (own_up, ANY), "own_down": (own_down, ANY),
             **fetch_inputs(weights), **({} if cotangent is None else {"cotangent": (cotangent, VMEM), "scale": (scale, VMEM)}),
@@ -987,7 +1017,7 @@
         loads.append(Loading(r.own_out.at[layer], w_out, r.out, r.local.at[3]))
         if not first:
             every(loads, "start")
-        greet(*GROUP, *(FETCH if weights else ()), *((("c", "zh"),) if first else ()))
+        r.greet(*GROUP, *(FETCH if weights else ()), *((("c", "zh"),) if first else ()))
         jobs = fetch_jobs(r, weights, layer)
         stream = r.stream
         r.ready()
@@ -1101,9 +1131,8 @@
         for copy in stores + late:
             copy.wait()
 
-    return run(
+    return plan(
         body,
-        1 + layer,
         {
             "stream": (stream, VMEM), "gains": (gains, VMEM), "shifts": (shifts, VMEM), "own_qkv": (own_qkv, ANY), "own_out": (own_out, ANY),
             **fetch_inputs(weights), **({"ids": (groups[0], VMEM), "sizes": (groups[1], VMEM)} if first else {"w_qkv": (w_qkv, ANY), "w_out": (w_out, ANY)}),
@@ -1423,20 +1452,25 @@
 def per_device(hidden_in, cotangent, group_ids, group_sizes, w_qkv, w_out, w_up, w_down, gains, shifts):
     groups = (group_ids.reshape(1, 1), group_sizes.reshape(1, -1))
     own_att, own_ffn = (w_qkv, w_out), (w_up, w_down)
-    att_zero = attention_forward(
-        0, hidden_in, gains, shifts, None, None, *own_att, {"up": w_up, "down": w_down}, groups
+    links = {"middle": "middle", "gains": "gains", "shifts": "shifts", "w_up": "up_to", "w_down": "down_to"}
+    rows = jax.ShapeDtypeStruct(hidden_in.shape, f32)
+    up, down = [jax.ShapeDtypeStruct(value.shape[1:], bf16) for value in own_ffn]
+    att_zero, ffn_zero = run_both(
+        1,
+        attention_forward(0, hidden_in, gains, shifts, None, None, *own_att, {"up": w_up, "down": w_down}, groups),
+        ffn_forward(0, rows, gains, shifts, up, down, *own_ffn, {"qkv": w_qkv, "out": w_out, "down": w_down}),
+        links,
     )
-    att_weights = [(att_zero.qkv_to, att_zero.out_to)]
-    ffn_weights = [(att_zero.up_to, att_zero.down_to)]
-    ffn_zero = ffn_forward(
-        0, att_zero.middle, gains, shifts, *ffn_weights[0], *own_ffn, {"qkv": w_qkv, "out": w_out, "down": w_down}
+    att_weights = [(att_zero.qkv_to, att_zero.out_to), (ffn_zero.qkv_to, ffn_zero.out_to)]
+    links.pop("w_down")
+    att_one, ffn_one = run_both(
+        2,
+        attention_forward(1, ffn_zero.stream, gains, shifts, *att_weights[1], *own_att, {"up": w_up}),
+        ffn_forward(1, rows, gains, shifts, up, ffn_zero.down_to, *own_ffn, {}, cotangent, att_zero.scale),
+        links,
+        (("c", "zh"),),
     )
-    att_weights.append((ffn_zero.qkv_to, ffn_zero.out_to))
-    att_one = attention_forward(1, ffn_zero.stream, gains, shifts, *att_weights[1], *own_att, {"up": w_up})
-    ffn_weights.append((att_one.up_to, ffn_zero.down_to))
-    ffn_one = ffn_forward(
-        1, att_one.middle, gains, shifts, *ffn_weights[1], *own_ffn, {}, cotangent, att_zero.scale
-    )
+    ffn_weights = [(att_zero.up_to, att_zero.down_to), (att_one.up_to, ffn_zero.down_to)]
     ffn_zero.middle, ffn_one.middle = att_zero.middle, att_one.middle
     back_one = ffn_backward(1, ffn_one.grad, ffn_one, gains, shifts, *ffn_weights[1], *own_ffn, {})
     deep_one = attention_backward(

time: 476 us -> 467 us (0.981)
  Pallas kernels: 446 us -> 437 us
    pallas_call x8 -> x6, Pallas kernels: 446 us -> 437 us  [run(): pl.pallas_call(kernel, out_shape=tuple((jax.ShapeDtypeStruct(shape, kind)...]
where the time goes in v8:
time: 467 us; the launch traced here: 458 us
  Pallas kernels  437 us (94%)
  other arithmetic  12.7 us (3%)
  local copies, waits for them, and re-layouts  6.48 us (1%)
    pallas_call x6, Pallas kernels, run(): pl.pallas_call(kernel, out_shape=tuple((jax.ShapeDtypeStruct(shape, kind)...  437 us
    convert_element_type x3, other arithmetic, per_device(): jnp.stack(pair).astype(f32)  12.7 us

profile of v8, /device:TPU:0, one launch (start us, length us, event | category | flops | bytes accessed | tf_op | source)
XLA Modules:
  0.0 458.1 jit_solution(18243317305794249883)
XLA Ops:
  1.3 112.8 %shard_map.161 = (f32[272,1024]{1,0:T(8,128)}, f32[272,1024]{1,0:T(8,128)}, bf16[1088,1024]{1,0:T(8,128)(2,1)}, bf16[1088,768]{1,0:T(8,128)(2,1)}, bf16[1088,256...) custom-call(bf16[272,1024]{1,0:T(8,128)(2,1)} %refs_0_.1, ...), custom_call_target="tpu_custom_call" | custom-call | flops 6274678784 | bytes 29982756 | tf_op jit(solution)/shard_map/pallas_call | solution.py:179
  114.1 77.8 %shard_map.162 = (f32[272,1024]{1,0:T(8,128)}, f32[272,1024]{1,0:T(8,128)}, bf16[1088,1024]{1,0:T(8,128)(2,1)}, bf16[1088,768]{1,0:T(8,128)(2,1)}, bf16[1088,256...) custom-call(f32[272,1024]{1,0:T(8,128)} %get-tuple-element.68.refs_0, ...), custom_call_target="tpu_custom_call" | custom-call | flops 6274678784 | bytes 22712320 | tf_op jit(solution)/shard_map/pallas_call | solution.py:179
  192.0 36.2 %shard_map.163 = (f32[272,1024]{1,0:T(8,128)}, f32[4,1024]{1,0:T(4,128)}, bf16[1024,1024]{1,0:T(8,128)(2,1)}, bf16[1024,1024]{1,0:T(8,128)(2,1)}) custom-call(f32[272,1024]{1,0:T(8,128)} %get-tuple-element.73.refs_0_, f32[272,1024]{1,0:T(8,128)} %get-tuple-element.74.refs_1_, f32[272,1024]{1,0:T(8,128)} %get-tuple-element.75.refs_2_, ...), custom_call_target="tpu_custom_call" | custom-call | flops 9126805504 | bytes 22675456 | tf_op jit(solution)/shard_map/pallas_call | solution.py:179
  228.2 57.2 %shard_map.164 = (bf16[256,1024]{1,0:T(8,128)(2,1)}, bf16[256,1024]{1,0:T(8,128)(2,1)}, f32[272,1024]{1,0:T(8,128)}, f32[272,1024]{1,0:T(8,128)}, f32[4,1024]{1,...) custom-call(f32[272,1024]{1,0:T(8,128)} %get-tuple-element.80.refs_0_, ...), custom_call_target="tpu_custom_call" | custom-call | flops 4278190080 | bytes 20021248 | tf_op jit(solution)/shard_map/pallas_call | solution.py:179
  285.4 46.7 %shard_map.165 = (bf16[1024,1024]{1,0:T(8,128)(2,1)}, bf16[1024,1024]{1,0:T(8,128)(2,1)}, bf16[3,256,256]{2,1,0:T(8,128)(2,1)}, bf16[64,1024]{1,0:T(8,128)(2,1)}...) custom-call(f32[272,1024]{1,0:T(8,128)} %get-tuple-element.90.refs_0_, ...), custom_call_target="tpu_custom_call" | custom-call | flops 9126805504 | bytes 25821184 | tf_op jit(solution)/shard_map/pallas_call | solution.py:179
  332.1 106.2 %shard_map.166 = (bf16[3,1024,256]{2,1,0:T(8,128)(2,1)}, bf16[256,1024]{1,0:T(8,128)(2,1)}, bf16[1024,1024]{1,0:T(8,128)(2,1)}, bf16[1024,1024]{1,0:T(8,128)(2,1...) custom-call(f32[272,1024]{1,0:T(8,128)} %get-tuple-element.102.refs_0_,, ...), custom_call_target="tpu_custom_call" | custom-call | flops 4278190080 | bytes 19480576 | tf_op jit(solution)/shard_map/pallas_call | solution.py:179
  438.4 0.0 copy-start.4
  438.4 0.0 copy-start.5
  438.4 1.0 reshape.27
  439.4 0.1 fusion
  439.5 0.6 copy_bitcast_fusion
  440.1 2.7 maximum_convert_fusion.3
  442.8 0.0 copy-done.4
  442.8 0.0 copy-done.5
  442.8 3.6 maximum_convert_fusion.2
  446.4 0.0 copy-done
  446.4 0.6 copy-done.1
  447.0 0.9 copy-done.2
  447.9 0.6 copy-done.3
  448.5 6.5 %maximum_convert_fusion = (f32[2,1024,1024]{2,1,0:T(8,128)}, f32[2,1024,1024]{2,1,0:T(8,128)}) fusion(bf16[1,1024,1024]{2,1,0:T(8,128)(2,1)S(1)} %bitcast.15, bf16[1,1024,1024]{2,1,0:T(8,128)(2,1)S(1)} %bitcast.17, bf16[1,1024,1024]{2,1,0:T(8,128)(2,1)S(1)} %bitcast.16, bf16[1,1024,1024]{2,1,0:T(8,128)(2,1)S(1)} %bitcast.18), kind=kLoop, calls=%fused_computation | loop fusion | flops 8388608 | bytes 25165824 | tf_op jit(solution)/shard_map/convert_element_type | solution.py:1494
  455.0 0.0 copy-done.6
  455.0 1.0 copy.27
  456.0 0.7 copy-done.7
  456.6 1.0 copy.28
  (6 shorter events, 0.0 us)
Async XLA Ops:
  438.4 4.4 copy-start.4
  438.4 4.4 copy-start.5
  442.8 3.6 copy-start
  442.8 4.2 copy-start.1
  442.8 5.1 %copy-start.2 = (bf16[1024,1024]{1,0:T(8,128)(2,1)S(1)}, bf16[1024,1024]{1,0:T(8,128)(2,1)}, u32[]{:S(2)}) copy-start(bf16[1024,1024]{1,0:T(8,128)(2,1)} %get-tuple-element.123) | copy-start | bytes 6291460
  442.8 5.7 %copy-start.3 = (bf16[1024,1024]{1,0:T(8,128)(2,1)S(1)}, bf16[1024,1024]{1,0:T(8,128)(2,1)}, u32[]{:S(2)}) copy-start(bf16[1024,1024]{1,0:T(8,128)(2,1)} %get-tuple-element.125) | copy-start | bytes 6291460
  448.5 6.5 %copy-start.6 = (f32[272,1024]{1,0:T(8,128)S(1)}, f32[272,1024]{1,0:T(8,128)}, u32[]{:S(2)}) copy-start(f32[272,1024]{1,0:T(8,128)} %get-tuple-element.142) | copy-start | bytes 3342340
  455.0 1.6 copy-start.7

commit v9 on v8

--- a/solution.py
+++ b/solution.py
@@ -1449,6 +1449,32 @@
     )
 
 
+def widened(*pairs):
+    steps = 4
+
+    def block(shape):
+        return part_shape(shape, steps)
+
+    def place(rank):
+        return lambda step: (*[0] * (rank - 2), step, 0)
+
+    def body(*refs):
+        count = len(pairs)
+        for index in range(count):
+            for layer in range(2):
+                refs[2 * count + index][layer] = refs[2 * index + layer][...].astype(f32)
+
+    values = [value for pair in pairs for value in pair]
+    return pl.pallas_call(
+        body,
+        grid=(steps,),
+        out_shape=tuple(jax.ShapeDtypeStruct((2, *one.shape), f32) for one, _ in pairs),
+        in_specs=[pl.BlockSpec(block(value.shape), place(value.ndim)) for value in values],
+        out_specs=tuple(pl.BlockSpec((2, *block(one.shape)), place(one.ndim + 1)) for one, _ in pairs),
+        compiler_params=pltpu.CompilerParams(vmem_limit_bytes=60 << 20),
+    )(*values)
+
+
 def per_device(hidden_in, cotangent, group_ids, group_sizes, w_qkv, w_out, w_up, w_down, gains, shifts):
     groups = (group_ids.reshape(1, 1), group_sizes.reshape(1, -1))
     own_att, own_ffn = (w_qkv, w_out), (w_up, w_down)
@@ -1490,15 +1516,12 @@
         },
         (back_zero.norms, deep_one.norms, back_one.norms),
     )
-    grads = [
-        jnp.stack(pair).astype(f32)
-        for pair in (
-            (last.qkv_last_out, last.qkv1_out),
-            (last.out_last_out, last.out1_out),
-            (last.up0_out, back_zero.up1_out),
-            (last.down0_out, back_zero.down1_out),
-        )
-    ]
+    grads = widened(
+        (last.qkv_last_out, last.qkv1_out),
+        (last.out_last_out, last.out1_out),
+        (last.up0_out, back_zero.up1_out),
+        (last.down0_out, back_zero.down1_out),
+    )
     sums = last.norms.reshape(2, 4, 2, -1)
     if lax.axis_size("gh") > 1:
         grads, sums = lax.psum((grads, sums), "gh")

time: 467 us -> 464 us (level)
  Pallas kernels: 437 us -> 450 us
  other arithmetic: 12.7 us -> 0 us
    pallas_call x0 -> x1, Pallas kernels: none -> 12.7 us  [widened(): pl.pallas_call(body, grid=(steps,), out_shape=tuple((jax.ShapeDtypeStruct...]
    convert_element_type x3 -> x0, other arithmetic: 12.7 us -> none  [per_device(): jnp.stack(pair).astype(f32)]
where the time goes in v9:
time: 464 us; the launch traced here: 455 us
  Pallas kernels  450 us (97%)
    pallas_call x6, Pallas kernels, run(): pl.pallas_call(kernel, out_shape=tuple((jax.ShapeDtypeStruct(shape, kind)...  437 us
    pallas_call x1, Pallas kernels, widened(): pl.pallas_call(body, grid=(steps,), out_shape=tuple((jax.ShapeDtypeStruct...  12.7 us

profile of v9, /device:TPU:0, one launch (start us, length us, event | category | flops | bytes accessed | tf_op | source)
XLA Modules:
  0.0 455.5 jit_solution(695618470571762599)
XLA Ops:
  1.3 112.8 %shard_map.161 = (f32[272,1024]{1,0:T(8,128)}, f32[272,1024]{1,0:T(8,128)}, bf16[1088,1024]{1,0:T(8,128)(2,1)}, bf16[1088,768]{1,0:T(8,128)(2,1)}, bf16[1088,256...) custom-call(bf16[272,1024]{1,0:T(8,128)(2,1)} %refs_0_.1, ...), custom_call_target="tpu_custom_call" | custom-call | flops 6274678784 | bytes 29982756 | tf_op jit(solution)/shard_map/pallas_call | solution.py:179
  114.1 77.7 %shard_map.162 = (f32[272,1024]{1,0:T(8,128)}, f32[272,1024]{1,0:T(8,128)}, bf16[1088,1024]{1,0:T(8,128)(2,1)}, bf16[1088,768]{1,0:T(8,128)(2,1)}, bf16[1088,256...) custom-call(f32[272,1024]{1,0:T(8,128)} %get-tuple-element.72.refs_0, ...), custom_call_target="tpu_custom_call" | custom-call | flops 6274678784 | bytes 22712320 | tf_op jit(solution)/shard_map/pallas_call | solution.py:179
  191.8 36.2 %shard_map.163 = (f32[272,1024]{1,0:T(8,128)}, f32[4,1024]{1,0:T(4,128)}, bf16[1024,1024]{1,0:T(8,128)(2,1)}, bf16[1024,1024]{1,0:T(8,128)(2,1)}) custom-call(f32[272,1024]{1,0:T(8,128)} %get-tuple-element.77.refs_0_, f32[272,1024]{1,0:T(8,128)} %get-tuple-element.78.refs_1_, f32[272,1024]{1,0:T(8,128)} %get-tuple-element.79.refs_2_, ...), custom_call_target="tpu_custom_call" | custom-call | flops 9126805504 | bytes 22675456 | tf_op jit(solution)/shard_map/pallas_call | solution.py:179
  228.0 57.1 %shard_map.164 = (bf16[256,1024]{1,0:T(8,128)(2,1)}, bf16[256,1024]{1,0:T(8,128)(2,1)}, f32[272,1024]{1,0:T(8,128)}, f32[272,1024]{1,0:T(8,128)}, f32[4,1024]{1,...) custom-call(f32[272,1024]{1,0:T(8,128)} %get-tuple-element.84.refs_0_, ...), custom_call_target="tpu_custom_call" | custom-call | flops 4278190080 | bytes 20021248 | tf_op jit(solution)/shard_map/pallas_call | solution.py:179
  285.2 46.7 %shard_map.165 = (bf16[1024,1024]{1,0:T(8,128)(2,1)}, bf16[1024,1024]{1,0:T(8,128)(2,1)}, bf16[3,256,256]{2,1,0:T(8,128)(2,1)}, bf16[64,1024]{1,0:T(8,128)(2,1)}...) custom-call(f32[272,1024]{1,0:T(8,128)} %get-tuple-element.94.refs_0_, ...), custom_call_target="tpu_custom_call" | custom-call | flops 9126805504 | bytes 25821184 | tf_op jit(solution)/shard_map/pallas_call | solution.py:179
  331.9 106.2 %shard_map.166 = (bf16[3,1024,256]{2,1,0:T(8,128)(2,1)}, bf16[256,1024]{1,0:T(8,128)(2,1)}, bf16[1024,1024]{1,0:T(8,128)(2,1)}, bf16[1024,1024]{1,0:T(8,128)(2,1...) custom-call(f32[272,1024]{1,0:T(8,128)} %get-tuple-element.106.refs_0_,, ...), custom_call_target="tpu_custom_call" | custom-call | flops 4278190080 | bytes 19480576 | tf_op jit(solution)/shard_map/pallas_call | solution.py:179
  438.1 0.9 reshape.27
  439.0 0.1 fusion
  439.1 0.6 copy_bitcast_fusion
  439.7 0.0 copy-start
  439.7 12.7 %shard_map.167 = (f32[2,3,1024,256]{3,2,1,0:T(8,128)}, f32[2,256,1024]{2,1,0:T(8,128)}, f32[2,1024,1024]{2,1,0:T(8,128)}, f32[2,1024,1024]{2,1,0:T(8,128)}) custom-call(bf16[3,1024,256]{2,1,0:T(8,128)(2,1)} %get-tuple-element.123.refs_0_, bf16[3,1024,256]{2,1,0:T(8,128)(2,1)} %get-tuple-element.124.refs_1_, bf16[256,1024]{1,0:T(8,128)(2,1)} %get-tuple-element.125.refs_2_, ...), custom_call_target="tpu_custom_call" | custom-call | tf_op jit(solution)/shard_map/pallas_call | solution.py:1468
  452.5 0.0 copy-start.1
  452.5 0.0 copy-done
  452.5 1.0 copy.27
  453.5 0.6 copy-done.1
  454.1 1.0 copy.28
Async XLA Ops:
  439.7 12.7 %copy-start = (f32[272,1024]{1,0:T(8,128)S(1)}, f32[272,1024]{1,0:T(8,128)}, u32[]{:S(2)}) copy-start(f32[272,1024]{1,0:T(8,128)} %get-tuple-element.148) | copy-start | bytes 3342340
  452.5 1.6 copy-start.1
